TPU v7x, 128 devices: a whole 4x4x4 slice. The times are simulated.
128 devices in a mesh: attn: 16 (over y, z), ffn: 8 (over x, core).
Axes of the slice: x: 4, y: 4, z: 4, core: 2. Of those that a mesh axis runs over, the one named last changes fastest.
Arguments:
- stream: bfloat16 [512, 16384], P(None, 'attn'), may hold values from -12 to 12
- queries: bfloat16 [512, 16384], P('attn', 'ffn'), may hold values from -16 to 16
- k_pool: bfloat16 [4096, 16, 1024], P('attn', None, 'ffn'), may hold values from -6 to 6
- v_pool: bfloat16 [4096, 16, 1024], P('attn', None, 'ffn'), may hold values from -24 to 24
- page_table: int32 [512, 32], replicated, may hold values from 0 to 255, as said below
- lengths: int32 [512], replicated, may hold values from 1 to 512
- home_device: int32 [512, 1], replicated, may hold values from 0 to 15; in each aligned block of 32 rows (0 to 31, 32 to 63, ...) at most 4 rows name the same one
- w_out: bfloat16 [16384, 16384], P('ffn', 'attn'), may hold values from -0.046875 to 0.046875
- norm_gain: bfloat16 [16384], P('attn'), may hold values from 0.099609375 to 1.8984375
- w_gate: bfloat16 [16384, 26624], P('attn', 'ffn'), may hold values from -0.046875 to 0.046875
- w_up: bfloat16 [16384, 26624], P('attn', 'ffn'), may hold values from -0.046875 to 0.046875
Outputs:
- residual: bfloat16 [512, 16384], P(None, 'attn')
- hidden: bfloat16 [512, 26624], P('attn', 'ffn')
Inputs may be any that keep to these rules, and one draw needn't show every extreme that they name: `page_table`: entries past a request's length are unused; pages may be shared. `home_device`: among the 32 rows of one index of attn, at most 4 name the same attention device.
All inputs are finite; a program needn't handle non-finite values.
Results may differ from a plain program's by a relative error of at most 0.035.
Values may be sent and summed in bfloat16 or wider, within the bound.
No kernel may reach another device: no remote copies, remote signals or barrier semaphores. Data moves between devices by JAX's collectives and lax.ppermute only.
A program may use at most 128 MiB of HBM per device.

v0:
```python
import jax
import jax.numpy as jnp
from jax import lax
from jax.sharding import PartitionSpec as P

D = 16384
HD = 128


eps = 1e-05


def attend(slot_queries, page_rows, length_rows, k_pool, v_pool):
    slot_count = slot_queries.shape[0]
    heads_kv = k_pool.shape[2] // HD
    per_group = slot_queries.shape[1] // (heads_kv * HD)
    key_rows = k_pool[page_rows].reshape(slot_count, -1, heads_kv, HD)
    value_rows = v_pool[page_rows].reshape(slot_count, -1, heads_kv, HD)
    context = key_rows.shape[1]
    queried = slot_queries.reshape(slot_count, heads_kv, per_group, HD)
    scores = jnp.einsum(
        "skgd,stkd->skgt", queried, key_rows, preferred_element_type=jnp.float32
    ) * HD ** (-0.5)
    visible = (jnp.arange(context, dtype=jnp.int32)[None, :] < length_rows[:, None])[
        :, None, None, :
    ]
    maxima = jnp.max(jnp.where(visible, scores, -jnp.inf), axis=-1, keepdims=True)
    weights = jnp.where(visible, jnp.exp(scores - maxima), jnp.float32(0.0))
    totals = jnp.sum(weights, axis=-1)
    blended = jnp.einsum(
        "skgt,stkd->skgd",
        weights.astype(jnp.bfloat16),
        value_rows,
        preferred_element_type=jnp.float32,
    )
    return (blended / totals[..., None]).astype(jnp.bfloat16).reshape(slot_count, -1)


def on_device(
    stream,
    queries,
    k_pool,
    v_pool,
    page_table,
    lengths,
    home_device,
    w_out,
    norm_gain,
    w_gate,
    w_up,
):
    n_attn = lax.axis_size("attn")
    mine = lax.axis_index("attn")
    req_total = home_device.shape[0]
    req_local = req_total // n_attn
    capacity = max(2, req_local // n_attn * 2)
    slot_total = n_attn * capacity
    owners = home_device[:, 0]
    blocks = owners.reshape(n_attn, req_local)
    targets = jnp.arange(n_attn, dtype=jnp.int32)
    onehot = (blocks[:, :, None] == targets[None, None, :]).astype(jnp.int32)
    before = jnp.cumsum(onehot, axis=1) - onehot
    ranks = jnp.sum(before * onehot, axis=2)
    my_owner = lax.dynamic_slice_in_dim(blocks, mine, 1, 0)[0]
    my_rank = lax.dynamic_slice_in_dim(ranks, mine, 1, 0)[0]
    dest = my_owner * capacity + my_rank
    placing = (dest[None, :] == jnp.arange(slot_total, dtype=jnp.int32)[:, None]).astype(
        jnp.bfloat16
    )
    outgoing = jnp.dot(placing, queries, preferred_element_type=jnp.float32).astype(jnp.bfloat16)
    arrived = lax.all_to_all(
        outgoing.reshape(n_attn, capacity, -1), "attn", split_axis=0, concat_axis=0, tiled=True
    )
    cap_ids = jnp.arange(capacity, dtype=jnp.int32)
    matched = (blocks == mine)[:, None, :] & (ranks[:, None, :] == cap_ids[None, :, None])
    request_ids = jnp.arange(req_total, dtype=jnp.int32).reshape(n_attn, 1, req_local)
    arrived_ids = jnp.sum(jnp.where(matched, request_ids, 0), axis=2).reshape(-1)
    occupied = jnp.any(matched, axis=2).reshape(-1)
    page_rows = page_table[arrived_ids]
    length_rows = jnp.where(occupied, lengths[arrived_ids], 1)
    outputs_home = attend(arrived.reshape(slot_total, -1), page_rows, length_rows, k_pool, v_pool)
    by_slot = jnp.dot(
        lax.all_gather(outputs_home, "attn", axis=0, tiled=True),
        w_out,
        preferred_element_type=jnp.float32,
    )
    sources = jnp.arange(req_total, dtype=jnp.int32) // req_local
    global_slot = owners * slot_total + sources * capacity + ranks.reshape(-1)
    partial_value = by_slot[global_slot]
    attended = lax.psum(partial_value.astype(jnp.bfloat16), "ffn").astype(jnp.float32)
    residual = (stream.astype(jnp.float32) + attended).astype(jnp.bfloat16)
    widened = residual.astype(jnp.float32)
    squares = lax.psum(jnp.sum(widened * widened, axis=1), "attn")
    scaling = lax.rsqrt(squares / D + eps)
    normed = (widened * scaling[:, None] * norm_gain.astype(jnp.float32)[None, :]).astype(
        jnp.bfloat16
    )
    width_local = w_gate.shape[1]
    gate_part = jnp.dot(normed, w_gate, preferred_element_type=jnp.float32)
    up_part = jnp.dot(normed, w_up, preferred_element_type=jnp.float32)
    whole = lax.psum(
        jnp.concatenate([gate_part, up_part], axis=1).astype(jnp.bfloat16), "attn"
    ).astype(jnp.float32)
    summed = lax.dynamic_slice_in_dim(whole, mine * req_local, req_local, 0)
    gate = summed[:, :width_local]
    up_sum = summed[:, width_local:]
    hidden = (jax.nn.silu(gate) * up_sum).astype(jnp.bfloat16)
    return (residual, hidden)


def solution(mesh):
    return jax.shard_map(
        on_device,
        mesh=mesh,
        in_specs=(
            P(None, "attn"),
            P("attn", "ffn"),
            P("attn", None, "ffn"),
            P("attn", None, "ffn"),
            P(),
            P(),
            P(),
            P("ffn", "attn"),
            P("attn"),
            P("attn", "ffn"),
            P("attn", "ffn"),
        ),
        out_specs=(P(None, "attn"), P("attn", "ffn")),
        check_vma=False,
    )
```

profile of v0, /device:TPU:0, one launch (start us, length us, event | category | flops | bytes accessed | tf_op | source)
XLA Modules:
  0.0 388.6 jit_solution(2893513062856180313)
XLA Ops:
  7.7 1.3 reduce.9
  9.2 0.8 fusion.28
  10.2 1.1 convolution_convert_fusion.2
  11.3 0.8 reshape.195
  12.2 8.1 %all-to-all-start = ((bf16[16,4,2048]{2,1,0:T(4,128)(2,1)}), bf16[16,4,2048]{2,1,0:T(4,128)(2,1)S(1)}, u32[]{:S(2)}, u32[]{:S(2)}) async-start(bf16[16,4,2048]{2,1,0:T(4,128)(2,1)} %reshape.195), calls=%async_computation | async-start | bytes 524288 | tf_op jit(solution)/shard_map/all_to_all | solution.py:71
  21.1 1.0 copy.30
  22.1 1.5 gather_fusion
  24.3 16.3 %gather_fusion.2 = bf16[2048,16,128]{2,1,0:T(8,128)(2,1)} fusion(bf16[256,16,128]{2,1,0:T(8,128)(2,1)S(1)} %copy-done, s32[2048]{0:T(1024)S(1)} %broadcast_clamp_fusion), kind=kCustom, calls=%fused_computation.2 | custom fusion | bytes 16785408 | tf_op jit(solution)/shard_map/gather | solution.py:17
  40.7 16.2 %gather_fusion.3 = bf16[2048,16,128]{2,1,0:T(8,128)(2,1)} fusion(bf16[256,16,128]{2,1,0:T(8,128)(2,1)S(1)} %copy-done.2, s32[2048]{0:T(1024)S(1)} %broadcast_clamp_fusion), kind=kCustom, calls=%fused_computation.3 | custom fusion | bytes 16785408 | tf_op jit(solution)/shard_map/gather | solution.py:18
  57.2 10.6 %fusion.29 = (f32[64,16]{1,0:T(8,128)S(1)}, bf16[64,16,512]{2,1,0:T(8,128)(2,1)S(1)}) fusion(pred[64,512]{1,0:T(8,128)(4,1)S(1)} %iota_compare_fusion.2, bf16[64,16,128]{2,1,0:T(8,128)(2,1)S(1)} %reshape.196, bf16[64,512,128]{2,1,0:T(8,128)(2,1)} %bitcast.25), kind=kOutput, calls=%fused_computation.64 | convolution fusion | flops 272105984 | bytes 9736192 | tf_op jit(solution)/shard_map/sub | solution.py:28
  67.7 4.6 %fusion.8 = bf16[64,16,128]{2,1,0:T(8,128)(2,1)S(1)} fusion(bf16[64,512,128]{2,1,0:T(8,128)(2,1)} %bitcast.26, bf16[64,16,512]{2,1,0:T(8,128)(2,1)S(1)} %get-tuple-element.5, f32[64,16]{1,0:T(8,128)S(1)} %get-tuple-element.4), kind=kOutput, calls=%fused_computation.21 | convolution fusion | flops 134479872 | bytes 9703424 | tf_op jit(solution)/shard_map/skgt,stkd->skgd/dot_general | solution.py:30
  72.3 0.8 copy.34
  73.3 53.2 %all-gather.2.cloned.1.call-done = bf16[1024,2048]{1,0:T(8,128)(2,1)} async-done(((bf16[64,2048]{1,0:T(8,128)(2,1)}), bf16[1024,2048]{1,0:T(8,128)(2,1)}) %all-gather.2.cloned.1.call-update) | async-done | bytes 4194320 | tf_op jit(solution)/shard_map/all_gather | solution.py:83
  126.5 7.9 %fusion.32 = bf16[1024,1024]{1,0:T(8,128)(2,1)S(1)} fusion(bf16[1024,2048]{1,0:T(8,128)(2,1)} %all-gather.2.cloned.1.call-done, bf16[2048,1024]{1,0:T(8,128)(2,1)} %param.18), kind=kOutput, calls=%fused_computation.66 | convolution fusion | flops 4294967296 | bytes 10485760 | tf_op jit(solution)/shard_map/dot_general | solution.py:82
  134.5 2.8 gather_fusion.4
  137.4 62.0 %all-reduce.3.cloned.1.call-done = bf16[512,1024]{1,0:T(8,128)(2,1)} async-done(((bf16[512,1024]{1,0:T(8,128)(2,1)}), bf16[512,1024]{1,0:T(8,128)(2,1)}) %all-reduce.3.cloned.1.call-update) | async-done | bytes 1048592 | tf_op jit(solution)/shard_map/psum | solution.py:90
  199.4 1.7 fusion.1
  201.1 40.8 %psum.22 = f32[512]{0:T(512)S(1)} all-reduce(f32[512]{0:T(512)S(1)} %get-tuple-element.2), channel_id=1, replica_groups=mesh['attn'=16,'ffn'=8] {'attn'}, use_global_device_ids=true, to_apply=%region_8.9 | all-reduce | flops 512 | bytes 4096 | tf_op jit(solution)/shard_map/psum | solution.py:93
  241.8 7.0 %convolution_convert_fusion.1 = bf16[512,3328]{1,0:T(8,128)(2,1)S(1)} fusion(bf16[1024,3328]{1,0:T(8,128)(2,1)} %param.20, bf16[512,1024]{1,0:T(8,128)(2,1)S(1)} %get-tuple-element.3, f32[1024]{0:T(1024)S(1)} %convert_element_type.52, f32[512]{0:T(512)S(1)} %add_rsqrt_fusion), kind=kOutput, calls=%fused_computation.8 | convolution fusion | flops 3493462016 | bytes 11278336 | tf_op jit(solution)/shard_map/dot_general | solution.py:99
  248.8 7.0 %convolution_convert_fusion = bf16[512,3328]{1,0:T(8,128)(2,1)S(1)} fusion(bf16[1024,3328]{1,0:T(8,128)(2,1)} %param.21, bf16[512,1024]{1,0:T(8,128)(2,1)} %copy-done.4, f32[1024]{0:T(1024)S(1)} %convert_element_type.52, f32[512]{0:T(512)S(1)} %add_rsqrt_fusion), kind=kOutput, calls=%fused_computation.7 | convolution fusion | flops 3493462016 | bytes 11278336 | tf_op jit(solution)/shard_map/dot_general | solution.py:100
  255.9 3.4 pad_maximum_fusion
  259.3 120.9 %all-reduce.5.cloned.1.call-done = bf16[512,6656]{1,0:T(8,128)(2,1)} async-done(((bf16[512,6656]{1,0:T(8,128)(2,1)}), bf16[512,6656]{1,0:T(8,128)(2,1)}) %all-reduce.5.cloned.1.call-update) | async-done | bytes 6815760 | tf_op jit(solution)/shard_map/psum | solution.py:101
  380.2 1.1 dynamic-slice_convert_fusion
  381.2 0.8 fusion.14
  (48 shorter events, 2.9 us)
Async XLA Ops:
  7.2 17.1 %copy-start = (bf16[256,16,128]{2,1,0:T(8,128)(2,1)S(1)}, bf16[256,16,128]{2,1,0:T(8,128)(2,1)}, u32[]{:S(2)}) copy-start(bf16[256,16,128]{2,1,0:T(8,128)(2,1)} %param.13) | copy-start | bytes 3145732
  12.2 44.8 %all-to-all-start = ((bf16[16,4,2048]{2,1,0:T(4,128)(2,1)}), bf16[16,4,2048]{2,1,0:T(4,128)(2,1)S(1)}, u32[]{:S(2)}, u32[]{:S(2)}) async-start(bf16[16,4,2048]{2,1,0:T(4,128)(2,1)} %reshape.195), calls=%async_computation | async-start | bytes 524288 | tf_op jit(solution)/shard_map/all_to_all | solution.py:71
  20.3 106.2 %all-gather.2.cloned.1.call-start = ((), (), s32[]{:S(2)}) async-start(), calls=%async_computation.1 | async-start | bytes 4456448 | tf_op jit(solution)/shard_map/all_gather | solution.py:83
  24.3 16.4 %copy-start.2 = (bf16[256,16,128]{2,1,0:T(8,128)(2,1)S(1)}, bf16[256,16,128]{2,1,0:T(8,128)(2,1)}, u32[]{:S(2)}) copy-start(bf16[256,16,128]{2,1,0:T(8,128)(2,1)} %param.14) | copy-start | bytes 3145732
  67.7 5.5 %copy-start.5 = (s32[512,1]{0,1:T(1,128)S(1)}, s32[512,1]{0,1:T(1,128)}, u32[]{:S(2)}) copy-start(s32[512,1]{0,1:T(1,128)} %param.17) | copy-start | bytes 6148
  73.2 126.2 %all-reduce.3.cloned.1.call-start = ((), (), s32[]{:S(2)}) async-start(), calls=%async_computation.2 | async-start | bytes 2097152 | tf_op jit(solution)/shard_map/psum | solution.py:90
  134.5 2.9 copy-start.6
  134.5 64.9 %copy-start.3 = (bf16[512,1024]{1,0:T(8,128)(2,1)S(1)}, bf16[512,1024]{1,0:T(8,128)(2,1)}, u32[]{:S(2)}) copy-start(bf16[512,1024]{1,0:T(8,128)(2,1)} %param.11) | copy-start | bytes 3145732
  137.3 242.8 %all-reduce.5.cloned.1.call-start = ((), (), s32[]{:S(2)}) async-start(), calls=%async_computation.3 | async-start | bytes 13631488 | tf_op jit(solution)/shard_map/psum | solution.py:101
  201.1 40.8 %copy-start.4 = (bf16[512,1024]{1,0:T(8,128)(2,1)}, bf16[512,1024]{1,0:T(8,128)(2,1)S(1)}, u32[]{:S(2)}) copy-start(bf16[512,1024]{1,0:T(8,128)(2,1)S(1)} %get-tuple-element.3) | copy-start | bytes 3145732
  259.3 122.8 %copy-start.1 = (bf16[256,16,128]{2,1,0:T(8,128)(2,1)S(1)}, bf16[256,16,128]{2,1,0:T(8,128)(2,1)}, u32[]{:S(2)}) copy-start(bf16[256,16,128]{2,1,0:T(8,128)(2,1)} %param.13) | copy-start | bytes 3145732
Sparse Core Ops, SparseCore 0:
  73.3 53.2 all-gather.1
  137.4 61.9 all-reduce.2
  259.4 120.6 all-reduce.4
where the time goes:
time: 390 us; the launch traced here: 389 us
  waiting for transfers between devices  236 us (61%)
  local copies, waits for them, and re-layouts  41.5 us (11%)
  blocking collectives  40.8 us (10%)
  matrix products  38.3 us (10%)
  between operations  13.9 us (4%)
  other arithmetic  9.72 us (2%)
  starting transfers between devices  8.25 us (2%)
    psum x1, waiting for transfers between devices, on_device(): lax.psum(jnp.concatenate([gate_part, up_part], axis=1).astype(jnp.bfloat1...  121 us
    psum x1, waiting for transfers between devices, on_device(): lax.psum(partial_value.astype(jnp.bfloat16), 'ffn').astype(jnp.float32)  62 us
    all_gather x1, waiting for transfers between devices, on_device(): lax.all_gather(outputs_home, 'attn', axis=0, tiled=True)  53.2 us
    psum x1, blocking collectives, on_device(): squares = lax.psum(jnp.sum(widened * widened, axis=1), 'attn')  40.8 us
    gather x1, local copies, waits for them, and re-layouts, attend(): key_rows = k_pool[page_rows].reshape(slot_count, -1, heads_kv, HD)  16.3 us
    gather x1, local copies, waits for them, and re-layouts, attend(): value_rows = v_pool[page_rows].reshape(slot_count, -1, heads_kv, HD)  16.2 us
    sub x1, matrix products, attend(): weights = jnp.where(visible, jnp.exp(scores - maxima), jnp.float32(0.0))  10.6 us
    all_to_all x1, starting transfers between devices, on_device(): lax.all_to_all(outgoing.reshape(n_attn, capacity, -1), 'attn', split_axis...  8.13 us
  transfers between devices with their start and end apart: 4, of which 3 were waited for; matrix products, arithmetic and copies ran while one was open for 9% of the time, Pallas kernels for 0%

commit v1 on v0

v1 whole, which is shorter than its diff:
```python
import functools
import jax
import jax.numpy as jnp
from jax import lax
from jax.experimental import pallas as pl
from jax.experimental.pallas import tpu as pltpu
from jax.sharding import PartitionSpec as P

D = 16384
HD = 128
HEADS = 16
PAGE = 16
MAXP = 32
CTX = PAGE * MAXP
REQS = 512
N_ATTN = 16
ROWS = 32
CAP = 4
SLOTS = N_ATTN * CAP
SIDE = 4
WIDTH = 1024
GROUP = 4
EPS = 1e-05
VMEM_BYTES = 50 * 1024 * 1024

SMEM = pl.BlockSpec(memory_space=pltpu.SMEM)
VMEM = pl.BlockSpec(memory_space=pltpu.VMEM)


def params():
    return pltpu.CompilerParams(vmem_limit_bytes=VMEM_BYTES)


def dispatch_body(mine_ref, home_ref, queries_ref, out_ref, count_ref):
    out_ref[...] = jnp.zeros_like(out_ref)
    for target in range(N_ATTN):
        count_ref[target] = 0
    base = mine_ref[0] * ROWS
    for row in range(ROWS):
        target = home_ref[0, base + row]
        rank = count_ref[target]
        count_ref[target] = rank + 1
        out_ref[target * CAP + rank] = queries_ref[row]


def dispatch(mine, home, queries):
    return pl.pallas_call(
        dispatch_body,
        out_shape=jax.ShapeDtypeStruct((SLOTS, HEADS, HD), jnp.bfloat16),
        in_specs=[SMEM, SMEM, VMEM],
        out_specs=VMEM,
        scratch_shapes=[pltpu.SMEM((N_ATTN,), jnp.int32)],
        compiler_params=params(),
    )(mine, home, queries)


def attend_body(
    mine_ref,
    home_ref,
    lengths_ref,
    table_ref,
    queries_ref,
    k_ref,
    v_ref,
    out_ref,
    ids_ref,
    slots_ref,
):
    mine = mine_ref[0]
    out_ref[...] = jnp.zeros_like(out_ref)

    def scan_source(source, found):
        start = found
        for row in range(ROWS):
            request = source * ROWS + row
            ids_ref[found] = request
            slots_ref[found] = source * CAP + found - start
            found = found + jnp.where(home_ref[0, request] == mine, 1, 0)
        return found

    found = lax.fori_loop(0, N_ATTN, scan_source, jnp.int32(0))
    last = jnp.maximum(found - 1, 0)
    last_id = ids_ref[last]
    last_slot = slots_ref[last]
    for extra in range(GROUP):
        ids_ref[found + extra] = last_id
        slots_ref[found + extra] = last_slot

    positions = lax.broadcasted_iota(jnp.int32, (HEADS, CTX), 1)

    def step(index, carry):
        chosen = []
        for member in range(GROUP):
            place = index * GROUP + member
            request = ids_ref[place]
            slot = slots_ref[place]
            pages = [table_ref[page, request] for page in range(MAXP)]
            chosen.append((request, slot, pages))
        scores = []
        for request, slot, pages in chosen:
            keys = jnp.concatenate([k_ref[page] for page in pages], axis=0)
            scores.append(
                lax.dot_general(
                    queries_ref[slot],
                    keys,
                    (((1,), (1,)), ((), ())),
                    preferred_element_type=jnp.float32,
                )
                * HD ** (-0.5)
            )
        outputs = []
        for (request, slot, pages), score in zip(chosen, scores):
            visible = positions < lengths_ref[0, request]
            maxima = jnp.max(jnp.where(visible, score, -jnp.inf), axis=1, keepdims=True)
            weights = jnp.where(visible, jnp.exp(score - maxima), 0.0)
            totals = jnp.sum(weights, axis=1, keepdims=True)
            outputs.append((weights.astype(jnp.bfloat16), totals))
        for (request, slot, pages), (weights, totals) in zip(chosen, outputs):
            values = jnp.concatenate([v_ref[page] for page in pages], axis=0)
            blended = jnp.dot(weights, values, preferred_element_type=jnp.float32)
            out_ref[slot] = (blended / totals).astype(jnp.bfloat16)
        return carry

    lax.fori_loop(0, (found + GROUP - 1) // GROUP, step, 0)


def attend(mine, home, lengths, table, queries, k_pool, v_pool):
    return pl.pallas_call(
        attend_body,
        out_shape=jax.ShapeDtypeStruct((SLOTS, HEADS, HD), jnp.bfloat16),
        in_specs=[SMEM] * 4 + [VMEM] * 3,
        out_specs=VMEM,
        scratch_shapes=[
            pltpu.SMEM((SLOTS + GROUP + 4,), jnp.int32),
            pltpu.SMEM((SLOTS + GROUP + 4,), jnp.int32),
        ],
        compiler_params=params(),
    )(mine, home, lengths, table, queries, k_pool, v_pool)


def collect_body(mine_ref, home_ref, slots_ref, out_ref, wide_ref, count_ref):
    for target in range(N_ATTN):
        count_ref[target] = 0
    base = mine_ref[0] * ROWS
    for row in range(ROWS):
        target = home_ref[0, base + row]
        rank = count_ref[target]
        count_ref[target] = rank + 1
        heads = slots_ref[target * CAP + rank].astype(jnp.float32)
        for head in range(HEADS):
            wide_ref[row : row + 1, head * HD : (head + 1) * HD] = heads[head : head + 1]
    out_ref[...] = wide_ref[...].astype(jnp.bfloat16)


def collect(mine, home, slots):
    return pl.pallas_call(
        collect_body,
        out_shape=jax.ShapeDtypeStruct((ROWS, HEADS * HD), jnp.bfloat16),
        in_specs=[SMEM, SMEM, VMEM],
        out_specs=VMEM,
        scratch_shapes=[
            pltpu.VMEM((ROWS, HEADS * HD), jnp.float32),
            pltpu.SMEM((N_ATTN,), jnp.int32),
        ],
        compiler_params=params(),
    )(mine, home, slots)


TILE = 256


def project_body(count, picks_ref, rows_ref, weight_ref, out_ref):
    blocks = [rows_ref[picks_ref[2 * k], picks_ref[2 * k + 1]] for k in range(count)]
    lhs = jnp.concatenate(blocks, axis=0)
    out_ref[...] = jnp.dot(lhs, weight_ref[...], preferred_element_type=jnp.float32).astype(
        jnp.bfloat16
    )


def project(picks, rows, weight):
    count = picks.shape[0] // 2
    columns = weight.shape[1]
    return pl.pallas_call(
        functools.partial(project_body, count),
        out_shape=jax.ShapeDtypeStruct((count * ROWS, columns), jnp.bfloat16),
        grid_spec=pltpu.PrefetchScalarGridSpec(
            num_scalar_prefetch=1,
            grid=(columns // TILE,),
            in_specs=[
                pl.BlockSpec((SIDE, SIDE, ROWS, WIDTH), lambda n, _: (0, 0, 0, 0)),
                pl.BlockSpec((WIDTH, TILE), lambda n, _: (0, n)),
            ],
            out_specs=pl.BlockSpec((count * ROWS, TILE), lambda n, _: (0, n)),
        ),
        compiler_params=params(),
    )(picks, rows, weight)


def merge_body(picks_ref, own_ref, direct_ref, relayed_ref, one_ref, two_ref, three_ref, home_ref, sums_ref):
    sums_ref[...] = (
        own_ref[...].astype(jnp.float32)
        + direct_ref[...].astype(jnp.float32)
        + relayed_ref[...].astype(jnp.float32)
    )
    for k, out in enumerate((one_ref, two_ref, three_ref)):
        out[...] = sums_ref[picks_ref[k]].astype(jnp.bfloat16)
    home_ref[...] = sums_ref[picks_ref[3]]


def merge(picks, own, direct, relayed):
    columns = own.shape[-1]
    own, direct, relayed = (a.reshape(SIDE, ROWS, columns) for a in (own, direct, relayed))
    return pl.pallas_call(
        merge_body,
        out_shape=[jax.ShapeDtypeStruct((ROWS, columns), jnp.bfloat16)] * 3
        + [jax.ShapeDtypeStruct((ROWS, columns), jnp.float32)],
        in_specs=[SMEM] + [VMEM] * 3,
        out_specs=[VMEM] * 4,
        scratch_shapes=[pltpu.VMEM((SIDE, ROWS, columns), jnp.float32)],
        compiler_params=params(),
    )(picks, own, direct, relayed)


def along_z(x, shift):
    return lax.ppermute(
        x, "attn", [(y * SIDE + z, y * SIDE + (z + shift) % SIDE) for y in range(SIDE) for z in range(SIDE)]
    )


def along_y(x, shift):
    return lax.ppermute(
        x, "attn", [(y * SIDE + z, (y + shift) % SIDE * SIDE + z) for y in range(SIDE) for z in range(SIDE)]
    )


def to_sibling(x):
    return lax.ppermute(x, "ffn", [(f, f ^ 1) for f in range(8)])


def along_x(x):
    groups = [[chip * 2 + core for chip in range(SIDE)] for core in range(2)]
    return lax.all_to_all(x, "ffn", split_axis=0, concat_axis=0, axis_index_groups=groups, tiled=True)


def scatter_start(shift, pick, here, rows, weight):
    two, one, minus = (here + 2) % SIDE, (here + 1) % SIDE, (here + 3) % SIDE
    first = project(pick([(two, 0), (one, 1), (two, 1), (minus, 0)]), rows, weight)
    columns = weight.shape[1]
    first = first.reshape(2, 2 * SIDE * ROWS // 2, columns)
    up = shift(first[0], 1)
    down = shift(first[1], -1)
    return up, down


def scatter_finish(shift, cross, pick, here, there, up, down, rows, weight):
    columns = weight.shape[1]
    half = 2 * ROWS
    one, minus = (here + 1) % SIDE, (here + 3) % SIDE
    rest = project(pick([(one, 0), (minus, 1), (here, 0), (here, 1)]), rows, weight)
    f32 = jnp.float32
    up_next = (rest[:half].astype(f32) + up[:half].astype(f32)).astype(jnp.bfloat16)
    down_next = (rest[half : 2 * half].astype(f32) + down[:half].astype(f32)).astype(jnp.bfloat16)
    from_below = shift(up_next, 1)
    from_above = shift(down_next, -1)
    own = rest[2 * half :]
    direct = jnp.concatenate([down[half:], up[half:]], axis=0)
    relayed = jnp.concatenate([from_below, from_above], axis=0)
    picks = jnp.stack([(there + 1) % SIDE, (there + 2) % SIDE, (there + 3) % SIDE, there])
    one_on, two_on, three_on, mine = merge(picks, own, direct, relayed)
    return (mine, cross(one_on, 1), cross(two_on, 2), cross(three_on, 3))


def on_device(
    stream,
    queries,
    k_pool,
    v_pool,
    page_table,
    lengths,
    home_device,
    w_out,
    norm_gain,
    w_gate,
    w_up,
):
    f32 = jnp.float32
    attn = lax.axis_index("attn").astype(jnp.int32)
    ffn = lax.axis_index("ffn").astype(jnp.int32)
    chip, core = ffn // 2, ffn % 2
    y, z = attn // SIDE, attn % SIDE
    mine = attn.reshape(1)
    home = home_device.reshape(1, REQS)

    outgoing = dispatch(mine, home, queries.reshape(ROWS, HEADS, HD))
    arrived = lax.all_to_all(outgoing, "attn", split_axis=0, concat_axis=0, tiled=True)
    blended = attend(
        mine, home, lengths.reshape(1, REQS), page_table.T, arrived, k_pool, v_pool
    )
    returned = lax.all_to_all(blended, "attn", split_axis=0, concat_axis=0, tiled=True)
    attention = collect(mine, home, returned)
    gathered = lax.all_to_all(
        jnp.broadcast_to(attention[None], (N_ATTN,) + attention.shape),
        "attn",
        split_axis=0,
        concat_axis=0,
        tiled=True,
    ).reshape(REQS, HEADS * HD)
    partial = jnp.dot(gathered, w_out, preferred_element_type=f32).astype(jnp.bfloat16)

    half = REQS // 2
    part = half // SIDE
    kept = lax.dynamic_slice_in_dim(partial, core * half, half, 0)
    given = lax.dynamic_slice_in_dim(partial, (1 - core) * half, half, 0)
    pair = (kept.astype(f32) + to_sibling(given).astype(f32)).astype(jnp.bfloat16)
    pieces = along_x(pair.reshape(SIDE, part, WIDTH))
    stream_rows = lax.dynamic_slice_in_dim(stream, core * half + chip * part, part, 0)
    mine_rows = (stream_rows.astype(f32) + jnp.sum(pieces.astype(f32), axis=0)).astype(jnp.bfloat16)
    this_half = along_x(jnp.broadcast_to(mine_rows[None], (SIDE, part, WIDTH))).reshape(half, WIDTH)
    other_half = to_sibling(this_half)
    residual = jnp.where(
        core == 0,
        jnp.concatenate([this_half, other_half], axis=0),
        jnp.concatenate([other_half, this_half], axis=0),
    )
    widened = residual.astype(f32)
    squares = jnp.sum(widened * widened, axis=1)
    scaled = (widened * norm_gain.astype(f32)[None, :]).astype(jnp.bfloat16)
    rows = scaled.reshape(SIDE, SIDE, ROWS, WIDTH)

    def pick_z(pairs):
        return jnp.stack([i for at, h in pairs for k in (2 * h, 2 * h + 1) for i in (jnp.int32(k), at)])

    def pick_y(pairs):
        return jnp.stack([i for at, h in pairs for k in (2 * h, 2 * h + 1) for i in (at, jnp.int32(k))])

    square_sums = jnp.sum(
        lax.all_to_all(
            squares.reshape(N_ATTN, 1, ROWS), "attn", split_axis=0, concat_axis=0, tiled=True
        ),
        axis=(0, 1),
    )
    gate_up, gate_down = scatter_start(along_z, pick_z, z, rows, w_gate)
    up_up, up_down = scatter_start(along_y, pick_y, y, rows, w_up)
    gate_parts = scatter_finish(along_z, along_y, pick_z, z, y, gate_up, gate_down, rows, w_gate)
    up_parts = scatter_finish(along_y, along_z, pick_y, y, z, up_up, up_down, rows, w_up)
    scaling = lax.rsqrt(square_sums / D + EPS)[:, None]
    gate = sum(p.astype(f32) for p in gate_parts) * scaling
    up = sum(p.astype(f32) for p in up_parts) * scaling
    hidden = (jax.nn.silu(gate) * up).astype(jnp.bfloat16)
    return (residual, hidden)


def solution(mesh):
    return jax.shard_map(
        on_device,
        mesh=mesh,
        in_specs=(
            P(None, "attn"),
            P("attn", "ffn"),
            P("attn", None, "ffn"),
            P("attn", None, "ffn"),
            P(),
            P(),
            P(),
            P("ffn", "attn"),
            P("attn"),
            P("attn", "ffn"),
            P("attn", "ffn"),
        ),
        out_specs=(P(None, "attn"), P("attn", "ffn")),
        check_vma=False,
    )
```

time: 390 us -> 210 us (0.54)
  waiting for transfers between devices: 236 us -> 48.8 us
  Pallas kernels: 0 us -> 52 us
  matrix products: 38.3 us -> 4.51 us
  starting transfers between devices: 8.25 us -> 35 us
  local copies, waits for them, and re-layouts: 41.5 us -> 17.1 us
  between operations: 13.9 us -> 1.02 us
    psum x2 -> x0, waiting for transfers between devices: 183 us -> none  [the longest x1 121 us: on_device(): lax.psum(jnp.concatenate([gate_part, up_part], axis=1).astype(jnp.bfloat1...]
    all_gather x1 -> x0, waiting for transfers between devices: 53.2 us -> none  [on_device(): lax.all_gather(outputs_home, 'attn', axis=0, tiled=True)]
    pallas_call x0 -> x9, Pallas kernels: none -> 52 us  [the longest x4 40.7 us: project(): pl.pallas_call(functools.partial(project_body, count), out_shape=jax.Shap...]
    all_to_all x0 -> x3, blocking collectives: none -> 42.5 us  [the longest x1 16.4 us: on_device(): lax.all_to_all(outgoing, 'attn', split_axis=0, concat_axis=0, tiled=True)]
    psum x1 -> x0, blocking collectives: 40.8 us -> none  [on_device(): squares = lax.psum(jnp.sum(widened * widened, axis=1), 'attn')]
    all_to_all x1 -> x3, waiting for transfers between devices: 0.01 us -> 37.5 us  [the longest x1 27.8 us: on_device(): lax.all_to_all(jnp.broadcast_to(attention[None], (N_ATTN,) + attention.sh...]
    gather x5 -> x0, local copies, waits for them, and re-layouts: 37.4 us -> none  [the longest x1 16.3 us: attend(): key_rows = k_pool[page_rows].reshape(slot_count, -1, heads_kv, HD)]
    dot_general x5 -> x1, matrix products: 27.7 us -> 4.51 us  [on_device(): jnp.dot(gathered, w_out, preferred_element_type=f32).astype(jnp.bfloat16)]
  transfers between devices with their start and end apart: 4 -> 19, of which waited for: 3 -> 9; matrix products, arithmetic and copies ran while one was open for 9% -> 5% of each run, Pallas kernels for 0% -> 16%
where the time goes in v1:
time: 210 us; the launch traced here: 208 us
  Pallas kernels  52 us (25%)
  waiting for transfers between devices  48.8 us (23%)
  blocking collectives  42.5 us (20%)
  starting transfers between devices  35 us (17%)
  local copies, waits for them, and re-layouts  17.1 us (8%)
  other arithmetic  7.03 us (3%)
  matrix products  4.51 us (2%)
    pallas_call x4, Pallas kernels, project(): pl.pallas_call(functools.partial(project_body, count), out_shape=jax.Shap...  40.7 us
    all_to_all x1, waiting for transfers between devices, on_device(): lax.all_to_all(jnp.broadcast_to(attention[None], (N_ATTN,) + attention.sh...  27.8 us
    all_to_all x1, blocking collectives, on_device(): lax.all_to_all(outgoing, 'attn', split_axis=0, concat_axis=0, tiled=True)  16.4 us
    all_to_all x1, blocking collectives, on_device(): lax.all_to_all(blended, 'attn', split_axis=0, concat_axis=0, tiled=True)  14.8 us
    all_to_all x1, blocking collectives, along_x(): lax.all_to_all(x, 'ffn', split_axis=0, concat_axis=0, axis_index_groups=g...  11.3 us
    ppermute x7, starting transfers between devices, along_y(): lax.ppermute(x, 'attn', [(y * SIDE + z, (y + shift) % SIDE * SIDE + z) fo...  11.3 us
    ppermute x7, starting transfers between devices, along_z(): lax.ppermute(x, 'attn', [(y * SIDE + z, y * SIDE + (z + shift) % SIDE) fo...  11 us
    all_to_all x1, waiting for transfers between devices, along_x(): lax.all_to_all(x, 'ffn', split_axis=0, concat_axis=0, axis_index_groups=g...  9.78 us
  transfers between devices with their start and end apart: 19, of which 9 were waited for; matrix products, arithmetic and copies ran while one was open for 5% of the time, Pallas kernels for 16%

profile of v1, /device:TPU:0, one launch (start us, length us, event | category | flops | bytes accessed | tf_op | source)
XLA Modules:
  0.0 208.0 jit_solution(1155241989171542666)
XLA Ops:
  3.0 16.4 %all_to_all.30.queries_ref = bf16[64,16,128]{2,1,0:T(8,128)(2,1)S(1)} all-to-all(bf16[64,16,128]{2,1,0:T(8,128)(2,1)S(1)} %shard_map.122), channel_id=1, replica_groups=mesh['attn'=16,'ffn'=8] {'attn'}, dimensions={0} | all-to-all | bytes 524288 | tf_op jit(solution)/shard_map/all_to_all | solution.py:295
  24.1 7.5 %shard_map.123 = bf16[64,16,128]{2,1,0:T(8,128)(2,1)S(1)} custom-call(s32[1]{0:T(128)} %bitcast.mine_ref, s32[1,512]{1,0:T(1,128)S(1)} %bitcast.37, s32[1,512]{1,0:T(1,128)S(1)} %bitcast.39, s32[32,512]{1,0:T(8,128)S(1)} %bitcast.35, bf16[64,16,128]{2,1,0:T(8,128)(2,1)S(1)} %all_to_all.30.queries_ref, bf16[256,16,128]{2,1,0:T(8,128)(2,1)S(1)} %copy-done.2, ...), custom_call_target="tpu_custom_call" | custom-call | tf_op jit(solution)/shard_map/pallas_call | solution.py:128
  31.6 14.8 %all_to_all.31.slots_ref = bf16[64,16,128]{2,1,0:T(8,128)(2,1)S(1)} all-to-all(bf16[64,16,128]{2,1,0:T(8,128)(2,1)S(1)} %shard_map.123), channel_id=1, replica_groups=mesh['attn'=16,'ffn'=8] {'attn'}, dimensions={0} | all-to-all | bytes 524288 | tf_op jit(solution)/shard_map/all_to_all | solution.py:299
  47.2 1.6 broadcast_in_dim.4
  48.8 3.7 %all-to-all-start.2 = ((bf16[16,32,2048]{2,1,0:T(8,128)(2,1)}), bf16[16,32,2048]{2,1,0:T(8,128)(2,1)S(1)}, u32[]{:S(2)}, u32[]{:S(2)}) async-start(bf16[16,32,2048]{2,1,0:T(8,128)(2,1)} %broadcast_in_dim.4), calls=%async_computation.2 | async-start | bytes 4194304 | tf_op jit(solution)/shard_map/all_to_all | solution.py:301
  52.5 27.8 %all-to-all-done.2 = bf16[16,32,2048]{2,1,0:T(8,128)(2,1)S(1)} async-done(((bf16[16,32,2048]{2,1,0:T(8,128)(2,1)}), bf16[16,32,2048]{2,1,0:T(8,128)(2,1)S(1)}, u32[]{:S(2)}, u32[]{:S(2)}) %all-to-all-start.2) | async-done | bytes 2097184 | tf_op jit(solution)/shard_map/all_to_all | solution.py:301
  80.3 4.5 %convolution_convert_fusion = bf16[512,1024]{1,0:T(8,128)(2,1)S(1)} fusion(bf16[512,2048]{1,0:T(8,128)(2,1)S(1)} %bitcast.41, bf16[2048,1024]{1,0:T(8,128)(2,1)} %param.18), kind=kOutput, calls=%fused_computation.2 | convolution fusion | flops 2148007936 | bytes 7340032 | tf_op jit(solution)/shard_map/dot_general | solution.py:308
  85.0 1.9 collective-permute-done
  87.9 4.4 %all-to-all-start.3 = ((bf16[4,64,1024]{2,1,0:T(8,128)(2,1)}), bf16[4,64,1024]{2,1,0:T(8,128)(2,1)S(1)}, u32[]{:S(2)}, u32[]{:S(2)}) async-start(bf16[4,64,1024]{2,1,0:T(8,128)(2,1)} %bitcast.5), calls=%async_computation.3 | async-start | bytes 1048576 | tf_op jit(solution)/shard_map/all_to_all | solution.py:242
  92.3 9.8 %all-to-all-done.3 = bf16[4,64,1024]{2,1,0:T(8,128)(2,1)S(1)} async-done(((bf16[4,64,1024]{2,1,0:T(8,128)(2,1)}), bf16[4,64,1024]{2,1,0:T(8,128)(2,1)S(1)}, u32[]{:S(2)}, u32[]{:S(2)}) %all-to-all-start.3) | async-done | bytes 524320 | tf_op jit(solution)/shard_map/all_to_all | solution.py:242
  103.1 11.3 %all_to_all.32 = bf16[4,64,1024]{2,1,0:T(8,128)(2,1)S(1)} all-to-all(bf16[4,64,1024]{2,1,0:T(8,128)(2,1)S(1)} %broadcast_in_dim.5), channel_id=1, replica_groups={{0,2,4,6},{1,3,5,7},{8,10,12,14},{9,11,13,15},{16,18,20,22},{17,19,21,2..., dimensions={0} | all-to-all | bytes 1048576 | tf_op jit(solution)/shard_map/all_to_all | solution.py:242
  117.1 10.2 %shard_map.126 = bf16[256,3328]{1,0:T(8,128)(2,1)S(1)} custom-call(s32[16]{0:T(128)S(1)} %stack.38.picks_ref, bf16[4,4,32,1024]{3,2,1,0:T(8,128)(2,1)S(1)} %multiply_convert_fusion.rows_ref, bf16[1024,3328]{1,0:T(8,128)(2,1)} %weight_ref.5), custom_call_target="tpu_custom_call" | custom-call | tf_op jit(solution)/shard_map/pallas_call | solution.py:183
  131.3 4.5 %all-to-all-start.5 = ((f32[16,1,32]{2,1,0:T(1,128)}), f32[16,1,32]{2,1,0:T(1,128)S(1)}, u32[]{:S(2)}, u32[]{:S(2)}) async-start(f32[16,1,32]{2,1,0:T(1,128)} %reshape.86), calls=%async_computation.5 | async-start | bytes 16384 | tf_op jit(solution)/shard_map/all_to_all | solution.py:337
  135.8 10.2 %shard_map.129 = bf16[256,3328]{1,0:T(8,128)(2,1)S(1)} custom-call(s32[16]{0:T(128)S(1)} %stack.41.picks_ref, bf16[4,4,32,1024]{3,2,1,0:T(8,128)(2,1)S(1)} %multiply_convert_fusion.rows_ref, bf16[1024,3328]{1,0:T(8,128)(2,1)} %weight_ref.7), custom_call_target="tpu_custom_call" | custom-call | tf_op jit(solution)/shard_map/pallas_call | solution.py:183
  147.4 10.2 %shard_map.125 = bf16[256,3328]{1,0:T(8,128)(2,1)S(1)} custom-call(s32[16]{0:T(128)S(1)} %stack.36.picks_ref, bf16[4,4,32,1024]{3,2,1,0:T(8,128)(2,1)S(1)} %multiply_convert_fusion.rows_ref, bf16[1024,3328]{1,0:T(8,128)(2,1)} %weight_ref.5), custom_call_target="tpu_custom_call" | custom-call | tf_op jit(solution)/shard_map/pallas_call | solution.py:183
  158.6 1.9 collective-permute-start.10
  160.5 1.7 collective-permute-start.9
  162.2 10.2 %shard_map.128 = bf16[256,3328]{1,0:T(8,128)(2,1)S(1)} custom-call(s32[16]{0:T(128)S(1)} %stack.40.picks_ref, bf16[4,4,32,1024]{3,2,1,0:T(8,128)(2,1)S(1)} %multiply_convert_fusion.rows_ref, bf16[1024,3328]{1,0:T(8,128)(2,1)} %weight_ref.7), custom_call_target="tpu_custom_call" | custom-call | tf_op jit(solution)/shard_map/pallas_call | solution.py:183
  175.7 1.7 collective-permute-start.5
  177.4 2.9 %collective-permute-done.10 = bf16[128,3328]{1,0:T(8,128)(2,1)} collective-permute-done((bf16[128,3328]{1,0:T(8,128)(2,1)}, bf16[128,3328]{1,0:T(8,128)(2,1)}, u32[]{:S(2)}, u32[]{:S(2)}) %collective-permute-start.10) | collective-permute-done | bytes 852000 | tf_op jit(solution)/shard_map/ppermute | solution.py:231
  183.3 1.8 collective-permute-start.12
  191.2 3.2 %collective-permute-start.7 = (bf16[32,3328]{1,0:T(8,128)(2,1)S(1)}, bf16[32,3328]{1,0:T(8,128)(2,1)S(1)}, u32[]{:S(2)}, u32[]{:S(2)}) collective-permute-start(bf16[32,3328]{1,0:T(8,128)(2,1)S(1)} %get-tuple-element.12), channel_id=1, source_target_pairs={{0,64},{8,72},{16,80},{24,88},{32,96},{40,104},{48,112},{56,120},{... | collective-permute-start | bytes 638984 | tf_op jit(solution)/shard_map/ppermute | solution.py:231
  197.8 2.7 %collective-permute-start.14 = (bf16[32,3328]{1,0:T(8,128)(2,1)S(1)}, bf16[32,3328]{1,0:T(8,128)(2,1)S(1)}, u32[]{:S(2)}, u32[]{:S(2)}) collective-permute-start(bf16[32,3328]{1,0:T(8,128)(2,1)S(1)} %get-tuple-element.16), channel_id=1, source_target_pairs={{0,16},{8,24},{16,0},{24,8},{32,48},{40,56},{48,32},{56,40},{64,80... | collective-permute-start | bytes 638984 | tf_op jit(solution)/shard_map/ppermute | solution.py:225
  204.7 2.3 %collective-permute-done.14 = bf16[32,3328]{1,0:T(8,128)(2,1)S(1)} collective-permute-done((bf16[32,3328]{1,0:T(8,128)(2,1)S(1)}, bf16[32,3328]{1,0:T(8,128)(2,1)S(1)}, u32[]{:S(2)}, u32[]{:S(2)}) %collective-permute-start.14) | collective-permute-done | bytes 213024 | tf_op jit(solution)/shard_map/ppermute | solution.py:225
  (81 shorter events, 39.9 us)
Async XLA Ops:
  19.4 1.2 copy-start.2
  48.8 31.5 %all-to-all-start.2 = ((bf16[16,32,2048]{2,1,0:T(8,128)(2,1)}), bf16[16,32,2048]{2,1,0:T(8,128)(2,1)S(1)}, u32[]{:S(2)}, u32[]{:S(2)}) async-start(bf16[16,32,2048]{2,1,0:T(8,128)(2,1)} %broadcast_in_dim.4), calls=%async_computation.2 | async-start | bytes 4194304 | tf_op jit(solution)/shard_map/all_to_all | solution.py:301
  84.9 2.0 collective-permute-start
  87.9 26.6 %copy-start.9 = (bf16[1024]{0:T(1024)(128)(2,1)S(1)}, bf16[1024]{0:T(1024)(128)(2,1)}, u32[]{:S(2)}) copy-start(bf16[1024]{0:T(1024)(128)(2,1)} %param.19) | copy-start | bytes 6148
  87.9 14.2 %all-to-all-start.3 = ((bf16[4,64,1024]{2,1,0:T(8,128)(2,1)}), bf16[4,64,1024]{2,1,0:T(8,128)(2,1)S(1)}, u32[]{:S(2)}, u32[]{:S(2)}) async-start(bf16[4,64,1024]{2,1,0:T(8,128)(2,1)} %bitcast.5), calls=%async_computation.3 | async-start | bytes 1048576 | tf_op jit(solution)/shard_map/all_to_all | solution.py:242
  114.4 1.9 collective-permute-start.1
  116.8 10.5 %copy-start.8 = (bf16[512,1024]{1,0:T(8,128)(2,1)}, bf16[512,1024]{1,0:T(8,128)(2,1)S(1)}, u32[]{:S(2)}) copy-start(bf16[512,1024]{1,0:T(8,128)(2,1)S(1)} %get-tuple-element.19) | copy-start | bytes 3145732
  128.6 43.9 %collective-permute-start.2 = (bf16[128,3328]{1,0:T(8,128)(2,1)}, bf16[128,3328]{1,0:T(8,128)(2,1)}, u32[]{:S(2)}, u32[]{:S(2)}) collective-permute-start(bf16[128,3328]{1,0:T(8,128)(2,1)} %get-tuple-element.22), channel_id=1, source_target_pairs={{0,24},{8,0},{16,8},{24,16},{32,56},{40,32},{48,40},{56,48},{64,88... | collective-permute-start | bytes 2555912 | tf_op jit(solution)/shard_map/ppermute | solution.py:225
  129.3 43.2 %collective-permute-start.3 = (bf16[128,3328]{1,0:T(8,128)(2,1)}, bf16[128,3328]{1,0:T(8,128)(2,1)}, u32[]{:S(2)}, u32[]{:S(2)}) collective-permute-start(bf16[128,3328]{1,0:T(8,128)(2,1)} %get-tuple-element.23), channel_id=1, source_target_pairs={{0,8},{8,16},{16,24},{24,0},{32,40},{40,48},{48,56},{56,32},{64,72... | collective-permute-start | bytes 2555912 | tf_op jit(solution)/shard_map/ppermute | solution.py:225
  131.3 41.1 %all-to-all-start.5 = ((f32[16,1,32]{2,1,0:T(1,128)}), f32[16,1,32]{2,1,0:T(1,128)S(1)}, u32[]{:S(2)}, u32[]{:S(2)}) async-start(f32[16,1,32]{2,1,0:T(1,128)} %reshape.86), calls=%async_computation.5 | async-start | bytes 16384 | tf_op jit(solution)/shard_map/all_to_all | solution.py:337
  157.5 3.0 %copy-start = (bf16[256,3328]{1,0:T(8,128)(2,1)}, bf16[256,3328]{1,0:T(8,128)(2,1)S(1)}, u32[]{:S(2)}) copy-start(bf16[256,3328]{1,0:T(8,128)(2,1)S(1)} %shard_map.125) | copy-start | bytes 5111812
  158.6 21.7 %collective-permute-start.10 = (bf16[128,3328]{1,0:T(8,128)(2,1)}, bf16[128,3328]{1,0:T(8,128)(2,1)}, u32[]{:S(2)}, u32[]{:S(2)}) collective-permute-start(bf16[128,3328]{1,0:T(8,128)(2,1)} %get-tuple-element.27), channel_id=1, source_target_pairs={{0,32},{8,40},{16,48},{24,56},{32,64},{40,72},{48,80},{56,88},{64,... | collective-permute-start | bytes 2555912 | tf_op jit(solution)/shard_map/ppermute | solution.py:231
  160.5 19.9 %collective-permute-start.9 = (bf16[128,3328]{1,0:T(8,128)(2,1)}, bf16[128,3328]{1,0:T(8,128)(2,1)}, u32[]{:S(2)}, u32[]{:S(2)}) collective-permute-start(bf16[128,3328]{1,0:T(8,128)(2,1)} %get-tuple-element.26), channel_id=1, source_target_pairs={{0,96},{8,104},{16,112},{24,120},{32,0},{40,8},{48,16},{56,24},{64... | collective-permute-start | bytes 2555912 | tf_op jit(solution)/shard_map/ppermute | solution.py:231
  174.1 15.4 %collective-permute-start.4 = (bf16[64,3328]{1,0:T(8,128)(2,1)S(1)}, bf16[64,3328]{1,0:T(8,128)(2,1)S(1)}, u32[]{:S(2)}, u32[]{:S(2)}) collective-permute-start(bf16[64,3328]{1,0:T(8,128)(2,1)S(1)} %get-tuple-element.20), channel_id=1, source_target_pairs={{0,8},{8,16},{16,24},{24,0},{32,40},{40,48},{48,56},{56,32},{64,72... | collective-permute-start | bytes 1277960 | tf_op jit(solution)/shard_map/ppermute | solution.py:225
  175.7 13.8 %collective-permute-start.5 = (bf16[64,3328]{1,0:T(8,128)(2,1)S(1)}, bf16[64,3328]{1,0:T(8,128)(2,1)S(1)}, u32[]{:S(2)}, u32[]{:S(2)}) collective-permute-start(bf16[64,3328]{1,0:T(8,128)(2,1)S(1)} %get-tuple-element.21), channel_id=1, source_target_pairs={{0,24},{8,0},{16,8},{24,16},{32,56},{40,32},{48,40},{56,48},{64,88... | collective-permute-start | bytes 1277960 | tf_op jit(solution)/shard_map/ppermute | solution.py:225
  181.8 13.3 %collective-permute-start.11 = (bf16[64,3328]{1,0:T(8,128)(2,1)S(1)}, bf16[64,3328]{1,0:T(8,128)(2,1)S(1)}, u32[]{:S(2)}, u32[]{:S(2)}) collective-permute-start(bf16[64,3328]{1,0:T(8,128)(2,1)S(1)} %get-tuple-element.24), channel_id=1, source_target_pairs={{0,32},{8,40},{16,48},{24,56},{32,64},{40,72},{48,80},{56,88},{64,... | collective-permute-start | bytes 1277960 | tf_op jit(solution)/shard_map/ppermute | solution.py:231
  183.3 11.8 %collective-permute-start.12 = (bf16[64,3328]{1,0:T(8,128)(2,1)S(1)}, bf16[64,3328]{1,0:T(8,128)(2,1)S(1)}, u32[]{:S(2)}, u32[]{:S(2)}) collective-permute-start(bf16[64,3328]{1,0:T(8,128)(2,1)S(1)} %get-tuple-element.25), channel_id=1, source_target_pairs={{0,96},{8,104},{16,112},{24,120},{32,0},{40,8},{48,16},{56,24},{64... | collective-permute-start | bytes 1277960 | tf_op jit(solution)/shard_map/ppermute | solution.py:231
  188.3 1.3 copy-start.1
  190.7 9.7 %collective-permute-start.6 = (bf16[32,3328]{1,0:T(8,128)(2,1)S(1)}, bf16[32,3328]{1,0:T(8,128)(2,1)S(1)}, u32[]{:S(2)}, u32[]{:S(2)}) collective-permute-start(bf16[32,3328]{1,0:T(8,128)(2,1)S(1)} %get-tuple-element.11), channel_id=1, source_target_pairs={{0,32},{8,40},{16,48},{24,56},{32,64},{40,72},{48,80},{56,88},{64,... | collective-permute-start | bytes 638984 | tf_op jit(solution)/shard_map/ppermute | solution.py:231
  191.2 12.2 %collective-permute-start.7 = (bf16[32,3328]{1,0:T(8,128)(2,1)S(1)}, bf16[32,3328]{1,0:T(8,128)(2,1)S(1)}, u32[]{:S(2)}, u32[]{:S(2)}) collective-permute-start(bf16[32,3328]{1,0:T(8,128)(2,1)S(1)} %get-tuple-element.12), channel_id=1, source_target_pairs={{0,64},{8,72},{16,80},{24,88},{32,96},{40,104},{48,112},{56,120},{... | collective-permute-start | bytes 638984 | tf_op jit(solution)/shard_map/ppermute | solution.py:231
  194.4 9.0 %collective-permute-start.8 = (bf16[32,3328]{1,0:T(8,128)(2,1)S(1)}, bf16[32,3328]{1,0:T(8,128)(2,1)S(1)}, u32[]{:S(2)}, u32[]{:S(2)}) collective-permute-start(bf16[32,3328]{1,0:T(8,128)(2,1)S(1)} %get-tuple-element.13), channel_id=1, source_target_pairs={{0,96},{8,104},{16,112},{24,120},{32,0},{40,8},{48,16},{56,24},{64... | collective-permute-start | bytes 638984 | tf_op jit(solution)/shard_map/ppermute | solution.py:231
  196.3 8.5 %collective-permute-start.13 = (bf16[32,3328]{1,0:T(8,128)(2,1)S(1)}, bf16[32,3328]{1,0:T(8,128)(2,1)S(1)}, u32[]{:S(2)}, u32[]{:S(2)}) collective-permute-start(bf16[32,3328]{1,0:T(8,128)(2,1)S(1)} %get-tuple-element.15), channel_id=1, source_target_pairs={{0,8},{8,16},{16,24},{24,0},{32,40},{40,48},{48,56},{56,32},{64,72... | collective-permute-start | bytes 638984 | tf_op jit(solution)/shard_map/ppermute | solution.py:225
  197.8 9.2 %collective-permute-start.14 = (bf16[32,3328]{1,0:T(8,128)(2,1)S(1)}, bf16[32,3328]{1,0:T(8,128)(2,1)S(1)}, u32[]{:S(2)}, u32[]{:S(2)}) collective-permute-start(bf16[32,3328]{1,0:T(8,128)(2,1)S(1)} %get-tuple-element.16), channel_id=1, source_target_pairs={{0,16},{8,24},{16,0},{24,8},{32,48},{40,56},{48,32},{56,40},{64,80... | collective-permute-start | bytes 638984 | tf_op jit(solution)/shard_map/ppermute | solution.py:225
  200.5 6.5 %collective-permute-start.15 = (bf16[32,3328]{1,0:T(8,128)(2,1)S(1)}, bf16[32,3328]{1,0:T(8,128)(2,1)S(1)}, u32[]{:S(2)}, u32[]{:S(2)}) collective-permute-start(bf16[32,3328]{1,0:T(8,128)(2,1)S(1)} %get-tuple-element.17), channel_id=1, source_target_pairs={{0,24},{8,0},{16,8},{24,16},{32,56},{40,32},{48,40},{56,48},{64,88... | collective-permute-start | bytes 638984 | tf_op jit(solution)/shard_map/ppermute | solution.py:225
  (5 other events, 4.1 us)

commit v2 on v1

v2 whole, which is shorter than its diff:
```python
import functools
import jax
import jax.numpy as jnp
from jax import lax
from jax.experimental import pallas as pl
from jax.experimental.pallas import tpu as pltpu
from jax.sharding import PartitionSpec as P

D = 16384
HD = 128
HEADS = 16
PAGE = 16
MAXP = 32
CTX = PAGE * MAXP
REQS = 512
N_ATTN = 16
ROWS = 32
CAP = 4
SLOTS = N_ATTN * CAP
SIDE = 4
WIDTH = 1024
GROUP = 4
EPS = 1e-05

SMEM = pl.BlockSpec(memory_space=pltpu.SMEM)
VMEM = pl.BlockSpec(memory_space=pltpu.VMEM)
HBM = pl.BlockSpec(memory_space=pltpu.HBM)


WIDE = 58


def params(mebibytes=16):
    return pltpu.CompilerParams(vmem_limit_bytes=mebibytes * 1024 * 1024)


def start_all(copies):
    for copy in copies:
        copy.start()
    return copies


def dispatch_body(mine_ref, home_hbm, queries_hbm, out_ref, queries_ref, tall_ref, home_ref, count_ref, sems):
    pairs = ((home_hbm, home_ref), (queries_hbm, queries_ref))
    copies = start_all([pltpu.make_async_copy(a, b, sems.at[k]) for k, (a, b) in enumerate(pairs)])
    out_ref[...] = jnp.zeros_like(out_ref)
    for copy in copies:
        copy.wait()
    for head in range(HEADS):
        tall_ref[pl.ds(head, ROWS, stride=HEADS), :] = queries_ref[
            :, head * HD : (head + 1) * HD
        ].astype(jnp.float32)
    for target in range(N_ATTN):
        count_ref[target] = 0
    base = mine_ref[0] * ROWS
    for row in range(ROWS):
        target = home_ref[0, base + row]
        rank = count_ref[target]
        count_ref[target] = rank + 1
        out_ref[target * CAP + rank] = tall_ref[row * HEADS : (row + 1) * HEADS].astype(jnp.bfloat16)


def dispatch(mine, home, queries):
    return pl.pallas_call(
        dispatch_body,
        out_shape=jax.ShapeDtypeStruct((SLOTS, HEADS, HD), jnp.bfloat16),
        in_specs=[SMEM, HBM, HBM],
        out_specs=VMEM,
        scratch_shapes=[
            pltpu.VMEM((ROWS, HEADS * HD), jnp.bfloat16),
            pltpu.VMEM((ROWS * HEADS, HD), jnp.float32),
            pltpu.SMEM((1, REQS), jnp.int32),
            pltpu.SMEM((N_ATTN,), jnp.int32),
            pltpu.SemaphoreType.DMA((2,)),
        ],
        compiler_params=params(WIDE),
    )(mine, home, queries)


def attend_body(
    mine_ref,
    home_hbm,
    lengths_hbm,
    table_hbm,
    queries_ref,
    k_hbm,
    v_hbm,
    out_ref,
    home_ref,
    lengths_ref,
    table_ref,
    k_ref,
    v_ref,
    ids_ref,
    slots_ref,
    sems,
):
    pairs = (
        (home_hbm, home_ref),
        (lengths_hbm, lengths_ref),
        (table_hbm, table_ref),
        (k_hbm, k_ref),
        (v_hbm, v_ref),
    )
    copies = start_all([pltpu.make_async_copy(a, b, sems.at[k]) for k, (a, b) in enumerate(pairs)])
    mine = mine_ref[0]
    out_ref[...] = jnp.zeros_like(out_ref)
    copies[0].wait()

    def scan_source(source, found):
        start = found
        for row in range(ROWS):
            request = source * ROWS + row
            ids_ref[found] = request
            slots_ref[found] = source * CAP + found - start
            found = found + jnp.where(home_ref[0, request] == mine, 1, 0)
        return found

    found = lax.fori_loop(0, N_ATTN, scan_source, jnp.int32(0))
    last = jnp.maximum(found - 1, 0)
    last_id = ids_ref[last]
    last_slot = slots_ref[last]
    for extra in range(GROUP):
        ids_ref[found + extra] = last_id
        slots_ref[found + extra] = last_slot
    for copy in copies[1:]:
        copy.wait()

    positions = lax.broadcasted_iota(jnp.int32, (HEADS, CTX), 1)

    def step(index, carry):
        chosen = []
        for member in range(GROUP):
            place = index * GROUP + member
            request = ids_ref[place]
            slot = slots_ref[place]
            pages = [table_ref[page, request] for page in range(MAXP)]
            chosen.append((request, slot, pages))
        scores = []
        for request, slot, pages in chosen:
            keys = jnp.concatenate([k_ref[page] for page in pages], axis=0)
            scores.append(
                lax.dot_general(
                    queries_ref[slot],
                    keys,
                    (((1,), (1,)), ((), ())),
                    preferred_element_type=jnp.float32,
                )
                * HD ** (-0.5)
            )
        outputs = []
        for (request, slot, pages), score in zip(chosen, scores):
            visible = positions < lengths_ref[0, request]
            maxima = jnp.max(jnp.where(visible, score, -jnp.inf), axis=1, keepdims=True)
            weights = jnp.where(visible, jnp.exp(score - maxima), 0.0)
            totals = jnp.sum(weights, axis=1, keepdims=True)
            outputs.append((weights.astype(jnp.bfloat16), totals))
        for (request, slot, pages), (weights, totals) in zip(chosen, outputs):
            values = jnp.concatenate([v_ref[page] for page in pages], axis=0)
            blended = jnp.dot(weights, values, preferred_element_type=jnp.float32)
            out_ref[slot] = (blended / totals).astype(jnp.bfloat16)
        return carry

    lax.fori_loop(0, (found + GROUP - 1) // GROUP, step, 0)


def attend(mine, home, lengths, table, queries, k_pool, v_pool):
    return pl.pallas_call(
        attend_body,
        out_shape=jax.ShapeDtypeStruct((SLOTS, HEADS, HD), jnp.bfloat16),
        in_specs=[SMEM, HBM, HBM, HBM, VMEM, HBM, HBM],
        out_specs=VMEM,
        scratch_shapes=[
            pltpu.SMEM(home.shape, jnp.int32),
            pltpu.SMEM(lengths.shape, jnp.int32),
            pltpu.SMEM(table.shape, jnp.int32),
            pltpu.VMEM(k_pool.shape, jnp.bfloat16),
            pltpu.VMEM(v_pool.shape, jnp.bfloat16),
            pltpu.SMEM((SLOTS + GROUP + 4,), jnp.int32),
            pltpu.SMEM((SLOTS + GROUP + 4,), jnp.int32),
            pltpu.SemaphoreType.DMA((5,)),
        ],
        compiler_params=params(WIDE),
    )(mine, home, lengths, table, queries, k_pool, v_pool)


def collect_body(mine_ref, home_hbm, slots_ref, out_hbm, wide_ref, whole_ref, home_ref, count_ref, sem, sems):
    copy = pltpu.make_async_copy(home_hbm, home_ref, sem)
    copy.start()
    for target in range(N_ATTN):
        count_ref[target] = 0
    base = mine_ref[0] * ROWS
    copy.wait()
    for row in range(ROWS):
        target = home_ref[0, base + row]
        rank = count_ref[target]
        count_ref[target] = rank + 1
        heads = slots_ref[target * CAP + rank].astype(jnp.float32)
        for head in range(HEADS):
            wide_ref[row : row + 1, head * HD : (head + 1) * HD] = heads[head : head + 1]
    whole_ref[...] = wide_ref[...].astype(jnp.bfloat16)
    copies = start_all(
        [pltpu.make_async_copy(whole_ref, out_hbm.at[k], sems.at[k]) for k in range(N_ATTN)]
    )
    for copy in copies:
        copy.wait()


def collect(mine, home, slots):
    return pl.pallas_call(
        collect_body,
        out_shape=jax.ShapeDtypeStruct((N_ATTN, ROWS, HEADS * HD), jnp.bfloat16),
        in_specs=[SMEM, HBM, VMEM],
        out_specs=HBM,
        scratch_shapes=[
            pltpu.VMEM((ROWS, HEADS * HD), jnp.float32),
            pltpu.VMEM((ROWS, HEADS * HD), jnp.bfloat16),
            pltpu.SMEM((1, REQS), jnp.int32),
            pltpu.SMEM((N_ATTN,), jnp.int32),
            pltpu.SemaphoreType.DMA,
            pltpu.SemaphoreType.DMA((N_ATTN,)),
        ],
        compiler_params=params(),
    )(mine, home, slots)


def fetch_body(place_ref, out_hbm, gate_hbm, up_hbm, stream_hbm, gain_hbm, after_hbm, *refs):
    out_ref, gate_ref, up_ref, stream_ref, gain_ref, sems = refs
    part = stream_ref.shape[0]
    first = pl.multiple_of(place_ref[3] * (SIDE * part) + place_ref[2] * part, part)
    pairs = (
        (out_hbm, out_ref),
        (gate_hbm, gate_ref),
        (up_hbm, up_ref),
        (stream_hbm.at[pl.ds(first, part)], stream_ref),
        (gain_hbm, gain_ref),
    )
    copies = start_all([pltpu.make_async_copy(a, b, sems.at[k]) for k, (a, b) in enumerate(pairs)])
    for copy in copies:
        copy.wait()


def fetch(place, weights, stream, gain, after):
    shapes = [w.shape for w in weights] + [(REQS // 8, WIDTH), gain.shape]
    return pl.pallas_call(
        fetch_body,
        out_shape=[jax.ShapeDtypeStruct(shape, jnp.bfloat16) for shape in shapes],
        in_specs=[SMEM] + [HBM] * 6,
        out_specs=[VMEM] * 5,
        scratch_shapes=[pltpu.SemaphoreType.DMA((5,))],
        compiler_params=params(40),
    )(place, *weights, stream, gain, after)


def half_body(sibling, place_ref, rows_ref, weight_ref, out_ref):
    core = place_ref[3]
    which = 1 - core if sibling else core
    out_ref[...] = jnp.dot(
        rows_ref[which], weight_ref[...], preferred_element_type=jnp.float32
    ).astype(jnp.bfloat16)


def half_project(sibling, place, rows, weight):
    return pl.pallas_call(
        functools.partial(half_body, sibling),
        out_shape=jax.ShapeDtypeStruct((rows.shape[1], weight.shape[1]), jnp.bfloat16),
        in_specs=[SMEM, VMEM, VMEM],
        out_specs=VMEM,
        compiler_params=params(),
    )(place, rows, weight)


def relative(at):
    return [(at + 1) % SIDE, (at + 2) % SIDE, (at + 3) % SIDE, at]


def pair_body(place_ref, kept_ref, came_ref, one_ref, two_ref, three_ref, own_ref):
    for at, out in zip(relative(place_ref[2]), (one_ref, two_ref, three_ref, own_ref)):
        out[...] = (kept_ref[at].astype(jnp.float32) + came_ref[at].astype(jnp.float32)).astype(out.dtype)


def pair(place, kept, came):
    part = kept.shape[0] // SIDE
    shape = (part, WIDTH)
    return pl.pallas_call(
        pair_body,
        out_shape=[jax.ShapeDtypeStruct(shape, jnp.bfloat16)] * 3
        + [jax.ShapeDtypeStruct(shape, jnp.float32)],
        in_specs=[SMEM, VMEM, VMEM],
        out_specs=[VMEM] * 4,
        compiler_params=params(),
    )(place, kept.reshape(SIDE, part, WIDTH), came.reshape(SIDE, part, WIDTH))


def settle_body(stream_ref, own_ref, a_ref, b_ref, c_ref, out_ref):
    total = own_ref[...]
    for piece in (a_ref, b_ref, c_ref):
        total = total + piece[...].astype(jnp.float32)
    out_ref[...] = (stream_ref[...].astype(jnp.float32) + total).astype(jnp.bfloat16)


def settle(stream_rows, own, pieces):
    return pl.pallas_call(
        settle_body,
        out_shape=jax.ShapeDtypeStruct(own.shape, jnp.bfloat16),
        in_specs=[VMEM] * 5,
        out_specs=VMEM,
        compiler_params=params(),
    )(stream_rows, own, *pieces)


def lay_body(place_ref, one_ref, two_ref, three_ref, own_ref, out_ref):
    for at, block in zip(relative(place_ref[2]), (one_ref, two_ref, three_ref, own_ref)):
        out_ref[at] = block[...]


def lay(place, blocks):
    return pl.pallas_call(
        lay_body,
        out_shape=jax.ShapeDtypeStruct((SIDE,) + blocks[0].shape, jnp.bfloat16),
        in_specs=[SMEM] + [VMEM] * 4,
        out_specs=VMEM,
        compiler_params=params(),
    )(place, *blocks)


def assemble_body(place_ref, this_ref, other_ref, gain_ref, residual_ref, rows_ref, squares_ref):
    core = place_ref[3]
    gain = gain_ref[...].astype(jnp.float32)
    for which, half_ref in ((core, this_ref), (1 - core, other_ref)):
        size = half_ref.shape[0]
        residual_ref[pl.ds(pl.multiple_of(which * size, size), size), :] = half_ref[...]
        widened = half_ref[...].astype(jnp.float32)
        totals = jnp.sum(widened * widened, axis=1, keepdims=True)
        first = which * (SIDE // 2)
        rows_ref[pl.ds(first, SIDE // 2)] = (
            (widened * gain).astype(jnp.bfloat16).reshape(SIDE // 2, SIDE, ROWS, WIDTH)
        )
        squares_ref[pl.ds(first, SIDE // 2)] = jnp.broadcast_to(totals, (size, HD)).reshape(
            SIDE // 2, SIDE, ROWS, HD
        )


def assemble(place, this_half, other_half, gain):
    return pl.pallas_call(
        assemble_body,
        out_shape=[
            jax.ShapeDtypeStruct((REQS, WIDTH), jnp.bfloat16),
            jax.ShapeDtypeStruct((SIDE, SIDE, ROWS, WIDTH), jnp.bfloat16),
            jax.ShapeDtypeStruct((SIDE, SIDE, ROWS, HD), jnp.float32),
        ],
        in_specs=[SMEM] + [VMEM] * 3,
        out_specs=[VMEM] * 3,
        compiler_params=params(),
    )(place, this_half, other_half, gain)


def project_body(line, groups, came, squared, place_ref, rows_ref, weight_ref, *refs):
    refs = list(refs)
    squares_ref = refs.pop(0) if squared else None
    added = [refs.pop(0) for _ in range(came)]
    here = place_ref[line]
    at = []
    for step, half in groups:
        there = (here + step) % SIDE
        for other in (2 * half, 2 * half + 1):
            at.append((other, there) if line else (there, other))
    lhs = jnp.concatenate([rows_ref[i, j] for i, j in at], axis=0)
    columns = weight_ref.shape[1]
    size = 2 * ROWS
    product = jnp.dot(lhs, weight_ref[...], preferred_element_type=jnp.float32)
    for k, out in enumerate(refs):
        piece = product[size * k : size * (k + 1)]
        if k < came:
            piece = piece + added[k][:, :columns].astype(jnp.float32)
        out[:, :columns] = piece.astype(out.dtype)
        if squared:
            extra = jnp.concatenate([squares_ref[i, j] for i, j in at[2 * k : 2 * k + 2]], axis=0)
            if k < came:
                extra = extra + added[k][:, columns:].astype(jnp.float32)
            out[:, columns:] = extra.astype(out.dtype)


def project(line, groups, place, rows, weight, squares, dtypes, came=()):
    squared = squares is not None
    columns = weight.shape[1] + (HD if squared else 0)
    operands = [place, rows, weight] + ([squares] if squared else []) + list(came)
    return pl.pallas_call(
        functools.partial(project_body, line, groups, len(came), squared),
        out_shape=[jax.ShapeDtypeStruct((2 * ROWS, columns), dtype) for dtype in dtypes],
        in_specs=[SMEM] + [VMEM] * (len(operands) - 1),
        out_specs=[VMEM] * len(dtypes),
        compiler_params=params(),
    )(*operands)


def merge_body(line, place_ref, *refs):
    ins, (one_ref, two_ref, three_ref, home_ref, sums_ref) = refs[:6], refs[6:]
    for k in range(2):
        total = ins[k][...]
        for piece in (ins[2 + k], ins[4 + k]):
            total = total + piece[...].astype(jnp.float32)
        sums_ref[2 * k : 2 * k + 2] = total.reshape(2, ROWS, sums_ref.shape[2])
    for at, out in zip(relative(place_ref[line]), (one_ref, two_ref, three_ref, home_ref)):
        out[...] = sums_ref[at].astype(out.dtype)


def merge(line, place, own, direct, relayed):
    columns = own[0].shape[1]
    return pl.pallas_call(
        functools.partial(merge_body, line),
        out_shape=[jax.ShapeDtypeStruct((ROWS, columns), jnp.bfloat16)] * 3
        + [jax.ShapeDtypeStruct((ROWS, columns), jnp.float32)],
        in_specs=[SMEM] + [VMEM] * 6,
        out_specs=[VMEM] * 4,
        scratch_shapes=[pltpu.VMEM((SIDE, ROWS, columns), jnp.float32)],
        compiler_params=params(),
    )(place, *own, *direct, *relayed)


def along_z(x, shift):
    return lax.ppermute(
        x, "attn", [(y * SIDE + z, y * SIDE + (z + shift) % SIDE) for y in range(SIDE) for z in range(SIDE)]
    )


def along_y(x, shift):
    return lax.ppermute(
        x, "attn", [(y * SIDE + z, (y + shift) % SIDE * SIDE + z) for y in range(SIDE) for z in range(SIDE)]
    )


def along_x(x, shift):
    return lax.ppermute(
        x, "ffn", [(chip * 2 + core, (chip + shift) % SIDE * 2 + core) for chip in range(SIDE) for core in range(2)]
    )


def to_sibling(x):
    return lax.ppermute(x, "ffn", [(f, f ^ 1) for f in range(8)])


LINES = (along_y, along_z)


def scatter_far(line, place, rows, weight, squares):
    groups = ((2, 0), (2, 1))
    up, down = project(line, groups, place, rows, weight, squares, [jnp.bfloat16] * 2)
    return LINES[line](up, 1), LINES[line](down, 3)


def scatter_near(line, place, rows, weight, squares):
    groups = ((1, 1), (3, 0))
    up, down = project(line, groups, place, rows, weight, squares, [jnp.bfloat16] * 2)
    return LINES[line](down, 3), LINES[line](up, 1)


def scatter_relay(line, place, far, rows, weight, squares):
    groups = ((1, 0), (3, 1), (0, 0), (0, 1))
    dtypes = [jnp.bfloat16] * 2 + [jnp.float32] * 2
    up, down, first, second = project(line, groups, place, rows, weight, squares, dtypes, far)
    return (first, second), (LINES[line](up, 1), LINES[line](down, 3))


def scatter_cross(line, place, own, near, relayed):
    one, two, three, mine = merge(line, place, own, near, relayed)
    cross = LINES[line]
    return mine, cross(two, 2), cross(one, 1), cross(three, 3)


def on_device(
    stream,
    queries,
    k_pool,
    v_pool,
    page_table,
    lengths,
    home_device,
    w_out,
    norm_gain,
    w_gate,
    w_up,
):
    f32 = jnp.float32
    attn = lax.axis_index("attn").astype(jnp.int32)
    ffn = lax.axis_index("ffn").astype(jnp.int32)
    place = jnp.stack([attn // SIDE, attn % SIDE, ffn // 2, ffn % 2])
    mine = attn.reshape(1)
    home = home_device.reshape(1, REQS)

    outgoing = dispatch(mine, home, queries)
    arrived = lax.all_to_all(outgoing, "attn", split_axis=0, concat_axis=0, tiled=True)
    blended = attend(
        mine, home, lengths.reshape(1, REQS), page_table.T, arrived, k_pool, v_pool
    )
    returned = lax.all_to_all(blended, "attn", split_axis=0, concat_axis=0, tiled=True)
    copies = collect(mine, home, returned)
    half = REQS // 2
    out_weight, gate_weight, up_weight, stream_rows, gain = fetch(
        place, (w_out, w_gate, w_up), stream, norm_gain.reshape(1, WIDTH), copies
    )
    gathered = lax.all_to_all(copies, "attn", split_axis=0, concat_axis=0, tiled=True)
    gathered = gathered.reshape(2, half, HEADS * HD)

    came = to_sibling(half_project(True, place, gathered, out_weight))
    kept = half_project(False, place, gathered, out_weight)
    one, two, three, own = pair(place, kept, came)
    pieces = (along_x(two, 2), along_x(one, 1), along_x(three, 3))
    mine_rows = settle(stream_rows, own, pieces)
    others = (along_x(mine_rows, 3), along_x(mine_rows, 2), along_x(mine_rows, 1))
    this_half = lay(place, others + (mine_rows,)).reshape(half, WIDTH)
    other_half = to_sibling(this_half)
    residual, rows, squares = assemble(place, this_half, other_half, gain)

    gate_far = scatter_far(1, place, rows, gate_weight, squares)
    up_far = scatter_far(0, place, rows, up_weight, None)
    gate_near = scatter_near(1, place, rows, gate_weight, squares)
    up_near = scatter_near(0, place, rows, up_weight, None)
    gate_own, gate_relayed = scatter_relay(1, place, gate_far, rows, gate_weight, squares)
    up_own, up_relayed = scatter_relay(0, place, up_far, rows, up_weight, None)
    gate_parts = scatter_cross(0, place, gate_own, gate_near, gate_relayed)
    up_parts = scatter_cross(1, place, up_own, up_near, up_relayed)
    gate = sum(p.astype(f32) for p in gate_parts)
    columns = w_gate.shape[1]
    scaling = lax.rsqrt(gate[:, columns : columns + 1] / D + EPS)
    gate = gate[:, :columns] * scaling
    up = sum(p.astype(f32) for p in up_parts) * scaling
    hidden = (jax.nn.silu(gate) * up).astype(jnp.bfloat16)
    return (residual, hidden)


def solution(mesh):
    return jax.shard_map(
        on_device,
        mesh=mesh,
        in_specs=(
            P(None, "attn"),
            P("attn", "ffn"),
            P("attn", None, "ffn"),
            P("attn", None, "ffn"),
            P(),
            P(),
            P(),
            P("ffn", "attn"),
            P("attn"),
            P("attn", "ffn"),
            P("attn", "ffn"),
        ),
        out_specs=(P(None, "attn"), P("attn", "ffn")),
        check_vma=False,
    )
```

time: 210 us -> 174 us (0.83)
  blocking collectives: 42.5 us -> 31.7 us
  local copies, waits for them, and re-layouts: 17.1 us -> 7.06 us
  Pallas kernels: 52 us -> 43.2 us
  other arithmetic: 7.03 us -> 1.21 us
  matrix products: 4.51 us -> 0 us
  waiting for transfers between devices: 48.8 us -> 52.6 us
    all_to_all x3 -> x1, waiting for transfers between devices: 37.5 us -> 12.7 us  [on_device(): lax.all_to_all(copies, 'attn', split_axis=0, concat_axis=0, tiled=True)]
    ppermute x7 -> x9, waiting for transfers between devices: 3.62 us -> 18.7 us  [along_z(): lax.ppermute(x, 'attn', [(y * SIDE + z, y * SIDE + (z + shift) % SIDE) fo...]
    all_to_all x1 -> x0, blocking collectives: 11.3 us -> none  [along_x(): lax.all_to_all(x, 'ffn', split_axis=0, concat_axis=0, axis_index_groups=g...]
    ppermute x0 -> x6, starting transfers between devices: none -> 11.1 us  [along_x(): lax.ppermute(x, 'ffn', [(chip * 2 + core, (chip + shift) % SIDE * 2 + cor...]
    pallas_call x7 -> x16, Pallas kernels: 43.7 us -> 33 us  [the longest x6 11.3 us: project(): pl.pallas_call(functools.partial(project_body, line, groups, len(came), s...]
    ppermute x0 -> x6, waiting for transfers between devices: none -> 9.11 us  [along_x(): lax.ppermute(x, 'ffn', [(chip * 2 + core, (chip + shift) % SIDE * 2 + cor...]
    all_to_all x3 -> x1, starting transfers between devices: 12.6 us -> 3.73 us  [on_device(): lax.all_to_all(copies, 'attn', split_axis=0, concat_axis=0, tiled=True)]
    slice x8 -> x0, local copies, waits for them, and re-layouts: 8.03 us -> none  [the longest x4 4.22 us: scatter_finish(): direct = jnp.concatenate([down[half:], up[half:]], axis=0)]
  transfers between devices with their start and end apart: 19 -> 27, of which waited for: 9 -> 17; matrix products, arithmetic and copies ran while one was open for 5% -> 0% of each run, Pallas kernels for 16% -> 14%
where the time goes in v2:
time: 174 us; the launch traced here: 173 us
  waiting for transfers between devices  52.6 us (30%)
  Pallas kernels  43.2 us (25%)
  starting transfers between devices  36.3 us (21%)
  blocking collectives  31.7 us (18%)
  local copies, waits for them, and re-layouts  7.06 us (4%)
    ppermute x9, waiting for transfers between devices, along_z(): lax.ppermute(x, 'attn', [(y * SIDE + z, y * SIDE + (z + shift) % SIDE) fo...  18.7 us
    all_to_all x1, blocking collectives, on_device(): lax.all_to_all(outgoing, 'attn', split_axis=0, concat_axis=0, tiled=True)  16.8 us
    all_to_all x1, blocking collectives, on_device(): lax.all_to_all(blended, 'attn', split_axis=0, concat_axis=0, tiled=True)  14.9 us
    all_to_all x1, waiting for transfers between devices, on_device(): lax.all_to_all(copies, 'attn', split_axis=0, concat_axis=0, tiled=True)  12.7 us
    ppermute x9, starting transfers between devices, along_z(): lax.ppermute(x, 'attn', [(y * SIDE + z, y * SIDE + (z + shift) % SIDE) fo...  12 us
    pallas_call x6, Pallas kernels, project(): pl.pallas_call(functools.partial(project_body, line, groups, len(came), s...  11.3 us
    ppermute x6, starting transfers between devices, along_x(): lax.ppermute(x, 'ffn', [(chip * 2 + core, (chip + shift) % SIDE * 2 + cor...  11.1 us
    pallas_call x1, Pallas kernels, fetch(): pl.pallas_call(fetch_body, out_shape=[jax.ShapeDtypeStruct(shape, jnp.bfl...  10.7 us
  transfers between devices with their start and end apart: 27, of which 17 were waited for; matrix products, arithmetic and copies ran while one was open for 0% of the time, Pallas kernels for 14%

profile of v2, /device:TPU:0, one launch (start us, length us, event | category | flops | bytes accessed | tf_op | source)
XLA Modules:
  0.0 173.0 jit_solution(3669434311365935026)
XLA Ops:
  2.6 16.8 %all_to_all.15.queries_ref = bf16[64,16,128]{2,1,0:T(8,128)(2,1)} all-to-all(bf16[64,16,128]{2,1,0:T(8,128)(2,1)} %shard_map.122), channel_id=1, replica_groups=mesh['attn'=16,'ffn'=8] {'attn'}, dimensions={0} | all-to-all | bytes 524288 | tf_op jit(solution)/shard_map/all_to_all | solution.py:492
  19.4 8.3 %shard_map.123 = bf16[64,16,128]{2,1,0:T(8,128)(2,1)} custom-call(s32[1]{0:T(128)} %bitcast.4.mine_ref, s32[1,512]{1,0:T(1,128)} %bitcast.23, s32[1,512]{1,0:T(1,128)} %bitcast.26, s32[32,512]{1,0:T(8,128)} %bitcast.25, bf16[64,16,128]{2,1,0:T(8,128)(2,1)} %all_to_all.15.queries_ref, bf16[256,16,128]{2,1,0:T(8,128)(2,1)} %k_hbm.1, bf16[256,16,128]{2,1,0:T(8,128)(2,1)} %v_hbm.1), custom_call_target="tpu_custom_call" | custom-call | tf_op jit(solution)/shard_map/pallas_call | solution.py:168
  27.6 14.9 %all_to_all.16.slots_ref = bf16[64,16,128]{2,1,0:T(8,128)(2,1)S(1)} all-to-all(bf16[64,16,128]{2,1,0:T(8,128)(2,1)} %shard_map.123), channel_id=1, replica_groups=mesh['attn'=16,'ffn'=8] {'attn'}, dimensions={0} | all-to-all | bytes 524288 | tf_op jit(solution)/shard_map/all_to_all | solution.py:496
  43.2 2.2 %shard_map.124.after_hbm = bf16[16,32,2048]{2,1,0:T(8,128)(2,1)} custom-call(s32[1]{0:T(128)} %bitcast.4.mine_ref, s32[1,512]{1,0:T(1,128)S(1)} %bitcast.24, bf16[64,16,128]{2,1,0:T(8,128)(2,1)S(1)} %all_to_all.16.slots_ref), custom_call_target="tpu_custom_call" | custom-call | tf_op jit(solution)/shard_map/pallas_call | solution.py:210
  45.5 3.7 %all-to-all-start.2 = ((bf16[16,32,2048]{2,1,0:T(8,128)(2,1)}), bf16[16,32,2048]{2,1,0:T(8,128)(2,1)S(1)}, u32[]{:S(2)}, u32[]{:S(2)}) async-start(bf16[16,32,2048]{2,1,0:T(8,128)(2,1)} %shard_map.124.after_hbm), calls=%async_computation.2 | async-start | bytes 4194304 | tf_op jit(solution)/shard_map/all_to_all | solution.py:502
  51.6 10.7 %shard_map.125 = (bf16[2048,1024]{1,0:T(8,128)(2,1)S(1)}, bf16[1024,3328]{1,0:T(8,128)(2,1)}, bf16[1024,3328]{1,0:T(8,128)(2,1)}, bf16[64,1024]{1,0:T(8,128)(2,1)S(1)}, bf16[1,1024]{1,0:T(2,128)(2,1)S(1)}) custom-call(s32[4]{0:T(128)S(1)} %pad_add_fusion.place_ref, bf16[2048,1024]{1,0:T(8,128)(2,1)S(1)} %copy-done.2, bf16[1024,3328]{1,0:T(8,128)(2,1)} %gate_hbm.1, ...), custom_call_target="tpu_custom_call" | custom-call | tf_op jit(solution)/shard_map/pallas_call | solution.py:245
  64.2 12.7 %all-to-all-done.2 = bf16[16,32,2048]{2,1,0:T(8,128)(2,1)S(1)} async-done(((bf16[16,32,2048]{2,1,0:T(8,128)(2,1)}), bf16[16,32,2048]{2,1,0:T(8,128)(2,1)S(1)}, u32[]{:S(2)}, u32[]{:S(2)}) %all-to-all-start.2) | async-done | bytes 2097184 | tf_op jit(solution)/shard_map/all_to_all | solution.py:502
  83.6 3.1 %collective-permute-start.1 = (bf16[64,1024]{1,0:T(8,128)(2,1)S(1)}, bf16[64,1024]{1,0:T(8,128)(2,1)S(1)}, u32[]{:S(2)}, u32[]{:S(2)}) collective-permute-start(bf16[64,1024]{1,0:T(8,128)(2,1)S(1)} %get-tuple-element.41), channel_id=1, source_target_pairs={{0,4},{1,5},{2,6},{3,7},{4,0},{5,1},{6,2},{7,3},{8,12},{9,13},{10,... | collective-permute-start | bytes 393224 | tf_op jit(solution)/shard_map/ppermute | solution.py:434
  87.3 2.6 %collective-permute-start.3 = (bf16[64,1024]{1,0:T(8,128)(2,1)S(1)}, bf16[64,1024]{1,0:T(8,128)(2,1)S(1)}, u32[]{:S(2)}, u32[]{:S(2)}) collective-permute-start(bf16[64,1024]{1,0:T(8,128)(2,1)S(1)} %get-tuple-element.43), channel_id=1, source_target_pairs={{0,6},{1,7},{2,0},{3,1},{4,2},{5,3},{6,4},{7,5},{8,14},{9,15},{10,... | collective-permute-start | bytes 393224 | tf_op jit(solution)/shard_map/ppermute | solution.py:434
  91.5 2.4 %collective-permute-done.2.b_ref = bf16[64,1024]{1,0:T(8,128)(2,1)S(1)} collective-permute-done((bf16[64,1024]{1,0:T(8,128)(2,1)S(1)}, bf16[64,1024]{1,0:T(8,128)(2,1)S(1)}, u32[]{:S(2)}, u32[]{:S(2)}) %collective-permute-start.2) | collective-permute-done | bytes 131104 | tf_op jit(solution)/shard_map/ppermute | solution.py:434
  95.5 2.8 %collective-permute-start.5 = (bf16[64,1024]{1,0:T(8,128)(2,1)S(1)}, bf16[64,1024]{1,0:T(8,128)(2,1)S(1)}, u32[]{:S(2)}, u32[]{:S(2)}) collective-permute-start(bf16[64,1024]{1,0:T(8,128)(2,1)S(1)} %shard_map.129.own_ref), channel_id=1, source_target_pairs={{0,4},{1,5},{2,6},{3,7},{4,0},{5,1},{6,2},{7,3},{8,12},{9,13},{10,... | collective-permute-start | bytes 393224 | tf_op jit(solution)/shard_map/ppermute | solution.py:434
  98.8 2.7 %collective-permute-done.6.three_ref = bf16[64,1024]{1,0:T(8,128)(2,1)S(1)} collective-permute-done((bf16[64,1024]{1,0:T(8,128)(2,1)S(1)}, bf16[64,1024]{1,0:T(8,128)(2,1)S(1)}, u32[]{:S(2)}, u32[]{:S(2)}) %collective-permute-start.6) | collective-permute-done | bytes 131104 | tf_op jit(solution)/shard_map/ppermute | solution.py:434
  101.4 2.4 %collective-permute-done.5.two_ref = bf16[64,1024]{1,0:T(8,128)(2,1)S(1)} collective-permute-done((bf16[64,1024]{1,0:T(8,128)(2,1)S(1)}, bf16[64,1024]{1,0:T(8,128)(2,1)S(1)}, u32[]{:S(2)}, u32[]{:S(2)}) %collective-permute-start.5) | collective-permute-done | bytes 131104 | tf_op jit(solution)/shard_map/ppermute | solution.py:434
  110.6 2.7 %collective-permute-start.9 = (bf16[64,3456]{1,0:T(8,128)(2,1)S(1)}, bf16[64,3456]{1,0:T(8,128)(2,1)S(1)}, u32[]{:S(2)}, u32[]{:S(2)}) collective-permute-start(bf16[64,3456]{1,0:T(8,128)(2,1)S(1)} %get-tuple-element.50), channel_id=1, source_target_pairs={{0,24},{8,0},{16,8},{24,16},{32,56},{40,32},{48,40},{56,48},{64,88... | collective-permute-start | bytes 1327112 | tf_op jit(solution)/shard_map/ppermute | solution.py:422
  116.7 3.3 %collective-permute-start.18 = (bf16[64,3328]{1,0:T(8,128)(2,1)S(1)}, bf16[64,3328]{1,0:T(8,128)(2,1)S(1)}, u32[]{:S(2)}, u32[]{:S(2)}) collective-permute-start(bf16[64,3328]{1,0:T(8,128)(2,1)S(1)} %get-tuple-element.63), channel_id=1, source_target_pairs={{0,96},{8,104},{16,112},{24,120},{32,0},{40,8},{48,16},{56,24},{64... | collective-permute-start | bytes 1277960 | tf_op jit(solution)/shard_map/ppermute | solution.py:428
  120.0 3.5 %collective-permute-done.8.refs_1_ = bf16[64,3456]{1,0:T(8,128)(2,1)S(1)} collective-permute-done((bf16[64,3456]{1,0:T(8,128)(2,1)S(1)}, bf16[64,3456]{1,0:T(8,128)(2,1)S(1)}, u32[]{:S(2)}, u32[]{:S(2)}) %collective-permute-start.8) | collective-permute-done | bytes 442400 | tf_op jit(solution)/shard_map/ppermute | solution.py:422
  123.9 2.5 %shard_map.133 = (bf16[64,3456]{1,0:T(8,128)(2,1)S(1)}, bf16[64,3456]{1,0:T(8,128)(2,1)S(1)}, f32[64,3456]{1,0:T(8,128)S(1)}, f32[64,3456]{1,0:T(8,128)S(1)}) custom-call(s32[4]{0:T(128)S(1)} %pad_add_fusion.place_ref, bf16[4,4,32,1024]{3,2,1,0:T(8,128)(2,1)S(1)} %get-tuple-element.46.rows_ref, bf16[1024,3328]{1,0:T(8,128)(2,1)S(1)} %bitcast.15, ...), custom_call_target="tpu_custom_call" | custom-call | tf_op jit(solution)/shard_map/pallas_call | solution.py:388
  127.5 2.7 %collective-permute-start.13 = (bf16[64,3456]{1,0:T(8,128)(2,1)S(1)}, bf16[64,3456]{1,0:T(8,128)(2,1)S(1)}, u32[]{:S(2)}, u32[]{:S(2)}) collective-permute-start(bf16[64,3456]{1,0:T(8,128)(2,1)S(1)} %get-tuple-element.56), channel_id=1, source_target_pairs={{0,24},{8,0},{16,8},{24,16},{32,56},{40,32},{48,40},{56,48},{64,88... | collective-permute-start | bytes 1327112 | tf_op jit(solution)/shard_map/ppermute | solution.py:422
  133.9 2.5 %shard_map.137 = (bf16[64,3328]{1,0:T(8,128)(2,1)S(1)}, bf16[64,3328]{1,0:T(8,128)(2,1)S(1)}, f32[64,3328]{1,0:T(8,128)S(1)}, f32[64,3328]{1,0:T(8,128)S(1)}) custom-call(s32[4]{0:T(128)S(1)} %pad_add_fusion.place_ref, bf16[4,4,32,1024]{3,2,1,0:T(8,128)(2,1)S(1)} %get-tuple-element.46.rows_ref, bf16[1024,3328]{1,0:T(8,128)(2,1)S(1)} %bitcast.13, ...), custom_call_target="tpu_custom_call" | custom-call | tf_op jit(solution)/shard_map/pallas_call | solution.py:388
  137.8 7.8 %collective-permute-done.12.refs_4_ = bf16[64,3456]{1,0:T(8,128)(2,1)S(1)} collective-permute-done((bf16[64,3456]{1,0:T(8,128)(2,1)S(1)}, bf16[64,3456]{1,0:T(8,128)(2,1)S(1)}, u32[]{:S(2)}, u32[]{:S(2)}) %collective-permute-start.12) | collective-permute-done | bytes 442400 | tf_op jit(solution)/shard_map/ppermute | solution.py:422
  148.8 2.7 %collective-permute-start.16 = (bf16[32,3456]{1,0:T(8,128)(2,1)S(1)}, bf16[32,3456]{1,0:T(8,128)(2,1)S(1)}, u32[]{:S(2)}, u32[]{:S(2)}) collective-permute-start(bf16[32,3456]{1,0:T(8,128)(2,1)S(1)} %get-tuple-element.60), channel_id=1, source_target_pairs={{0,96},{8,104},{16,112},{24,120},{32,0},{40,8},{48,16},{56,24},{64... | collective-permute-start | bytes 663560 | tf_op jit(solution)/shard_map/ppermute | solution.py:428
  151.5 8.9 %collective-permute-done.21.refs_4_ = bf16[64,3328]{1,0:T(8,128)(2,1)S(1)} collective-permute-done((bf16[64,3328]{1,0:T(8,128)(2,1)S(1)}, bf16[64,3328]{1,0:T(8,128)(2,1)S(1)}, u32[]{:S(2)}, u32[]{:S(2)}) %collective-permute-start.21) | collective-permute-done | bytes 426016 | tf_op jit(solution)/shard_map/ppermute | solution.py:428
  161.4 2.6 %collective-permute-start.23 = (bf16[32,3328]{1,0:T(8,128)(2,1)S(1)}, bf16[32,3328]{1,0:T(8,128)(2,1)S(1)}, u32[]{:S(2)}, u32[]{:S(2)}) collective-permute-start(bf16[32,3328]{1,0:T(8,128)(2,1)S(1)} %get-tuple-element.71), channel_id=1, source_target_pairs={{0,16},{8,24},{16,0},{24,8},{32,48},{40,56},{48,32},{56,40},{64,80... | collective-permute-start | bytes 638984 | tf_op jit(solution)/shard_map/ppermute | solution.py:422
  168.8 2.3 %collective-permute-done.24 = bf16[32,3328]{1,0:T(8,128)(2,1)S(1)} collective-permute-done((bf16[32,3328]{1,0:T(8,128)(2,1)S(1)}, bf16[32,3328]{1,0:T(8,128)(2,1)S(1)}, u32[]{:S(2)}, u32[]{:S(2)}) %collective-permute-start.24) | collective-permute-done | bytes 213024 | tf_op jit(solution)/shard_map/ppermute | solution.py:422
  (77 shorter events, 45.4 us)
Async XLA Ops:
  45.5 31.5 %all-to-all-start.2 = ((bf16[16,32,2048]{2,1,0:T(8,128)(2,1)}), bf16[16,32,2048]{2,1,0:T(8,128)(2,1)S(1)}, u32[]{:S(2)}, u32[]{:S(2)}) async-start(bf16[16,32,2048]{2,1,0:T(8,128)(2,1)} %shard_map.124.after_hbm), calls=%async_computation.2 | async-start | bytes 4194304 | tf_op jit(solution)/shard_map/all_to_all | solution.py:502
  83.6 7.9 %collective-permute-start.1 = (bf16[64,1024]{1,0:T(8,128)(2,1)S(1)}, bf16[64,1024]{1,0:T(8,128)(2,1)S(1)}, u32[]{:S(2)}, u32[]{:S(2)}) collective-permute-start(bf16[64,1024]{1,0:T(8,128)(2,1)S(1)} %get-tuple-element.41), channel_id=1, source_target_pairs={{0,4},{1,5},{2,6},{3,7},{4,0},{5,1},{6,2},{7,3},{8,12},{9,13},{10,... | collective-permute-start | bytes 393224 | tf_op jit(solution)/shard_map/ppermute | solution.py:434
  86.7 7.2 %collective-permute-start.2 = (bf16[64,1024]{1,0:T(8,128)(2,1)S(1)}, bf16[64,1024]{1,0:T(8,128)(2,1)S(1)}, u32[]{:S(2)}, u32[]{:S(2)}) collective-permute-start(bf16[64,1024]{1,0:T(8,128)(2,1)S(1)} %get-tuple-element.42), channel_id=1, source_target_pairs={{0,2},{1,3},{2,4},{3,5},{4,6},{5,7},{6,0},{7,1},{8,10},{9,11},{10,... | collective-permute-start | bytes 393224 | tf_op jit(solution)/shard_map/ppermute | solution.py:434
  87.3 6.6 %collective-permute-start.3 = (bf16[64,1024]{1,0:T(8,128)(2,1)S(1)}, bf16[64,1024]{1,0:T(8,128)(2,1)S(1)}, u32[]{:S(2)}, u32[]{:S(2)}) collective-permute-start(bf16[64,1024]{1,0:T(8,128)(2,1)S(1)} %get-tuple-element.43), channel_id=1, source_target_pairs={{0,6},{1,7},{2,0},{3,1},{4,2},{5,3},{6,4},{7,5},{8,14},{9,15},{10,... | collective-permute-start | bytes 393224 | tf_op jit(solution)/shard_map/ppermute | solution.py:434
  94.0 7.4 %collective-permute-start.6 = (bf16[64,1024]{1,0:T(8,128)(2,1)S(1)}, bf16[64,1024]{1,0:T(8,128)(2,1)S(1)}, u32[]{:S(2)}, u32[]{:S(2)}) collective-permute-start(bf16[64,1024]{1,0:T(8,128)(2,1)S(1)} %shard_map.129.own_ref), channel_id=1, source_target_pairs={{0,2},{1,3},{2,4},{3,5},{4,6},{5,7},{6,0},{7,1},{8,10},{9,11},{10,... | collective-permute-start | bytes 393224 | tf_op jit(solution)/shard_map/ppermute | solution.py:434
  95.5 8.3 %collective-permute-start.5 = (bf16[64,1024]{1,0:T(8,128)(2,1)S(1)}, bf16[64,1024]{1,0:T(8,128)(2,1)S(1)}, u32[]{:S(2)}, u32[]{:S(2)}) collective-permute-start(bf16[64,1024]{1,0:T(8,128)(2,1)S(1)} %shard_map.129.own_ref), channel_id=1, source_target_pairs={{0,4},{1,5},{2,6},{3,7},{4,0},{5,1},{6,2},{7,3},{8,12},{9,13},{10,... | collective-permute-start | bytes 393224 | tf_op jit(solution)/shard_map/ppermute | solution.py:434
  110.0 13.5 %collective-permute-start.8 = (bf16[64,3456]{1,0:T(8,128)(2,1)S(1)}, bf16[64,3456]{1,0:T(8,128)(2,1)S(1)}, u32[]{:S(2)}, u32[]{:S(2)}) collective-permute-start(bf16[64,3456]{1,0:T(8,128)(2,1)S(1)} %get-tuple-element.49), channel_id=1, source_target_pairs={{0,8},{8,16},{16,24},{24,0},{32,40},{40,48},{48,56},{56,32},{64,72... | collective-permute-start | bytes 1327112 | tf_op jit(solution)/shard_map/ppermute | solution.py:422
  110.6 13.2 %collective-permute-start.9 = (bf16[64,3456]{1,0:T(8,128)(2,1)S(1)}, bf16[64,3456]{1,0:T(8,128)(2,1)S(1)}, u32[]{:S(2)}, u32[]{:S(2)}) collective-permute-start(bf16[64,3456]{1,0:T(8,128)(2,1)S(1)} %get-tuple-element.50), channel_id=1, source_target_pairs={{0,24},{8,0},{16,8},{24,16},{32,56},{40,32},{48,40},{56,48},{64,88... | collective-permute-start | bytes 1327112 | tf_op jit(solution)/shard_map/ppermute | solution.py:422
  114.9 12.6 %collective-permute-start.17 = (bf16[64,3328]{1,0:T(8,128)(2,1)S(1)}, bf16[64,3328]{1,0:T(8,128)(2,1)S(1)}, u32[]{:S(2)}, u32[]{:S(2)}) collective-permute-start(bf16[64,3328]{1,0:T(8,128)(2,1)S(1)} %get-tuple-element.62), channel_id=1, source_target_pairs={{0,32},{8,40},{16,48},{24,56},{32,64},{40,72},{48,80},{56,88},{64,... | collective-permute-start | bytes 1277960 | tf_op jit(solution)/shard_map/ppermute | solution.py:428
  116.6 16.7 %collective-permute-start.10 = (bf16[64,3456]{1,0:T(8,128)(2,1)S(1)}, bf16[64,3456]{1,0:T(8,128)(2,1)S(1)}, u32[]{:S(2)}, u32[]{:S(2)}) collective-permute-start(bf16[64,3456]{1,0:T(8,128)(2,1)S(1)} %get-tuple-element.53), channel_id=1, source_target_pairs={{0,24},{8,0},{16,8},{24,16},{32,56},{40,32},{48,40},{56,48},{64,88... | collective-permute-start | bytes 1327112 | tf_op jit(solution)/shard_map/ppermute | solution.py:422
  116.7 15.1 %collective-permute-start.18 = (bf16[64,3328]{1,0:T(8,128)(2,1)S(1)}, bf16[64,3328]{1,0:T(8,128)(2,1)S(1)}, u32[]{:S(2)}, u32[]{:S(2)}) collective-permute-start(bf16[64,3328]{1,0:T(8,128)(2,1)S(1)} %get-tuple-element.63), channel_id=1, source_target_pairs={{0,96},{8,104},{16,112},{24,120},{32,0},{40,8},{48,16},{56,24},{64... | collective-permute-start | bytes 1277960 | tf_op jit(solution)/shard_map/ppermute | solution.py:428
  123.5 14.3 %collective-permute-start.11 = (bf16[64,3456]{1,0:T(8,128)(2,1)S(1)}, bf16[64,3456]{1,0:T(8,128)(2,1)S(1)}, u32[]{:S(2)}, u32[]{:S(2)}) collective-permute-start(bf16[64,3456]{1,0:T(8,128)(2,1)S(1)} %get-tuple-element.54), channel_id=1, source_target_pairs={{0,8},{8,16},{16,24},{24,0},{32,40},{40,48},{48,56},{56,32},{64,72... | collective-permute-start | bytes 1327112 | tf_op jit(solution)/shard_map/ppermute | solution.py:422
  126.3 19.2 %collective-permute-start.12 = (bf16[64,3456]{1,0:T(8,128)(2,1)S(1)}, bf16[64,3456]{1,0:T(8,128)(2,1)S(1)}, u32[]{:S(2)}, u32[]{:S(2)}) collective-permute-start(bf16[64,3456]{1,0:T(8,128)(2,1)S(1)} %get-tuple-element.55), channel_id=1, source_target_pairs={{0,8},{8,16},{16,24},{24,0},{32,40},{40,48},{48,56},{56,32},{64,72... | collective-permute-start | bytes 1327112 | tf_op jit(solution)/shard_map/ppermute | solution.py:422
  127.5 18.5 %collective-permute-start.13 = (bf16[64,3456]{1,0:T(8,128)(2,1)S(1)}, bf16[64,3456]{1,0:T(8,128)(2,1)S(1)}, u32[]{:S(2)}, u32[]{:S(2)}) collective-permute-start(bf16[64,3456]{1,0:T(8,128)(2,1)S(1)} %get-tuple-element.56), channel_id=1, source_target_pairs={{0,24},{8,0},{16,8},{24,16},{32,56},{40,32},{48,40},{56,48},{64,88... | collective-permute-start | bytes 1327112 | tf_op jit(solution)/shard_map/ppermute | solution.py:422
  131.8 16.0 %collective-permute-start.19 = (bf16[64,3328]{1,0:T(8,128)(2,1)S(1)}, bf16[64,3328]{1,0:T(8,128)(2,1)S(1)}, u32[]{:S(2)}, u32[]{:S(2)}) collective-permute-start(bf16[64,3328]{1,0:T(8,128)(2,1)S(1)} %get-tuple-element.66), channel_id=1, source_target_pairs={{0,96},{8,104},{16,112},{24,120},{32,0},{40,8},{48,16},{56,24},{64... | collective-permute-start | bytes 1277960 | tf_op jit(solution)/shard_map/ppermute | solution.py:428
  133.3 15.5 %collective-permute-start.20 = (bf16[64,3328]{1,0:T(8,128)(2,1)S(1)}, bf16[64,3328]{1,0:T(8,128)(2,1)S(1)}, u32[]{:S(2)}, u32[]{:S(2)}) collective-permute-start(bf16[64,3328]{1,0:T(8,128)(2,1)S(1)} %get-tuple-element.67), channel_id=1, source_target_pairs={{0,32},{8,40},{16,48},{24,56},{32,64},{40,72},{48,80},{56,88},{64,... | collective-permute-start | bytes 1277960 | tf_op jit(solution)/shard_map/ppermute | solution.py:428
  137.8 22.6 %collective-permute-start.21 = (bf16[64,3328]{1,0:T(8,128)(2,1)S(1)}, bf16[64,3328]{1,0:T(8,128)(2,1)S(1)}, u32[]{:S(2)}, u32[]{:S(2)}) collective-permute-start(bf16[64,3328]{1,0:T(8,128)(2,1)S(1)} %get-tuple-element.68), channel_id=1, source_target_pairs={{0,32},{8,40},{16,48},{24,56},{32,64},{40,72},{48,80},{56,88},{64,... | collective-permute-start | bytes 1277960 | tf_op jit(solution)/shard_map/ppermute | solution.py:428
  145.5 14.8 %collective-permute-start.22 = (bf16[64,3328]{1,0:T(8,128)(2,1)S(1)}, bf16[64,3328]{1,0:T(8,128)(2,1)S(1)}, u32[]{:S(2)}, u32[]{:S(2)}) collective-permute-start(bf16[64,3328]{1,0:T(8,128)(2,1)S(1)} %get-tuple-element.69), channel_id=1, source_target_pairs={{0,96},{8,104},{16,112},{24,120},{32,0},{40,8},{48,16},{56,24},{64... | collective-permute-start | bytes 1277960 | tf_op jit(solution)/shard_map/ppermute | solution.py:428
  147.0 19.0 %collective-permute-start.14 = (bf16[32,3456]{1,0:T(8,128)(2,1)S(1)}, bf16[32,3456]{1,0:T(8,128)(2,1)S(1)}, u32[]{:S(2)}, u32[]{:S(2)}) collective-permute-start(bf16[32,3456]{1,0:T(8,128)(2,1)S(1)} %get-tuple-element.58), channel_id=1, source_target_pairs={{0,64},{8,72},{16,80},{24,88},{32,96},{40,104},{48,112},{56,120},{... | collective-permute-start | bytes 663560 | tf_op jit(solution)/shard_map/ppermute | solution.py:428
  147.8 19.4 %collective-permute-start.15 = (bf16[32,3456]{1,0:T(8,128)(2,1)S(1)}, bf16[32,3456]{1,0:T(8,128)(2,1)S(1)}, u32[]{:S(2)}, u32[]{:S(2)}) collective-permute-start(bf16[32,3456]{1,0:T(8,128)(2,1)S(1)} %get-tuple-element.59), channel_id=1, source_target_pairs={{0,32},{8,40},{16,48},{24,56},{32,64},{40,72},{48,80},{56,88},{64,... | collective-permute-start | bytes 663560 | tf_op jit(solution)/shard_map/ppermute | solution.py:428
  148.8 18.4 %collective-permute-start.16 = (bf16[32,3456]{1,0:T(8,128)(2,1)S(1)}, bf16[32,3456]{1,0:T(8,128)(2,1)S(1)}, u32[]{:S(2)}, u32[]{:S(2)}) collective-permute-start(bf16[32,3456]{1,0:T(8,128)(2,1)S(1)} %get-tuple-element.60), channel_id=1, source_target_pairs={{0,96},{8,104},{16,112},{24,120},{32,0},{40,8},{48,16},{56,24},{64... | collective-permute-start | bytes 663560 | tf_op jit(solution)/shard_map/ppermute | solution.py:428
  161.4 7.4 %collective-permute-start.23 = (bf16[32,3328]{1,0:T(8,128)(2,1)S(1)}, bf16[32,3328]{1,0:T(8,128)(2,1)S(1)}, u32[]{:S(2)}, u32[]{:S(2)}) collective-permute-start(bf16[32,3328]{1,0:T(8,128)(2,1)S(1)} %get-tuple-element.71), channel_id=1, source_target_pairs={{0,16},{8,24},{16,0},{24,8},{32,48},{40,56},{48,32},{56,40},{64,80... | collective-permute-start | bytes 638984 | tf_op jit(solution)/shard_map/ppermute | solution.py:422
  164.0 7.1 %collective-permute-start.24 = (bf16[32,3328]{1,0:T(8,128)(2,1)S(1)}, bf16[32,3328]{1,0:T(8,128)(2,1)S(1)}, u32[]{:S(2)}, u32[]{:S(2)}) collective-permute-start(bf16[32,3328]{1,0:T(8,128)(2,1)S(1)} %get-tuple-element.72), channel_id=1, source_target_pairs={{0,8},{8,16},{16,24},{24,0},{32,40},{40,48},{48,56},{56,32},{64,72... | collective-permute-start | bytes 638984 | tf_op jit(solution)/shard_map/ppermute | solution.py:422
  166.0 6.1 %collective-permute-start.25 = (bf16[32,3328]{1,0:T(8,128)(2,1)S(1)}, bf16[32,3328]{1,0:T(8,128)(2,1)S(1)}, u32[]{:S(2)}, u32[]{:S(2)}) collective-permute-start(bf16[32,3328]{1,0:T(8,128)(2,1)S(1)} %get-tuple-element.73), channel_id=1, source_target_pairs={{0,24},{8,0},{16,8},{24,16},{32,56},{40,32},{48,40},{56,48},{64,88... | collective-permute-start | bytes 638984 | tf_op jit(solution)/shard_map/ppermute | solution.py:422
  (13 other events, 222.2 us)

commit v3 on v2

v3 whole, which is shorter than its diff:
```python
import functools
import jax
import jax.numpy as jnp
from jax import lax
from jax.experimental import pallas as pl
from jax.experimental.pallas import tpu as pltpu
from jax.sharding import PartitionSpec as P

D = 16384
HD = 128
HEADS = 16
PAGE = 16
MAXP = 32
CTX = PAGE * MAXP
REQS = 512
N_ATTN = 16
ROWS = 32
CAP = 4
SLOTS = N_ATTN * CAP
SIDE = 4
WIDTH = 1024
GROUP = 8
LISTED = 128
SHORT = MAXP // 2
EPS = 1e-05

SMEM = pl.BlockSpec(memory_space=pltpu.SMEM)
VMEM = pl.BlockSpec(memory_space=pltpu.VMEM)
HBM = pl.BlockSpec(memory_space=pltpu.HBM)


WIDE = 58


def params(mebibytes=16):
    return pltpu.CompilerParams(vmem_limit_bytes=mebibytes * 1024 * 1024)


def place():
    attn, ffn = lax.axis_index("attn"), lax.axis_index("ffn")
    return attn // SIDE, attn % SIDE, ffn // 2, ffn % 2


def start_all(copies):
    for copy in copies:
        copy.start()
    return copies


def dispatch_body(home_hbm, queries_hbm, out_ref, dest_ref, queries_ref, tall_ref, home_ref, count_ref, sems):
    pairs = ((home_hbm, home_ref), (queries_hbm, queries_ref))
    copies = start_all([pltpu.make_async_copy(a, b, sems.at[k]) for k, (a, b) in enumerate(pairs)])
    out_ref[...] = jnp.zeros_like(out_ref)
    for target in range(N_ATTN):
        count_ref[target] = 0
    base = (lax.axis_index("attn")) * ROWS
    copies[0].wait()
    dests = []
    for row in range(ROWS):
        target = home_ref[0, base + row]
        rank = count_ref[target]
        count_ref[target] = rank + 1
        dests.append(target * CAP + rank)
        dest_ref[row] = dests[row]
    copies[1].wait()
    for head in range(HEADS):
        tall_ref[pl.ds(head, ROWS, stride=HEADS), :] = queries_ref[
            :, head * HD : (head + 1) * HD
        ].astype(jnp.float32)
    for row in range(ROWS):
        out_ref[dests[row]] = tall_ref[row * HEADS : (row + 1) * HEADS].astype(jnp.bfloat16)


def dispatch(home, queries):
    return pl.pallas_call(
        dispatch_body,
        out_shape=[
            jax.ShapeDtypeStruct((SLOTS, HEADS, HD), jnp.bfloat16),
            jax.ShapeDtypeStruct((ROWS,), jnp.int32),
        ],
        in_specs=[HBM, HBM],
        out_specs=[VMEM, SMEM],
        scratch_shapes=[
            pltpu.VMEM((ROWS, HEADS * HD), jnp.bfloat16),
            pltpu.VMEM((ROWS * HEADS, HD), jnp.float32),
            pltpu.SMEM((1, REQS), jnp.int32),
            pltpu.SMEM((N_ATTN,), jnp.int32),
            pltpu.SemaphoreType.DMA((2,)),
        ],
        compiler_params=params(WIDE),
    )(home, queries)


def prepare_body(home_hbm, *refs):
    sources, list_ref, targets = refs[:4], refs[4], refs[5:9]
    home_ref, lengths_ref, found_ref, sems = refs[9:]
    pairs = [(home_hbm, home_ref), (sources[0], lengths_ref)] + list(zip(sources, targets))
    copies = start_all([pltpu.make_async_copy(a, b, sems.at[k]) for k, (a, b) in enumerate(pairs)])
    mine = lax.axis_index("attn")
    copies[0].wait()

    def scan_source(source, found):
        for row in range(ROWS):
            request = source * ROWS + row
            found_ref[found] = request
            found = found + jnp.where(home_ref[0, request] == mine, 1, 0)
        return found

    total = lax.fori_loop(0, N_ATTN, scan_source, jnp.int32(0))
    copies[1].wait()

    def sort_entry(index, state):
        short, long, before, rank = state
        request = found_ref[index]
        source = request // ROWS
        rank = jnp.where(source == before, rank + 1, 0)
        entry = request * SLOTS + source * CAP + rank
        list_ref[0, short] = entry
        list_ref[1, long] = entry
        is_long = jnp.where(lengths_ref[0, request] > SHORT * PAGE, 1, 0)
        return short + 1 - is_long, long + is_long, source, rank

    zero = jnp.int32(0)
    counts = lax.fori_loop(0, total, sort_entry, (zero, zero, zero - 1, zero))[:2]
    for kind in range(2):
        last = list_ref[kind, jnp.maximum(counts[kind] - 1, 0)]
        for extra in range(GROUP):
            list_ref[kind, counts[kind] + extra] = last
        list_ref[kind, LISTED - 1] = counts[kind]
    for copy in copies[2:]:
        copy.wait()


def prepare(home, *arrays):
    return pl.pallas_call(
        prepare_body,
        out_shape=[jax.ShapeDtypeStruct((2, LISTED), jnp.int32)]
        + [jax.ShapeDtypeStruct(a.shape, a.dtype) for a in arrays],
        in_specs=[HBM] * 5,
        out_specs=[SMEM] + [VMEM] * 4,
        scratch_shapes=[
            pltpu.SMEM(home.shape, jnp.int32),
            pltpu.SMEM(arrays[0].shape, jnp.int32),
            pltpu.SMEM((LISTED,), jnp.int32),
            pltpu.SemaphoreType.DMA((6,)),
        ],
        compiler_params=params(),
    )(home, *arrays)


def attend_body(lengths_vmem, table_vmem, list_ref, queries_ref, k_ref, v_ref, out_ref, lengths_ref, table_ref, sems):
    pairs = ((lengths_vmem, lengths_ref), (table_vmem, table_ref))
    copies = start_all([pltpu.make_async_copy(a, b, sems.at[k]) for k, (a, b) in enumerate(pairs)])
    out_ref[...] = jnp.zeros_like(out_ref)
    for copy in copies:
        copy.wait()

    def step(kind, count, index, carry):
        positions = lax.broadcasted_iota(jnp.int32, (HEADS, count * PAGE), 1)
        chosen = []
        for member in range(GROUP):
            entry = list_ref[kind, index * GROUP + member]
            request, slot = entry // SLOTS, entry % SLOTS
            pages = [table_ref[page, request] for page in range(count)]
            chosen.append((request, slot, pages))
        scores = []
        for request, slot, pages in chosen:
            keys = jnp.concatenate([k_ref[page] for page in pages], axis=0)
            scores.append(
                lax.dot_general(
                    queries_ref[slot],
                    keys,
                    (((1,), (1,)), ((), ())),
                    preferred_element_type=jnp.float32,
                )
                * HD ** (-0.5)
            )
        outputs = []
        for (request, slot, pages), score in zip(chosen, scores):
            visible = positions < lengths_ref[0, request]
            maxima = jnp.max(jnp.where(visible, score, -jnp.inf), axis=1, keepdims=True)
            weights = jnp.where(visible, jnp.exp(score - maxima), 0.0)
            totals = jnp.sum(weights, axis=1, keepdims=True)
            outputs.append((weights.astype(jnp.bfloat16), totals))
        for (request, slot, pages), (weights, totals) in zip(chosen, outputs):
            values = jnp.concatenate([v_ref[page] for page in pages], axis=0)
            blended = jnp.dot(weights, values, preferred_element_type=jnp.float32)
            out_ref[slot] = (blended / totals).astype(jnp.bfloat16)
        return carry

    for kind, count in ((0, SHORT), (1, MAXP)):
        groups = (list_ref[kind, LISTED - 1] + GROUP - 1) // GROUP
        lax.fori_loop(0, groups, functools.partial(step, kind, count), 0)


def attend(listed, queries, lengths, table, k_pool, v_pool):
    return pl.pallas_call(
        attend_body,
        out_shape=jax.ShapeDtypeStruct((SLOTS, HEADS, HD), jnp.bfloat16),
        in_specs=[VMEM, VMEM, SMEM] + [VMEM] * 3,
        out_specs=VMEM,
        scratch_shapes=[
            pltpu.SMEM(lengths.shape, jnp.int32),
            pltpu.SMEM(table.shape, jnp.int32),
            pltpu.SemaphoreType.DMA((2,)),
        ],
        compiler_params=params(),
    )(lengths, table, listed, queries, k_pool, v_pool)


def collect_body(dest_ref, slots_ref, left_ref, right_ref, wide_ref):
    for row in range(ROWS):
        heads = slots_ref[dest_ref[row]].astype(jnp.float32)
        for head in range(HEADS):
            wide_ref[row : row + 1, head * HD : (head + 1) * HD] = heads[head : head + 1]
    left_ref[...] = wide_ref[:, :WIDTH].astype(jnp.bfloat16)
    right_ref[...] = wide_ref[:, WIDTH:].astype(jnp.bfloat16)


def collect(dest, slots):
    return pl.pallas_call(
        collect_body,
        out_shape=[jax.ShapeDtypeStruct((ROWS, WIDTH), jnp.bfloat16)] * 2,
        in_specs=[SMEM, VMEM],
        out_specs=[VMEM] * 2,
        scratch_shapes=[pltpu.VMEM((ROWS, HEADS * HD), jnp.float32)],
        compiler_params=params(),
    )(dest, slots)


def gather_line_body(*refs):
    for line, ins, out in ((1, refs[:4], refs[8]), (0, refs[4:8], refs[9])):
        for at, block in zip(relative(place()[line]), ins):
            out[at] = block[...]


def gather_line(left, right):
    return pl.pallas_call(
        gather_line_body,
        out_shape=[jax.ShapeDtypeStruct((SIDE, ROWS, WIDTH), jnp.bfloat16)] * 2,
        in_specs=[VMEM] * 8,
        out_specs=[VMEM] * 2,
        compiler_params=params(),
    )(*left, *right)


def gather_all_body(*refs):
    out = refs[8]
    for at, block in zip(relative(place()[0]), refs[:4]):
        out[pl.ds(at * SIDE, SIDE), :, :WIDTH] = block[...]
    for at, block in zip(relative(place()[1]), refs[4:8]):
        for y in range(SIDE):
            out[y * SIDE + at, :, WIDTH:] = block[y]


def gather_all(left, right):
    return pl.pallas_call(
        gather_all_body,
        out_shape=jax.ShapeDtypeStruct((N_ATTN, ROWS, HEADS * HD), jnp.bfloat16),
        in_specs=[VMEM] * 8,
        out_specs=VMEM,
        compiler_params=params(),
    )(*left, *right)


def own_stream_body(stream_hbm, after_hbm, out_ref, sem):
    part = out_ref.shape[0]
    first = pl.multiple_of(place()[3] * (SIDE * part) + place()[2] * part, part)
    pltpu.async_copy(stream_hbm.at[pl.ds(first, part)], out_ref, sem).wait()


def own_stream(stream, after):
    return pl.pallas_call(
        own_stream_body,
        out_shape=jax.ShapeDtypeStruct((REQS // 8, WIDTH), stream.dtype),
        in_specs=[HBM] * 2,
        out_specs=VMEM,
        scratch_shapes=[pltpu.SemaphoreType.DMA],
        compiler_params=params(),
    )(stream, after)


def half_body(sibling, rows_ref, weight_ref, out_ref):
    core = place()[3]
    which = 1 - core if sibling else core
    out_ref[...] = jnp.dot(
        rows_ref[which], weight_ref[...], preferred_element_type=jnp.float32
    ).astype(jnp.bfloat16)


def half_project(sibling, rows, weight):
    return pl.pallas_call(
        functools.partial(half_body, sibling),
        out_shape=jax.ShapeDtypeStruct((rows.shape[1], weight.shape[1]), jnp.bfloat16),
        in_specs=[VMEM, VMEM],
        out_specs=VMEM,
        compiler_params=params(),
    )(rows, weight)


def relative(at):
    return [(at + 1) % SIDE, (at + 2) % SIDE, (at + 3) % SIDE, at]


def pair_body(kept_ref, came_ref, one_ref, two_ref, three_ref, own_ref):
    for at, out in zip(relative(place()[2]), (one_ref, two_ref, three_ref, own_ref)):
        out[...] = (kept_ref[at].astype(jnp.float32) + came_ref[at].astype(jnp.float32)).astype(out.dtype)


def pair(kept, came):
    part = kept.shape[0] // SIDE
    shape = (part, WIDTH)
    return pl.pallas_call(
        pair_body,
        out_shape=[jax.ShapeDtypeStruct(shape, jnp.bfloat16)] * 3
        + [jax.ShapeDtypeStruct(shape, jnp.float32)],
        in_specs=[VMEM, VMEM],
        out_specs=[VMEM] * 4,
        compiler_params=params(),
    )(kept.reshape(SIDE, part, WIDTH), came.reshape(SIDE, part, WIDTH))


def settle_body(stream_ref, own_ref, a_ref, b_ref, c_ref, out_ref):
    total = own_ref[...]
    for piece in (a_ref, b_ref, c_ref):
        total = total + piece[...].astype(jnp.float32)
    out_ref[...] = (stream_ref[...].astype(jnp.float32) + total).astype(jnp.bfloat16)


def settle(stream_rows, own, pieces):
    return pl.pallas_call(
        settle_body,
        out_shape=jax.ShapeDtypeStruct(own.shape, jnp.bfloat16),
        in_specs=[VMEM] * 5,
        out_specs=VMEM,
        compiler_params=params(),
    )(stream_rows, own, *pieces)


def lay_body(one_ref, two_ref, three_ref, own_ref, out_ref):
    for at, block in zip(relative(place()[2]), (one_ref, two_ref, three_ref, own_ref)):
        out_ref[at] = block[...]


def lay(blocks):
    return pl.pallas_call(
        lay_body,
        out_shape=jax.ShapeDtypeStruct((SIDE,) + blocks[0].shape, jnp.bfloat16),
        in_specs=[VMEM] * 4,
        out_specs=VMEM,
        compiler_params=params(),
    )(*blocks)


def assemble_body(this_ref, other_ref, gain_ref, residual_ref, rows_ref, squares_ref):
    core = place()[3]
    gain = gain_ref[...].astype(jnp.float32)
    for which, half_ref in ((core, this_ref), (1 - core, other_ref)):
        size = half_ref.shape[0]
        residual_ref[pl.ds(pl.multiple_of(which * size, size), size), :] = half_ref[...]
        widened = half_ref[...].astype(jnp.float32)
        totals = jnp.sum(widened * widened, axis=1, keepdims=True)
        first = which * (SIDE // 2)
        rows_ref[pl.ds(first, SIDE // 2)] = (
            (widened * gain).astype(jnp.bfloat16).reshape(SIDE // 2, SIDE, ROWS, WIDTH)
        )
        squares_ref[pl.ds(first, SIDE // 2)] = jnp.broadcast_to(totals, (size, HD)).reshape(
            SIDE // 2, SIDE, ROWS, HD
        )


def assemble(this_half, other_half, gain):
    return pl.pallas_call(
        assemble_body,
        out_shape=[
            jax.ShapeDtypeStruct((REQS, WIDTH), jnp.bfloat16),
            jax.ShapeDtypeStruct((SIDE, SIDE, ROWS, WIDTH), jnp.bfloat16),
            jax.ShapeDtypeStruct((SIDE, SIDE, ROWS, HD), jnp.float32),
        ],
        in_specs=[VMEM] * 3,
        out_specs=[VMEM] * 3,
        compiler_params=params(),
    )(this_half, other_half, gain)


def project_body(lines, outs, came, rows_ref, squares_ref, *refs):
    refs = list(refs)
    weights = [refs.pop(0) for _ in lines]
    added = [[refs.pop(0) for _ in range(came)] for _ in lines]
    size = 2 * ROWS
    for line, weight_ref, pieces in zip(lines, weights, added):
        targets = []
        for k, groups in enumerate(outs):
            out = refs.pop(0)
            for first, group in enumerate(groups):
                targets.append((out, first * size, pieces[k] if k < came and first == 0 else None, group))
        here = place()[line]
        at = []
        for _, _, _, (step, half) in targets:
            there = (here + step) % SIDE
            for other in (2 * half, 2 * half + 1):
                at.append((other, there) if line else (there, other))
        lhs = jnp.concatenate([rows_ref[i, j] for i, j in at], axis=0)
        columns = weight_ref.shape[1]
        product = jnp.dot(lhs, weight_ref[...], preferred_element_type=jnp.float32)
        for k, (out, first, extra, _) in enumerate(targets):
            piece = product[size * k : size * (k + 1)]
            if extra is not None:
                piece = piece + extra[:, :columns].astype(jnp.float32)
            out[first : first + size, :columns] = piece.astype(out.dtype)
            if line:
                piece = jnp.concatenate([squares_ref[i, j] for i, j in at[2 * k : 2 * k + 2]], axis=0)
                if extra is not None:
                    piece = piece + extra[:, columns:].astype(jnp.float32)
                out[first : first + size, columns:] = piece.astype(out.dtype)


def project(lines, outs, rows, squares, weights, dtypes, came=()):
    columns = [weights[line].shape[1] + (HD if line else 0) for line in lines]
    operands = [rows, squares] + [weights[line] for line in lines]
    operands += [piece for line in lines for piece in (came[line] if came else ())]
    results = pl.pallas_call(
        functools.partial(project_body, lines, outs, 2 if came else 0),
        out_shape=[
            jax.ShapeDtypeStruct((2 * ROWS * len(groups), n), dtype)
            for n in columns
            for groups, dtype in zip(outs, dtypes)
        ],
        in_specs=[VMEM] * len(operands),
        out_specs=[VMEM] * (len(lines) * len(outs)),
        compiler_params=params(),
    )(*operands)
    size = len(outs)
    return {line: results[size * k : size * (k + 1)] for k, line in enumerate(lines)}


def merge_body(*refs):
    sums = refs[-2:]
    size = 2 * ROWS
    for line in range(2):
        own_ref, before_ref, after_ref = refs[3 * line : 3 * line + 3]
        outs = refs[6 + 4 * line : 10 + 4 * line]
        sums_ref = sums[line]
        for k in range(2):
            total = own_ref[size * k : size * (k + 1)]
            for ref, first in ((before_ref, size * k), (after_ref, size * (1 - k))):
                total = total + ref[first : first + size].astype(jnp.float32)
            sums_ref[2 * k : 2 * k + 2] = total.reshape(2, ROWS, sums_ref.shape[2])
        for at, out in zip(relative(place()[1 - line]), outs):
            out[...] = sums_ref[at].astype(out.dtype)


def merge(parts):
    columns = [parts[line][0].shape[1] for line in range(2)]
    results = pl.pallas_call(
        merge_body,
        out_shape=[
            jax.ShapeDtypeStruct((ROWS, n), dtype)
            for n in columns
            for dtype in [jnp.bfloat16] * 3 + [jnp.float32]
        ],
        in_specs=[VMEM] * 6,
        out_specs=[VMEM] * 8,
        scratch_shapes=[pltpu.VMEM((SIDE, ROWS, n), jnp.float32) for n in columns],
        compiler_params=params(),
    )(*parts[0], *parts[1])
    return results[:4], results[4:]


def along_z(x, shift):
    return lax.ppermute(
        x, "attn", [(y * SIDE + z, y * SIDE + (z + shift) % SIDE) for y in range(SIDE) for z in range(SIDE)]
    )


def along_y(x, shift):
    return lax.ppermute(
        x, "attn", [(y * SIDE + z, (y + shift) % SIDE * SIDE + z) for y in range(SIDE) for z in range(SIDE)]
    )


def along_x(x, shift):
    return lax.ppermute(
        x, "ffn", [(chip * 2 + core, (chip + shift) % SIDE * 2 + core) for chip in range(SIDE) for core in range(2)]
    )


def to_sibling(x):
    return lax.ppermute(x, "ffn", [(f, f ^ 1) for f in range(8)])


LINES = (along_y, along_z)


def scatter(rows, squares, weights):
    far = project((1, 0), (((2, 0),), ((2, 1),)), rows, squares, weights, [jnp.bfloat16] * 2)
    came = {line: (LINES[line](far[line][0], 1), LINES[line](far[line][1], 3)) for line in (1, 0)}
    parts = {}
    for line in (1, 0):
        outs = (((1, 0), (1, 1)), ((3, 1), (3, 0)), ((0, 0), (0, 1)))
        dtypes = [jnp.bfloat16, jnp.bfloat16, jnp.float32]
        up, down, own = project((line,), outs, rows, squares, weights, dtypes, came)[line]
        parts[line] = (own, LINES[line](up, 1), LINES[line](down, 3))
    up_blocks, gate_blocks = merge(parts)
    sums = []
    for cross, (one, two, three, mine) in ((along_y, gate_blocks), (along_z, up_blocks)):
        sums.append((mine, cross(two, 2), cross(one, 1), cross(three, 3)))
    return sums


def line_of(shift, x):
    two, one, three = shift(x, 2), shift(x, 3), shift(x, 1)
    return one, two, three, x


def on_device(
    stream,
    queries,
    k_pool,
    v_pool,
    page_table,
    lengths,
    home_device,
    w_out,
    norm_gain,
    w_gate,
    w_up,
):
    f32 = jnp.float32
    home = home_device.reshape(1, REQS)
    lengths = lengths.reshape(1, REQS)

    table = page_table.T
    outgoing, dest = dispatch(home, queries)
    listed, *here = prepare(home, lengths, table, k_pool, v_pool)
    arrived = lax.all_to_all(outgoing, "attn", split_axis=0, concat_axis=0, tiled=True)
    blended = attend(listed, arrived, *here)
    returned = lax.all_to_all(blended, "attn", split_axis=0, concat_axis=0, tiled=True)
    left, right = collect(dest, returned)
    stream_rows = own_stream(stream, left)
    left, right = gather_line(line_of(along_z, left), line_of(along_y, right))
    gathered = gather_all(line_of(along_y, left), line_of(along_z, right))
    half = REQS // 2
    gathered = gathered.reshape(2, half, HEADS * HD)

    came = to_sibling(half_project(True, gathered, w_out))
    kept = half_project(False, gathered, w_out)
    one, two, three, own = pair(kept, came)
    pieces = (along_x(two, 2), along_x(one, 1), along_x(three, 3))
    mine_rows = settle(stream_rows, own, pieces)
    others = (along_x(mine_rows, 3), along_x(mine_rows, 2), along_x(mine_rows, 1))
    this_half = lay(others + (mine_rows,)).reshape(half, WIDTH)
    other_half = to_sibling(this_half)
    residual, rows, squares = assemble(this_half, other_half, norm_gain.reshape(1, WIDTH))

    gate_parts, up_parts = scatter(rows, squares, (w_up, w_gate))
    gate = sum(p.astype(f32) for p in gate_parts)
    columns = w_gate.shape[1]
    scaling = lax.rsqrt(gate[:, columns : columns + 1] / D + EPS)
    gate = gate[:, :columns] * scaling
    up = sum(p.astype(f32) for p in up_parts) * scaling
    hidden = (jax.nn.silu(gate) * up).astype(jnp.bfloat16)
    return (residual, hidden)


def solution(mesh):
    return jax.shard_map(
        on_device,
        mesh=mesh,
        in_specs=(
            P(None, "attn"),
            P("attn", "ffn"),
            P("attn", None, "ffn"),
            P("attn", None, "ffn"),
            P(),
            P(),
            P(),
            P("ffn", "attn"),
            P("attn"),
            P("attn", "ffn"),
            P("attn", "ffn"),
        ),
        out_specs=(P(None, "attn"), P("attn", "ffn")),
        check_vma=False,
    )
```

time: 174 us -> 162 us (0.931)
  starting transfers between devices: 36.3 us -> 57.3 us
  Pallas kernels: 43.2 us -> 23.9 us
  blocking collectives: 31.7 us -> 16.3 us
  waiting for transfers between devices: 52.6 us -> 58 us
  local copies, waits for them, and re-layouts: 7.06 us -> 4.7 us
    all_to_all x1 -> x0, blocking collectives: 16.8 us -> none  [on_device(): lax.all_to_all(outgoing, 'attn', split_axis=0, concat_axis=0, tiled=True)]
    ppermute x9 -> x13, waiting for transfers between devices: 10 us -> 26.5 us  [along_y(): lax.ppermute(x, 'attn', [(y * SIDE + z, (y + shift) % SIDE * SIDE + z) fo...]
    pallas_call x11 -> x10, Pallas kernels: 28.2 us -> 14.2 us  [the longest x3 7.55 us: project(): pl.pallas_call(functools.partial(project_body, lines, outs, 2 if came els...]
    all_to_all x1, waiting for transfers between devices: 12.7 us -> 1 us  [on_device(): lax.all_to_all(outgoing, 'attn', split_axis=0, concat_axis=0, tiled=True)]
    ppermute x9 -> x13, starting transfers between devices: 12 us -> 21.9 us  [along_z(): lax.ppermute(x, 'attn', [(y * SIDE + z, y * SIDE + (z + shift) % SIDE) fo...]
    ppermute x9 -> x13, starting transfers between devices: 9.29 us -> 16.7 us  [along_y(): lax.ppermute(x, 'attn', [(y * SIDE + z, (y + shift) % SIDE * SIDE + z) fo...]
    all_to_all x1, starting transfers between devices: 3.73 us -> 8.14 us  [on_device(): lax.all_to_all(outgoing, 'attn', split_axis=0, concat_axis=0, tiled=True)]
    pallas_call x1, Pallas kernels: 8.26 us -> 5.64 us  [attend(): pl.pallas_call(attend_body, out_shape=jax.ShapeDtypeStruct((SLOTS, HEADS,...]
  transfers between devices with their start and end apart: 27 -> 35, of which waited for: 17 -> 22; matrix products, arithmetic and copies ran while one was open for 0% -> 0% of each run, Pallas kernels for 14% -> 6%
where the time goes in v3:
time: 162 us
  waiting for transfers between devices  58 us (36%)
  starting transfers between devices  57.3 us (35%)
  Pallas kernels  23.9 us (15%)
  blocking collectives  16.3 us (10%)
  local copies, waits for them, and re-layouts  4.7 us (3%)
    ppermute x13, waiting for transfers between devices, along_y(): lax.ppermute(x, 'attn', [(y * SIDE + z, (y + shift) % SIDE * SIDE + z) fo...  26.5 us
    ppermute x13, starting transfers between devices, along_z(): lax.ppermute(x, 'attn', [(y * SIDE + z, y * SIDE + (z + shift) % SIDE) fo...  21.9 us
    ppermute x13, starting transfers between devices, along_y(): lax.ppermute(x, 'attn', [(y * SIDE + z, (y + shift) % SIDE * SIDE + z) fo...  16.7 us
    ppermute x13, waiting for transfers between devices, along_z(): lax.ppermute(x, 'attn', [(y * SIDE + z, y * SIDE + (z + shift) % SIDE) fo...  16.7 us
    all_to_all x1, blocking collectives, on_device(): lax.all_to_all(blended, 'attn', split_axis=0, concat_axis=0, tiled=True)  16.3 us
    ppermute x6, waiting for transfers between devices, along_x(): lax.ppermute(x, 'ffn', [(chip * 2 + core, (chip + shift) % SIDE * 2 + cor...  11.3 us
    ppermute x6, starting transfers between devices, along_x(): lax.ppermute(x, 'ffn', [(chip * 2 + core, (chip + shift) % SIDE * 2 + cor...  10.2 us
    all_to_all x1, starting transfers between devices, on_device(): lax.all_to_all(outgoing, 'attn', split_axis=0, concat_axis=0, tiled=True)  8.14 us
  transfers between devices with their start and end apart: 35, of which 22 were waited for; matrix products, arithmetic and copies ran while one was open for 0% of the time, Pallas kernels for 6%

profile of v3, /device:TPU:0, one launch (start us, length us, event | category | flops | bytes accessed | tf_op | source)
XLA Modules:
  0.0 162.3 jit_solution(17788389547437311888)
XLA Ops:
  2.4 8.1 %all-to-all-start = ((bf16[64,16,128]{2,1,0:T(8,128)(2,1)}), bf16[64,16,128]{2,1,0:T(8,128)(2,1)S(1)}, u32[]{:S(2)}, u32[]{:S(2)}) async-start(bf16[64,16,128]{2,1,0:T(8,128)(2,1)} %get-tuple-element.42), calls=%async_computation | async-start | bytes 524288 | tf_op jit(solution)/shard_map/all_to_all | solution.py:536
  15.2 2.8 %shard_map.123 = (s32[2,128]{1,0:T(2,128)S(1)}, s32[1,512]{1,0:T(1,128)S(1)}, s32[32,512]{1,0:T(8,128)S(1)}, bf16[256,16,128]{2,1,0:T(8,128)(2,1)S(1)}, bf16[256,16,128]{2,1,0:T(8,128)(2,1)S(1)}) custom-call(s32[1,512]{1,0:T(1,128)S(1)} %bitcast.19, s32[1,512]{1,0:T(1,128)S(1)} %bitcast.20, s32[32,512]{1,0:T(8,128)S(1)} %bitcast.17, ...), custom_call_target="tpu_custom_call" | custom-call | tf_op jit(solution)/shard_map/pallas_call | solution.py:135
  19.1 5.6 %shard_map.124 = bf16[64,16,128]{2,1,0:T(8,128)(2,1)S(1)} custom-call(s32[1,512]{1,0:T(1,128)S(1)} %get-tuple-element.39.lengths_vmem, s32[32,512]{1,0:T(8,128)S(1)} %get-tuple-element.40.table_vmem, s32[2,128]{1,0:T(2,128)S(1)} %get-tuple-element.41.list_ref, bf16[64,16,128]{2,1,0:T(8,128)(2,1)S(1)} %all-to-all-done.queries_ref, ...), custom_call_target="tpu_custom_call" | custom-call | tf_op jit(solution)/shard_map/pallas_call | solution.py:197
  24.7 16.3 %all_to_all.10.slots_ref = bf16[64,16,128]{2,1,0:T(8,128)(2,1)S(1)} all-to-all(bf16[64,16,128]{2,1,0:T(8,128)(2,1)S(1)} %shard_map.124), channel_id=1, replica_groups=mesh['attn'=16,'ffn'=8] {'attn'}, dimensions={0} | all-to-all | bytes 524288 | tf_op jit(solution)/shard_map/all_to_all | solution.py:538
  52.7 3.2 %collective-permute-start.10 = (bf16[4,32,1024]{2,1,0:T(8,128)(2,1)S(1)}, bf16[4,32,1024]{2,1,0:T(8,128)(2,1)S(1)}, u32[]{:S(2)}, u32[]{:S(2)}) collective-permute-start(bf16[4,32,1024]{2,1,0:T(8,128)(2,1)S(1)} %get-tuple-element.48.refs_7_), channel_id=1, source_target_pairs={{0,16},{8,24},{16,0},{24,8},{32,48},{40,56},{48,32},{56,40},{64,80... | collective-permute-start | bytes 786440 | tf_op jit(solution)/shard_map/ppermute | solution.py:471
  59.0 2.3 %collective-permute-done.10.refs_5_ = bf16[4,32,1024]{2,1,0:T(8,128)(2,1)S(1)} collective-permute-done((bf16[4,32,1024]{2,1,0:T(8,128)(2,1)S(1)}, bf16[4,32,1024]{2,1,0:T(8,128)(2,1)S(1)}, u32[]{:S(2)}, u32[]{:S(2)}) %collective-permute-start.10) | collective-permute-done | bytes 262176 | tf_op jit(solution)/shard_map/ppermute | solution.py:471
  61.3 4.7 %collective-permute-start.9 = (bf16[4,32,1024]{2,1,0:T(8,128)(2,1)S(1)}, bf16[4,32,1024]{2,1,0:T(8,128)(2,1)S(1)}, u32[]{:S(2)}, u32[]{:S(2)}) collective-permute-start(bf16[4,32,1024]{2,1,0:T(8,128)(2,1)S(1)} %get-tuple-element.48.refs_7_), channel_id=1, source_target_pairs={{0,24},{8,0},{16,8},{24,16},{32,56},{40,32},{48,40},{56,48},{64,88... | collective-permute-start | bytes 786440 | tf_op jit(solution)/shard_map/ppermute | solution.py:471
  66.0 2.2 %collective-permute-done.8.refs_2_ = bf16[4,32,1024]{2,1,0:T(8,128)(2,1)S(1)} collective-permute-done((bf16[4,32,1024]{2,1,0:T(8,128)(2,1)S(1)}, bf16[4,32,1024]{2,1,0:T(8,128)(2,1)S(1)}, u32[]{:S(2)}, u32[]{:S(2)}) %collective-permute-start.8) | collective-permute-done | bytes 262176 | tf_op jit(solution)/shard_map/ppermute | solution.py:477
  73.4 3.1 %collective-permute-start.13 = (bf16[64,1024]{1,0:T(8,128)(2,1)S(1)}, bf16[64,1024]{1,0:T(8,128)(2,1)S(1)}, u32[]{:S(2)}, u32[]{:S(2)}) collective-permute-start(bf16[64,1024]{1,0:T(8,128)(2,1)S(1)} %get-tuple-element.50), channel_id=1, source_target_pairs={{0,4},{1,5},{2,6},{3,7},{4,0},{5,1},{6,2},{7,3},{8,12},{9,13},{10,... | collective-permute-start | bytes 393224 | tf_op jit(solution)/shard_map/ppermute | solution.py:483
  77.1 2.6 %collective-permute-start.15 = (bf16[64,1024]{1,0:T(8,128)(2,1)S(1)}, bf16[64,1024]{1,0:T(8,128)(2,1)S(1)}, u32[]{:S(2)}, u32[]{:S(2)}) collective-permute-start(bf16[64,1024]{1,0:T(8,128)(2,1)S(1)} %get-tuple-element.52), channel_id=1, source_target_pairs={{0,6},{1,7},{2,0},{3,1},{4,2},{5,3},{6,4},{7,5},{8,14},{9,15},{10,... | collective-permute-start | bytes 393224 | tf_op jit(solution)/shard_map/ppermute | solution.py:483
  81.4 2.2 %collective-permute-done.14.b_ref = bf16[64,1024]{1,0:T(8,128)(2,1)S(1)} collective-permute-done((bf16[64,1024]{1,0:T(8,128)(2,1)S(1)}, bf16[64,1024]{1,0:T(8,128)(2,1)S(1)}, u32[]{:S(2)}, u32[]{:S(2)}) %collective-permute-start.14) | collective-permute-done | bytes 131104 | tf_op jit(solution)/shard_map/ppermute | solution.py:483
  83.7 2.9 %collective-permute-start.16 = (bf16[64,1024]{1,0:T(8,128)(2,1)S(1)}, bf16[64,1024]{1,0:T(8,128)(2,1)S(1)}, u32[]{:S(2)}, u32[]{:S(2)}) collective-permute-start(bf16[64,1024]{1,0:T(8,128)(2,1)S(1)} %shard_map.132.own_ref), channel_id=1, source_target_pairs={{0,6},{1,7},{2,0},{3,1},{4,2},{5,3},{6,4},{7,5},{8,14},{9,15},{10,... | collective-permute-start | bytes 393224 | tf_op jit(solution)/shard_map/ppermute | solution.py:483
  87.5 4.0 %collective-permute-done.16.one_ref = bf16[64,1024]{1,0:T(8,128)(2,1)S(1)} collective-permute-done((bf16[64,1024]{1,0:T(8,128)(2,1)S(1)}, bf16[64,1024]{1,0:T(8,128)(2,1)S(1)}, u32[]{:S(2)}, u32[]{:S(2)}) %collective-permute-start.16) | collective-permute-done | bytes 131104 | tf_op jit(solution)/shard_map/ppermute | solution.py:483
  91.5 2.3 %collective-permute-done.17.two_ref = bf16[64,1024]{1,0:T(8,128)(2,1)S(1)} collective-permute-done((bf16[64,1024]{1,0:T(8,128)(2,1)S(1)}, bf16[64,1024]{1,0:T(8,128)(2,1)S(1)}, u32[]{:S(2)}, u32[]{:S(2)}) %collective-permute-start.17) | collective-permute-done | bytes 131104 | tf_op jit(solution)/shard_map/ppermute | solution.py:483
  101.4 3.2 %collective-permute-start.25 = (bf16[64,3456]{1,0:T(8,128)(2,1)S(1)}, bf16[64,3456]{1,0:T(8,128)(2,1)S(1)}, u32[]{:S(2)}, u32[]{:S(2)}) collective-permute-start(bf16[64,3456]{1,0:T(8,128)(2,1)S(1)} %get-tuple-element.62), channel_id=1, source_target_pairs={{0,24},{8,0},{16,8},{24,16},{32,56},{40,32},{48,40},{56,48},{64,88... | collective-permute-start | bytes 1327112 | tf_op jit(solution)/shard_map/ppermute | solution.py:471
  104.8 3.0 %collective-permute-start.21 = (bf16[64,3328]{1,0:T(8,128)(2,1)S(1)}, bf16[64,3328]{1,0:T(8,128)(2,1)S(1)}, u32[]{:S(2)}, u32[]{:S(2)}) collective-permute-start(bf16[64,3328]{1,0:T(8,128)(2,1)S(1)} %get-tuple-element.57), channel_id=1, source_target_pairs={{0,96},{8,104},{16,112},{24,120},{32,0},{40,8},{48,16},{56,24},{64... | collective-permute-start | bytes 1277960 | tf_op jit(solution)/shard_map/ppermute | solution.py:477
  107.8 7.1 %collective-permute-done.24.refs_1_ = bf16[64,3456]{1,0:T(8,128)(2,1)S(1)} collective-permute-done((bf16[64,3456]{1,0:T(8,128)(2,1)S(1)}, bf16[64,3456]{1,0:T(8,128)(2,1)S(1)}, u32[]{:S(2)}, u32[]{:S(2)}) %collective-permute-start.24) | collective-permute-done | bytes 442400 | tf_op jit(solution)/shard_map/ppermute | solution.py:471
  115.0 2.8 %shard_map.137 = (bf16[128,3456]{1,0:T(8,128)(2,1)S(1)}, bf16[128,3456]{1,0:T(8,128)(2,1)S(1)}, f32[128,3456]{1,0:T(8,128)S(1)}) custom-call(bf16[4,4,32,1024]{3,2,1,0:T(8,128)(2,1)S(1)} %get-tuple-element.54.rows_ref, f32[4,4,32,128]{3,2,1,0:T(8,128)S(1)} %get-tuple-element.55.squares_ref, bf16[1024,3328]{1,0:T(8,128)(2,1)S(1)} %bitcast.8, ...), custom_call_target="tpu_custom_call" | custom-call | tf_op jit(solution)/shard_map/pallas_call | solution.py:422
  121.1 2.8 %shard_map.136 = (bf16[128,3328]{1,0:T(8,128)(2,1)S(1)}, bf16[128,3328]{1,0:T(8,128)(2,1)S(1)}, f32[128,3328]{1,0:T(8,128)S(1)}) custom-call(bf16[4,4,32,1024]{3,2,1,0:T(8,128)(2,1)S(1)} %get-tuple-element.54.rows_ref, f32[4,4,32,128]{3,2,1,0:T(8,128)S(1)} %get-tuple-element.55.squares_ref, bf16[1024,3328]{1,0:T(8,128)(2,1)S(1)} %bitcast.10, ...), custom_call_target="tpu_custom_call" | custom-call | tf_op jit(solution)/shard_map/pallas_call | solution.py:422
  124.1 3.0 %collective-permute-start.23 = (bf16[128,3328]{1,0:T(8,128)(2,1)S(1)}, bf16[128,3328]{1,0:T(8,128)(2,1)S(1)}, u32[]{:S(2)}, u32[]{:S(2)}) collective-permute-start(bf16[128,3328]{1,0:T(8,128)(2,1)S(1)} %get-tuple-element.60), channel_id=1, source_target_pairs={{0,96},{8,104},{16,112},{24,120},{32,0},{40,8},{48,16},{56,24},{64... | collective-permute-start | bytes 2555912 | tf_op jit(solution)/shard_map/ppermute | solution.py:477
  127.2 17.9 %collective-permute-done.22.refs_1_ = bf16[128,3328]{1,0:T(8,128)(2,1)S(1)} collective-permute-done((bf16[128,3328]{1,0:T(8,128)(2,1)S(1)}, bf16[128,3328]{1,0:T(8,128)(2,1)S(1)}, u32[]{:S(2)}, u32[]{:S(2)}) %collective-permute-start.22) | collective-permute-done | bytes 852000 | tf_op jit(solution)/shard_map/ppermute | solution.py:477
  147.6 2.3 %collective-permute-start.29 = (bf16[32,3456]{1,0:T(8,128)(2,1)S(1)}, bf16[32,3456]{1,0:T(8,128)(2,1)S(1)}, u32[]{:S(2)}, u32[]{:S(2)}) collective-permute-start(bf16[32,3456]{1,0:T(8,128)(2,1)S(1)} %get-tuple-element.68), channel_id=1, source_target_pairs={{0,32},{8,40},{16,48},{24,56},{32,64},{40,72},{48,80},{56,88},{64,... | collective-permute-start | bytes 663560 | tf_op jit(solution)/shard_map/ppermute | solution.py:477
  153.2 2.4 %collective-permute-done.28 = bf16[32,3456]{1,0:T(8,128)(2,1)S(1)} collective-permute-done((bf16[32,3456]{1,0:T(8,128)(2,1)S(1)}, bf16[32,3456]{1,0:T(8,128)(2,1)S(1)}, u32[]{:S(2)}, u32[]{:S(2)}) %collective-permute-start.28) | collective-permute-done | bytes 221216 | tf_op jit(solution)/shard_map/ppermute | solution.py:477
  159.2 2.1 %collective-permute-done.32 = bf16[32,3328]{1,0:T(8,128)(2,1)S(1)} collective-permute-done((bf16[32,3328]{1,0:T(8,128)(2,1)S(1)}, bf16[32,3328]{1,0:T(8,128)(2,1)S(1)}, u32[]{:S(2)}, u32[]{:S(2)}) %collective-permute-start.32) | collective-permute-done | bytes 213024 | tf_op jit(solution)/shard_map/ppermute | solution.py:471
  (96 shorter events, 52.1 us)
Async XLA Ops:
  2.4 16.7 %all-to-all-start = ((bf16[64,16,128]{2,1,0:T(8,128)(2,1)}), bf16[64,16,128]{2,1,0:T(8,128)(2,1)S(1)}, u32[]{:S(2)}, u32[]{:S(2)}) async-start(bf16[64,16,128]{2,1,0:T(8,128)(2,1)} %get-tuple-element.42), calls=%async_computation | async-start | bytes 524288 | tf_op jit(solution)/shard_map/all_to_all | solution.py:536
  52.7 8.5 %collective-permute-start.10 = (bf16[4,32,1024]{2,1,0:T(8,128)(2,1)S(1)}, bf16[4,32,1024]{2,1,0:T(8,128)(2,1)S(1)}, u32[]{:S(2)}, u32[]{:S(2)}) collective-permute-start(bf16[4,32,1024]{2,1,0:T(8,128)(2,1)S(1)} %get-tuple-element.48.refs_7_), channel_id=1, source_target_pairs={{0,16},{8,24},{16,0},{24,8},{32,48},{40,56},{48,32},{56,40},{64,80... | collective-permute-start | bytes 786440 | tf_op jit(solution)/shard_map/ppermute | solution.py:471
  55.9 10.0 %collective-permute-start.11 = (bf16[4,32,1024]{2,1,0:T(8,128)(2,1)S(1)}, bf16[4,32,1024]{2,1,0:T(8,128)(2,1)S(1)}, u32[]{:S(2)}, u32[]{:S(2)}) collective-permute-start(bf16[4,32,1024]{2,1,0:T(8,128)(2,1)S(1)} %get-tuple-element.48.refs_7_), channel_id=1, source_target_pairs={{0,8},{8,16},{16,24},{24,0},{32,40},{40,48},{48,56},{56,32},{64,72... | collective-permute-start | bytes 786440 | tf_op jit(solution)/shard_map/ppermute | solution.py:471
  56.3 9.6 %collective-permute-start.6 = (bf16[4,32,1024]{2,1,0:T(8,128)(2,1)S(1)}, bf16[4,32,1024]{2,1,0:T(8,128)(2,1)S(1)}, u32[]{:S(2)}, u32[]{:S(2)}) collective-permute-start(bf16[4,32,1024]{2,1,0:T(8,128)(2,1)S(1)} %get-tuple-element.47.refs_3_), channel_id=1, source_target_pairs={{0,96},{8,104},{16,112},{24,120},{32,0},{40,8},{48,16},{56,24},{64... | collective-permute-start | bytes 786440 | tf_op jit(solution)/shard_map/ppermute | solution.py:477
  57.5 8.4 %collective-permute-start.7 = (bf16[4,32,1024]{2,1,0:T(8,128)(2,1)S(1)}, bf16[4,32,1024]{2,1,0:T(8,128)(2,1)S(1)}, u32[]{:S(2)}, u32[]{:S(2)}) collective-permute-start(bf16[4,32,1024]{2,1,0:T(8,128)(2,1)S(1)} %get-tuple-element.47.refs_3_), channel_id=1, source_target_pairs={{0,64},{8,72},{16,80},{24,88},{32,96},{40,104},{48,112},{56,120},{... | collective-permute-start | bytes 786440 | tf_op jit(solution)/shard_map/ppermute | solution.py:477
  58.4 9.8 %collective-permute-start.8 = (bf16[4,32,1024]{2,1,0:T(8,128)(2,1)S(1)}, bf16[4,32,1024]{2,1,0:T(8,128)(2,1)S(1)}, u32[]{:S(2)}, u32[]{:S(2)}) collective-permute-start(bf16[4,32,1024]{2,1,0:T(8,128)(2,1)S(1)} %get-tuple-element.47.refs_3_), channel_id=1, source_target_pairs={{0,32},{8,40},{16,48},{24,56},{32,64},{40,72},{48,80},{56,88},{64,... | collective-permute-start | bytes 786440 | tf_op jit(solution)/shard_map/ppermute | solution.py:477
  61.3 8.6 %collective-permute-start.9 = (bf16[4,32,1024]{2,1,0:T(8,128)(2,1)S(1)}, bf16[4,32,1024]{2,1,0:T(8,128)(2,1)S(1)}, u32[]{:S(2)}, u32[]{:S(2)}) collective-permute-start(bf16[4,32,1024]{2,1,0:T(8,128)(2,1)S(1)} %get-tuple-element.48.refs_7_), channel_id=1, source_target_pairs={{0,24},{8,0},{16,8},{24,16},{32,56},{40,32},{48,40},{56,48},{64,88... | collective-permute-start | bytes 786440 | tf_op jit(solution)/shard_map/ppermute | solution.py:471
  73.4 7.9 %collective-permute-start.13 = (bf16[64,1024]{1,0:T(8,128)(2,1)S(1)}, bf16[64,1024]{1,0:T(8,128)(2,1)S(1)}, u32[]{:S(2)}, u32[]{:S(2)}) collective-permute-start(bf16[64,1024]{1,0:T(8,128)(2,1)S(1)} %get-tuple-element.50), channel_id=1, source_target_pairs={{0,4},{1,5},{2,6},{3,7},{4,0},{5,1},{6,2},{7,3},{8,12},{9,13},{10,... | collective-permute-start | bytes 393224 | tf_op jit(solution)/shard_map/ppermute | solution.py:483
  83.7 7.8 %collective-permute-start.16 = (bf16[64,1024]{1,0:T(8,128)(2,1)S(1)}, bf16[64,1024]{1,0:T(8,128)(2,1)S(1)}, u32[]{:S(2)}, u32[]{:S(2)}) collective-permute-start(bf16[64,1024]{1,0:T(8,128)(2,1)S(1)} %shard_map.132.own_ref), channel_id=1, source_target_pairs={{0,6},{1,7},{2,0},{3,1},{4,2},{5,3},{6,4},{7,5},{8,14},{9,15},{10,... | collective-permute-start | bytes 393224 | tf_op jit(solution)/shard_map/ppermute | solution.py:483
  86.6 7.2 %collective-permute-start.17 = (bf16[64,1024]{1,0:T(8,128)(2,1)S(1)}, bf16[64,1024]{1,0:T(8,128)(2,1)S(1)}, u32[]{:S(2)}, u32[]{:S(2)}) collective-permute-start(bf16[64,1024]{1,0:T(8,128)(2,1)S(1)} %shard_map.132.own_ref), channel_id=1, source_target_pairs={{0,4},{1,5},{2,6},{3,7},{4,0},{5,1},{6,2},{7,3},{8,12},{9,13},{10,... | collective-permute-start | bytes 393224 | tf_op jit(solution)/shard_map/ppermute | solution.py:483
  87.2 8.0 %collective-permute-start.18 = (bf16[64,1024]{1,0:T(8,128)(2,1)S(1)}, bf16[64,1024]{1,0:T(8,128)(2,1)S(1)}, u32[]{:S(2)}, u32[]{:S(2)}) collective-permute-start(bf16[64,1024]{1,0:T(8,128)(2,1)S(1)} %shard_map.132.own_ref), channel_id=1, source_target_pairs={{0,2},{1,3},{2,4},{3,5},{4,6},{5,7},{6,0},{7,1},{8,10},{9,11},{10,... | collective-permute-start | bytes 393224 | tf_op jit(solution)/shard_map/ppermute | solution.py:483
  100.7 14.2 %collective-permute-start.24 = (bf16[64,3456]{1,0:T(8,128)(2,1)S(1)}, bf16[64,3456]{1,0:T(8,128)(2,1)S(1)}, u32[]{:S(2)}, u32[]{:S(2)}) collective-permute-start(bf16[64,3456]{1,0:T(8,128)(2,1)S(1)} %get-tuple-element.61), channel_id=1, source_target_pairs={{0,8},{8,16},{16,24},{24,0},{32,40},{40,48},{48,56},{56,32},{64,72... | collective-permute-start | bytes 1327112 | tf_op jit(solution)/shard_map/ppermute | solution.py:471
  101.4 13.6 %collective-permute-start.25 = (bf16[64,3456]{1,0:T(8,128)(2,1)S(1)}, bf16[64,3456]{1,0:T(8,128)(2,1)S(1)}, u32[]{:S(2)}, u32[]{:S(2)}) collective-permute-start(bf16[64,3456]{1,0:T(8,128)(2,1)S(1)} %get-tuple-element.62), channel_id=1, source_target_pairs={{0,24},{8,0},{16,8},{24,16},{32,56},{40,32},{48,40},{56,48},{64,88... | collective-permute-start | bytes 1327112 | tf_op jit(solution)/shard_map/ppermute | solution.py:471
  104.6 16.5 %collective-permute-start.20 = (bf16[64,3328]{1,0:T(8,128)(2,1)S(1)}, bf16[64,3328]{1,0:T(8,128)(2,1)S(1)}, u32[]{:S(2)}, u32[]{:S(2)}) collective-permute-start(bf16[64,3328]{1,0:T(8,128)(2,1)S(1)} %get-tuple-element.56), channel_id=1, source_target_pairs={{0,32},{8,40},{16,48},{24,56},{32,64},{40,72},{48,80},{56,88},{64,... | collective-permute-start | bytes 1277960 | tf_op jit(solution)/shard_map/ppermute | solution.py:477
  104.8 16.3 %collective-permute-start.21 = (bf16[64,3328]{1,0:T(8,128)(2,1)S(1)}, bf16[64,3328]{1,0:T(8,128)(2,1)S(1)}, u32[]{:S(2)}, u32[]{:S(2)}) collective-permute-start(bf16[64,3328]{1,0:T(8,128)(2,1)S(1)} %get-tuple-element.57), channel_id=1, source_target_pairs={{0,96},{8,104},{16,112},{24,120},{32,0},{40,8},{48,16},{56,24},{64... | collective-permute-start | bytes 1277960 | tf_op jit(solution)/shard_map/ppermute | solution.py:477
  117.8 27.3 %collective-permute-start.26 = (bf16[128,3456]{1,0:T(8,128)(2,1)S(1)}, bf16[128,3456]{1,0:T(8,128)(2,1)S(1)}, u32[]{:S(2)}, u32[]{:S(2)}) collective-permute-start(bf16[128,3456]{1,0:T(8,128)(2,1)S(1)} %get-tuple-element.64), channel_id=1, source_target_pairs={{0,8},{8,16},{16,24},{24,0},{32,40},{40,48},{48,56},{56,32},{64,72... | collective-permute-start | bytes 2654216 | tf_op jit(solution)/shard_map/ppermute | solution.py:471
  119.0 26.1 %collective-permute-start.27 = (bf16[128,3456]{1,0:T(8,128)(2,1)S(1)}, bf16[128,3456]{1,0:T(8,128)(2,1)S(1)}, u32[]{:S(2)}, u32[]{:S(2)}) collective-permute-start(bf16[128,3456]{1,0:T(8,128)(2,1)S(1)} %get-tuple-element.65), channel_id=1, source_target_pairs={{0,24},{8,0},{16,8},{24,16},{32,56},{40,32},{48,40},{56,48},{64,88... | collective-permute-start | bytes 2654216 | tf_op jit(solution)/shard_map/ppermute | solution.py:471
  123.9 21.2 %collective-permute-start.22 = (bf16[128,3328]{1,0:T(8,128)(2,1)S(1)}, bf16[128,3328]{1,0:T(8,128)(2,1)S(1)}, u32[]{:S(2)}, u32[]{:S(2)}) collective-permute-start(bf16[128,3328]{1,0:T(8,128)(2,1)S(1)} %get-tuple-element.59), channel_id=1, source_target_pairs={{0,32},{8,40},{16,48},{24,56},{32,64},{40,72},{48,80},{56,88},{64,... | collective-permute-start | bytes 2555912 | tf_op jit(solution)/shard_map/ppermute | solution.py:477
  124.1 20.9 %collective-permute-start.23 = (bf16[128,3328]{1,0:T(8,128)(2,1)S(1)}, bf16[128,3328]{1,0:T(8,128)(2,1)S(1)}, u32[]{:S(2)}, u32[]{:S(2)}) collective-permute-start(bf16[128,3328]{1,0:T(8,128)(2,1)S(1)} %get-tuple-element.60), channel_id=1, source_target_pairs={{0,96},{8,104},{16,112},{24,120},{32,0},{40,8},{48,16},{56,24},{64... | collective-permute-start | bytes 2555912 | tf_op jit(solution)/shard_map/ppermute | solution.py:477
  146.1 9.5 %collective-permute-start.28 = (bf16[32,3456]{1,0:T(8,128)(2,1)S(1)}, bf16[32,3456]{1,0:T(8,128)(2,1)S(1)}, u32[]{:S(2)}, u32[]{:S(2)}) collective-permute-start(bf16[32,3456]{1,0:T(8,128)(2,1)S(1)} %get-tuple-element.67), channel_id=1, source_target_pairs={{0,64},{8,72},{16,80},{24,88},{32,96},{40,104},{48,112},{56,120},{... | collective-permute-start | bytes 663560 | tf_op jit(solution)/shard_map/ppermute | solution.py:477
  147.6 10.3 %collective-permute-start.29 = (bf16[32,3456]{1,0:T(8,128)(2,1)S(1)}, bf16[32,3456]{1,0:T(8,128)(2,1)S(1)}, u32[]{:S(2)}, u32[]{:S(2)}) collective-permute-start(bf16[32,3456]{1,0:T(8,128)(2,1)S(1)} %get-tuple-element.68), channel_id=1, source_target_pairs={{0,32},{8,40},{16,48},{24,56},{32,64},{40,72},{48,80},{56,88},{64,... | collective-permute-start | bytes 663560 | tf_op jit(solution)/shard_map/ppermute | solution.py:477
  150.0 7.9 %collective-permute-start.30 = (bf16[32,3456]{1,0:T(8,128)(2,1)S(1)}, bf16[32,3456]{1,0:T(8,128)(2,1)S(1)}, u32[]{:S(2)}, u32[]{:S(2)}) collective-permute-start(bf16[32,3456]{1,0:T(8,128)(2,1)S(1)} %get-tuple-element.69), channel_id=1, source_target_pairs={{0,96},{8,104},{16,112},{24,120},{32,0},{40,8},{48,16},{56,24},{64... | collective-permute-start | bytes 663560 | tf_op jit(solution)/shard_map/ppermute | solution.py:477
  150.9 8.4 %collective-permute-start.31 = (bf16[32,3328]{1,0:T(8,128)(2,1)S(1)}, bf16[32,3328]{1,0:T(8,128)(2,1)S(1)}, u32[]{:S(2)}, u32[]{:S(2)}) collective-permute-start(bf16[32,3328]{1,0:T(8,128)(2,1)S(1)} %get-tuple-element.71), channel_id=1, source_target_pairs={{0,16},{8,24},{16,0},{24,8},{32,48},{40,56},{48,32},{56,40},{64,80... | collective-permute-start | bytes 638984 | tf_op jit(solution)/shard_map/ppermute | solution.py:471
  152.1 9.3 %collective-permute-start.32 = (bf16[32,3328]{1,0:T(8,128)(2,1)S(1)}, bf16[32,3328]{1,0:T(8,128)(2,1)S(1)}, u32[]{:S(2)}, u32[]{:S(2)}) collective-permute-start(bf16[32,3328]{1,0:T(8,128)(2,1)S(1)} %get-tuple-element.72), channel_id=1, source_target_pairs={{0,8},{8,16},{16,24},{24,0},{32,40},{40,48},{48,56},{56,32},{64,72... | collective-permute-start | bytes 638984 | tf_op jit(solution)/shard_map/ppermute | solution.py:471
  (24 other events, 296.0 us)

commit v4 on v3

--- a/solution.py
+++ b/solution.py
@@ -19,7 +19,7 @@
 SLOTS = N_ATTN * CAP
 SIDE = 4
 WIDTH = 1024
-GROUP = 8
+GROUP = 4
 LISTED = 128
 SHORT = MAXP // 2
 EPS = 1e-05
@@ -149,11 +149,16 @@
 
 
 def attend_body(lengths_vmem, table_vmem, list_ref, queries_ref, k_ref, v_ref, out_ref, lengths_ref, table_ref, sems):
-    pairs = ((lengths_vmem, lengths_ref), (table_vmem, table_ref))
+    first, rest = pl.ds(0, SHORT), pl.ds(SHORT, MAXP - SHORT)
+    pairs = (
+        (lengths_vmem, lengths_ref),
+        (table_vmem.at[first], table_ref.at[first]),
+        (table_vmem.at[rest], table_ref.at[rest]),
+    )
     copies = start_all([pltpu.make_async_copy(a, b, sems.at[k]) for k, (a, b) in enumerate(pairs)])
     out_ref[...] = jnp.zeros_like(out_ref)
-    for copy in copies:
-        copy.wait()
+    copies[0].wait()
+    copies[1].wait()
 
     def step(kind, count, index, carry):
         positions = lax.broadcasted_iota(jnp.int32, (HEADS, count * PAGE), 1)
@@ -189,6 +194,8 @@
         return carry
 
     for kind, count in ((0, SHORT), (1, MAXP)):
+        if kind:
+            copies[2].wait()
         groups = (list_ref[kind, LISTED - 1] + GROUP - 1) // GROUP
         lax.fori_loop(0, groups, functools.partial(step, kind, count), 0)
 
@@ -202,7 +209,7 @@
         scratch_shapes=[
             pltpu.SMEM(lengths.shape, jnp.int32),
             pltpu.SMEM(table.shape, jnp.int32),
-            pltpu.SemaphoreType.DMA((2,)),
+            pltpu.SemaphoreType.DMA((3,)),
         ],
         compiler_params=params(),
     )(lengths, table, listed, queries, k_pool, v_pool)
@@ -383,88 +390,87 @@
     )(this_half, other_half, gain)
 
 
-def project_body(lines, outs, came, rows_ref, squares_ref, *refs):
-    refs = list(refs)
-    weights = [refs.pop(0) for _ in lines]
-    added = [[refs.pop(0) for _ in range(came)] for _ in lines]
+def project_body(outs, rows_ref, squares_ref, *refs):
     size = 2 * ROWS
-    for line, weight_ref, pieces in zip(lines, weights, added):
-        targets = []
+    for line in (1, 0):
+        weight_ref = refs[line]
+        here = place()[line]
+        targets, at = [], []
         for k, groups in enumerate(outs):
-            out = refs.pop(0)
-            for first, group in enumerate(groups):
-                targets.append((out, first * size, pieces[k] if k < came and first == 0 else None, group))
-        here = place()[line]
-        at = []
-        for _, _, _, (step, half) in targets:
-            there = (here + step) % SIDE
-            for other in (2 * half, 2 * half + 1):
-                at.append((other, there) if line else (there, other))
+            out = refs[2 + line * len(outs) + k]
+            for first, (step, half) in enumerate(groups):
+                targets.append((out, first * size))
+                there = (here + step) % SIDE
+                for other in (2 * half, 2 * half + 1):
+                    at.append((other, there) if line else (there, other))
         lhs = jnp.concatenate([rows_ref[i, j] for i, j in at], axis=0)
         columns = weight_ref.shape[1]
         product = jnp.dot(lhs, weight_ref[...], preferred_element_type=jnp.float32)
-        for k, (out, first, extra, _) in enumerate(targets):
-            piece = product[size * k : size * (k + 1)]
-            if extra is not None:
-                piece = piece + extra[:, :columns].astype(jnp.float32)
-            out[first : first + size, :columns] = piece.astype(out.dtype)
+        for k, (out, first) in enumerate(targets):
+            out[first : first + size, :columns] = product[size * k : size * (k + 1)].astype(out.dtype)
             if line:
                 piece = jnp.concatenate([squares_ref[i, j] for i, j in at[2 * k : 2 * k + 2]], axis=0)
-                if extra is not None:
-                    piece = piece + extra[:, columns:].astype(jnp.float32)
                 out[first : first + size, columns:] = piece.astype(out.dtype)
 
 
-def project(lines, outs, rows, squares, weights, dtypes, came=()):
-    columns = [weights[line].shape[1] + (HD if line else 0) for line in lines]
-    operands = [rows, squares] + [weights[line] for line in lines]
-    operands += [piece for line in lines for piece in (came[line] if came else ())]
+def project(outs, rows, squares, weights, dtypes):
+    columns = [weights[0].shape[1], weights[1].shape[1] + HD]
     results = pl.pallas_call(
-        functools.partial(project_body, lines, outs, 2 if came else 0),
+        functools.partial(project_body, outs),
         out_shape=[
             jax.ShapeDtypeStruct((2 * ROWS * len(groups), n), dtype)
             for n in columns
             for groups, dtype in zip(outs, dtypes)
         ],
-        in_specs=[VMEM] * len(operands),
-        out_specs=[VMEM] * (len(lines) * len(outs)),
-        compiler_params=params(),
-    )(*operands)
-    size = len(outs)
-    return {line: results[size * k : size * (k + 1)] for k, line in enumerate(lines)}
-
-
-def merge_body(*refs):
-    sums = refs[-2:]
+        in_specs=[VMEM] * 4,
+        out_specs=[VMEM] * (2 * len(outs)),
+        compiler_params=params(24),
+    )(rows, squares, *weights)
+    return results[: len(outs)], results[len(outs) :]
+
+
+def relay_body(*refs):
     size = 2 * ROWS
-    for line in range(2):
-        own_ref, before_ref, after_ref = refs[3 * line : 3 * line + 3]
-        outs = refs[6 + 4 * line : 10 + 4 * line]
-        sums_ref = sums[line]
-        for k in range(2):
-            total = own_ref[size * k : size * (k + 1)]
-            for ref, first in ((before_ref, size * k), (after_ref, size * (1 - k))):
-                total = total + ref[first : first + size].astype(jnp.float32)
-            sums_ref[2 * k : 2 * k + 2] = total.reshape(2, ROWS, sums_ref.shape[2])
-        for at, out in zip(relative(place()[1 - line]), outs):
-            out[...] = sums_ref[at].astype(out.dtype)
-
-
-def merge(parts):
-    columns = [parts[line][0].shape[1] for line in range(2)]
-    results = pl.pallas_call(
-        merge_body,
-        out_shape=[
-            jax.ShapeDtypeStruct((ROWS, n), dtype)
-            for n in columns
-            for dtype in [jnp.bfloat16] * 3 + [jnp.float32]
-        ],
+    for k in range(2):
+        part_ref, near_ref, came_ref, out = refs[k], refs[2 + k], refs[4 + k], refs[6 + k]
+        out[:size] = (part_ref[...] + came_ref[...].astype(jnp.float32)).astype(out.dtype)
+        out[size:] = near_ref[...]
+
+
+def relay(parts, nears, came):
+    shape = (4 * ROWS, parts[0].shape[1])
+    return pl.pallas_call(
+        relay_body,
+        out_shape=[jax.ShapeDtypeStruct(shape, jnp.bfloat16)] * 2,
         in_specs=[VMEM] * 6,
-        out_specs=[VMEM] * 8,
-        scratch_shapes=[pltpu.VMEM((SIDE, ROWS, n), jnp.float32) for n in columns],
-        compiler_params=params(),
-    )(*parts[0], *parts[1])
-    return results[:4], results[4:]
+        out_specs=[VMEM] * 2,
+        compiler_params=params(),
+    )(*parts, *nears, *came)
+
+
+def merge_body(line, own_ref, before_ref, after_ref, *refs):
+    outs, sums_ref = refs[:4], refs[4]
+    size = 2 * ROWS
+    for k in range(2):
+        total = own_ref[size * k : size * (k + 1)]
+        for ref, first in ((before_ref, size * k), (after_ref, size * (1 - k))):
+            total = total + ref[first : first + size].astype(jnp.float32)
+        sums_ref[2 * k : 2 * k + 2] = total.reshape(2, ROWS, sums_ref.shape[2])
+    for at, out in zip(relative(place()[1 - line]), outs):
+        out[...] = sums_ref[at].astype(out.dtype)
+
+
+def merge(line, own, before, after):
+    columns = own.shape[1]
+    return pl.pallas_call(
+        functools.partial(merge_body, line),
+        out_shape=[jax.ShapeDtypeStruct((ROWS, columns), jnp.bfloat16)] * 3
+        + [jax.ShapeDtypeStruct((ROWS, columns), jnp.float32)],
+        in_specs=[VMEM] * 3,
+        out_specs=[VMEM] * 4,
+        scratch_shapes=[pltpu.VMEM((SIDE, ROWS, columns), jnp.float32)],
+        compiler_params=params(),
+    )(own, before, after)
 
 
 def along_z(x, shift):
@@ -493,17 +499,19 @@
 
 
 def scatter(rows, squares, weights):
-    far = project((1, 0), (((2, 0),), ((2, 1),)), rows, squares, weights, [jnp.bfloat16] * 2)
+    far = project((((2, 0),), ((2, 1),)), rows, squares, weights, [jnp.bfloat16] * 2)
     came = {line: (LINES[line](far[line][0], 1), LINES[line](far[line][1], 3)) for line in (1, 0)}
+    outs = (((1, 0),), ((3, 1),), ((1, 1),), ((3, 0),), ((0, 0), (0, 1)))
+    dtypes = [jnp.float32] * 2 + [jnp.bfloat16] * 2 + [jnp.float32]
+    rest = project(outs, rows, squares, weights, dtypes)
     parts = {}
     for line in (1, 0):
-        outs = (((1, 0), (1, 1)), ((3, 1), (3, 0)), ((0, 0), (0, 1)))
-        dtypes = [jnp.bfloat16, jnp.bfloat16, jnp.float32]
-        up, down, own = project((line,), outs, rows, squares, weights, dtypes, came)[line]
-        parts[line] = (own, LINES[line](up, 1), LINES[line](down, 3))
-    up_blocks, gate_blocks = merge(parts)
+        up, down = relay(rest[line][:2], rest[line][2:4], came[line])
+        parts[line] = (rest[line][4], LINES[line](up, 1), LINES[line](down, 3))
     sums = []
-    for cross, (one, two, three, mine) in ((along_y, gate_blocks), (along_z, up_blocks)):
+    for line in (1, 0):
+        cross = LINES[1 - line]
+        one, two, three, mine = merge(line, *parts[line])
         sums.append((mine, cross(two, 2), cross(one, 1), cross(three, 3)))
     return sums
 

time: 162 us -> 155 us (0.957)
  waiting for transfers between devices: 58 us -> 47.8 us
  starting transfers between devices: 57.3 us -> 59.6 us
    ppermute x13, waiting for transfers between devices: 26.5 us -> 7.42 us  [along_y(): lax.ppermute(x, 'attn', [(y * SIDE + z, (y + shift) % SIDE * SIDE + z) fo...]
    ppermute x13, waiting for transfers between devices: 16.7 us -> 28.1 us  [along_z(): lax.ppermute(x, 'attn', [(y * SIDE + z, y * SIDE + (z + shift) % SIDE) fo...]
    ppermute x6, waiting for transfers between devices: 11.3 us -> 8.79 us  [along_x(): lax.ppermute(x, 'ffn', [(chip * 2 + core, (chip + shift) % SIDE * 2 + cor...]
    ppermute x13, starting transfers between devices: 16.7 us -> 18.9 us  [along_y(): lax.ppermute(x, 'attn', [(y * SIDE + z, (y + shift) % SIDE * SIDE + z) fo...]
    pallas_call x4 -> x6, Pallas kernels: 8.53 us -> 8.7 us  [the longest x2 7.38 us: project(): pl.pallas_call(functools.partial(project_body, outs), out_shape=[jax.Shap...]
  transfers between devices with their start and end apart: 35 -> 35, of which waited for: 22 -> 20; matrix products, arithmetic and copies ran while one was open for 0% -> 0% of each run, Pallas kernels for 6% -> 7%
where the time goes in v4:
time: 155 us; the launch traced here: 154 us
  starting transfers between devices  59.6 us (38%)
  waiting for transfers between devices  47.8 us (31%)
  Pallas kernels  24.1 us (16%)
  blocking collectives  15.8 us (10%)
  local copies, waits for them, and re-layouts  4.7 us (3%)
    ppermute x13, waiting for transfers between devices, along_z(): lax.ppermute(x, 'attn', [(y * SIDE + z, y * SIDE + (z + shift) % SIDE) fo...  28.1 us
    ppermute x13, starting transfers between devices, along_z(): lax.ppermute(x, 'attn', [(y * SIDE + z, y * SIDE + (z + shift) % SIDE) fo...  21.3 us
    ppermute x13, starting transfers between devices, along_y(): lax.ppermute(x, 'attn', [(y * SIDE + z, (y + shift) % SIDE * SIDE + z) fo...  18.9 us
    all_to_all x1, blocking collectives, on_device(): lax.all_to_all(blended, 'attn', split_axis=0, concat_axis=0, tiled=True)  15.8 us
    ppermute x6, starting transfers between devices, along_x(): lax.ppermute(x, 'ffn', [(chip * 2 + core, (chip + shift) % SIDE * 2 + cor...  11 us
    ppermute x6, waiting for transfers between devices, along_x(): lax.ppermute(x, 'ffn', [(chip * 2 + core, (chip + shift) % SIDE * 2 + cor...  8.79 us
    all_to_all x1, starting transfers between devices, on_device(): lax.all_to_all(outgoing, 'attn', split_axis=0, concat_axis=0, tiled=True)  8.14 us
    ppermute x13, waiting for transfers between devices, along_y(): lax.ppermute(x, 'attn', [(y * SIDE + z, (y + shift) % SIDE * SIDE + z) fo...  7.42 us
  transfers between devices with their start and end apart: 35, of which 20 were waited for; matrix products, arithmetic and copies ran while one was open for 0% of the time, Pallas kernels for 7%

profile of v4, /device:TPU:0, one launch (start us, length us, event | category | flops | bytes accessed | tf_op | source)
XLA Modules:
  0.0 154.1 jit_solution(17482196489595024983)
XLA Ops:
  2.4 8.1 %all-to-all-start = ((bf16[64,16,128]{2,1,0:T(8,128)(2,1)}), bf16[64,16,128]{2,1,0:T(8,128)(2,1)S(1)}, u32[]{:S(2)}, u32[]{:S(2)}) async-start(bf16[64,16,128]{2,1,0:T(8,128)(2,1)} %get-tuple-element.50), calls=%async_computation | async-start | bytes 524288 | tf_op jit(solution)/shard_map/all_to_all | solution.py:544
  15.2 2.8 %shard_map.123 = (s32[2,128]{1,0:T(2,128)S(1)}, s32[1,512]{1,0:T(1,128)S(1)}, s32[32,512]{1,0:T(8,128)S(1)}, bf16[256,16,128]{2,1,0:T(8,128)(2,1)S(1)}, bf16[256,16,128]{2,1,0:T(8,128)(2,1)S(1)}) custom-call(s32[1,512]{1,0:T(1,128)S(1)} %bitcast.19, s32[1,512]{1,0:T(1,128)S(1)} %bitcast.20, s32[32,512]{1,0:T(8,128)S(1)} %bitcast.17, ...), custom_call_target="tpu_custom_call" | custom-call | tf_op jit(solution)/shard_map/pallas_call | solution.py:135
  19.1 5.7 %shard_map.124 = bf16[64,16,128]{2,1,0:T(8,128)(2,1)S(1)} custom-call(s32[1,512]{1,0:T(1,128)S(1)} %get-tuple-element.47.lengths_vmem, s32[32,512]{1,0:T(8,128)S(1)} %get-tuple-element.48.table_vmem, s32[2,128]{1,0:T(2,128)S(1)} %get-tuple-element.49.list_ref, bf16[64,16,128]{2,1,0:T(8,128)(2,1)S(1)} %all-to-all-done.queries_ref, ...), custom_call_target="tpu_custom_call" | custom-call | tf_op jit(solution)/shard_map/pallas_call | solution.py:204
  24.8 15.8 %all_to_all.10.slots_ref = bf16[64,16,128]{2,1,0:T(8,128)(2,1)S(1)} all-to-all(bf16[64,16,128]{2,1,0:T(8,128)(2,1)S(1)} %shard_map.124), channel_id=1, replica_groups=mesh['attn'=16,'ffn'=8] {'attn'}, dimensions={0} | all-to-all | bytes 524288 | tf_op jit(solution)/shard_map/all_to_all | solution.py:546
  41.6 2.3 %collective-permute-start.4 = (bf16[32,1024]{1,0:T(8,128)(2,1)S(1)}, bf16[32,1024]{1,0:T(8,128)(2,1)S(1)}, u32[]{:S(2)}, u32[]{:S(2)}) collective-permute-start(bf16[32,1024]{1,0:T(8,128)(2,1)S(1)} %get-tuple-element.54.refs_7_), channel_id=1, source_target_pairs={{0,64},{8,72},{16,80},{24,88},{32,96},{40,104},{48,112},{56,120},{... | collective-permute-start | bytes 196616 | tf_op jit(solution)/shard_map/ppermute | solution.py:483
  54.8 2.5 %collective-permute-start.6 = (bf16[4,32,1024]{2,1,0:T(8,128)(2,1)S(1)}, bf16[4,32,1024]{2,1,0:T(8,128)(2,1)S(1)}, u32[]{:S(2)}, u32[]{:S(2)}) collective-permute-start(bf16[4,32,1024]{2,1,0:T(8,128)(2,1)S(1)} %get-tuple-element.55.refs_3_), channel_id=1, source_target_pairs={{0,96},{8,104},{16,112},{24,120},{32,0},{40,8},{48,16},{56,24},{64... | collective-permute-start | bytes 786440 | tf_op jit(solution)/shard_map/ppermute | solution.py:483
  58.7 2.8 %collective-permute-start.10 = (bf16[4,32,1024]{2,1,0:T(8,128)(2,1)S(1)}, bf16[4,32,1024]{2,1,0:T(8,128)(2,1)S(1)}, u32[]{:S(2)}, u32[]{:S(2)}) collective-permute-start(bf16[4,32,1024]{2,1,0:T(8,128)(2,1)S(1)} %get-tuple-element.56.refs_7_), channel_id=1, source_target_pairs={{0,16},{8,24},{16,0},{24,8},{32,48},{40,56},{48,32},{56,40},{64,80... | collective-permute-start | bytes 786440 | tf_op jit(solution)/shard_map/ppermute | solution.py:477
  63.5 2.4 %collective-permute-start.9 = (bf16[4,32,1024]{2,1,0:T(8,128)(2,1)S(1)}, bf16[4,32,1024]{2,1,0:T(8,128)(2,1)S(1)}, u32[]{:S(2)}, u32[]{:S(2)}) collective-permute-start(bf16[4,32,1024]{2,1,0:T(8,128)(2,1)S(1)} %get-tuple-element.56.refs_7_), channel_id=1, source_target_pairs={{0,24},{8,0},{16,8},{24,16},{32,56},{40,32},{48,40},{56,48},{64,88... | collective-permute-start | bytes 786440 | tf_op jit(solution)/shard_map/ppermute | solution.py:477
  65.9 2.7 %collective-permute-done.10.refs_5_ = bf16[4,32,1024]{2,1,0:T(8,128)(2,1)S(1)} collective-permute-done((bf16[4,32,1024]{2,1,0:T(8,128)(2,1)S(1)}, bf16[4,32,1024]{2,1,0:T(8,128)(2,1)S(1)}, u32[]{:S(2)}, u32[]{:S(2)}) %collective-permute-start.10) | collective-permute-done | bytes 262176 | tf_op jit(solution)/shard_map/ppermute | solution.py:477
  73.5 3.1 %collective-permute-start.13 = (bf16[64,1024]{1,0:T(8,128)(2,1)S(1)}, bf16[64,1024]{1,0:T(8,128)(2,1)S(1)}, u32[]{:S(2)}, u32[]{:S(2)}) collective-permute-start(bf16[64,1024]{1,0:T(8,128)(2,1)S(1)} %get-tuple-element.58), channel_id=1, source_target_pairs={{0,4},{1,5},{2,6},{3,7},{4,0},{5,1},{6,2},{7,3},{8,12},{9,13},{10,... | collective-permute-start | bytes 393224 | tf_op jit(solution)/shard_map/ppermute | solution.py:489
  77.2 2.6 %collective-permute-start.15 = (bf16[64,1024]{1,0:T(8,128)(2,1)S(1)}, bf16[64,1024]{1,0:T(8,128)(2,1)S(1)}, u32[]{:S(2)}, u32[]{:S(2)}) collective-permute-start(bf16[64,1024]{1,0:T(8,128)(2,1)S(1)} %get-tuple-element.60), channel_id=1, source_target_pairs={{0,6},{1,7},{2,0},{3,1},{4,2},{5,3},{6,4},{7,5},{8,14},{9,15},{10,... | collective-permute-start | bytes 393224 | tf_op jit(solution)/shard_map/ppermute | solution.py:489
  81.4 2.2 %collective-permute-done.14.b_ref = bf16[64,1024]{1,0:T(8,128)(2,1)S(1)} collective-permute-done((bf16[64,1024]{1,0:T(8,128)(2,1)S(1)}, bf16[64,1024]{1,0:T(8,128)(2,1)S(1)}, u32[]{:S(2)}, u32[]{:S(2)}) %collective-permute-start.14) | collective-permute-done | bytes 131104 | tf_op jit(solution)/shard_map/ppermute | solution.py:489
  85.2 3.0 %collective-permute-start.17 = (bf16[64,1024]{1,0:T(8,128)(2,1)S(1)}, bf16[64,1024]{1,0:T(8,128)(2,1)S(1)}, u32[]{:S(2)}, u32[]{:S(2)}) collective-permute-start(bf16[64,1024]{1,0:T(8,128)(2,1)S(1)} %shard_map.132.own_ref), channel_id=1, source_target_pairs={{0,4},{1,5},{2,6},{3,7},{4,0},{5,1},{6,2},{7,3},{8,12},{9,13},{10,... | collective-permute-start | bytes 393224 | tf_op jit(solution)/shard_map/ppermute | solution.py:489
  88.4 2.8 %collective-permute-done.18.three_ref = bf16[64,1024]{1,0:T(8,128)(2,1)S(1)} collective-permute-done((bf16[64,1024]{1,0:T(8,128)(2,1)S(1)}, bf16[64,1024]{1,0:T(8,128)(2,1)S(1)}, u32[]{:S(2)}, u32[]{:S(2)}) %collective-permute-start.18) | collective-permute-done | bytes 131104 | tf_op jit(solution)/shard_map/ppermute | solution.py:489
  91.2 2.2 %collective-permute-done.17.two_ref = bf16[64,1024]{1,0:T(8,128)(2,1)S(1)} collective-permute-done((bf16[64,1024]{1,0:T(8,128)(2,1)S(1)}, bf16[64,1024]{1,0:T(8,128)(2,1)S(1)}, u32[]{:S(2)}, u32[]{:S(2)}) %collective-permute-start.17) | collective-permute-done | bytes 131104 | tf_op jit(solution)/shard_map/ppermute | solution.py:489
  100.2 2.6 %collective-permute-start.21 = (bf16[64,3456]{1,0:T(8,128)(2,1)S(1)}, bf16[64,3456]{1,0:T(8,128)(2,1)S(1)}, u32[]{:S(2)}, u32[]{:S(2)}) collective-permute-start(bf16[64,3456]{1,0:T(8,128)(2,1)S(1)} %get-tuple-element.70), channel_id=1, source_target_pairs={{0,24},{8,0},{16,8},{24,16},{32,56},{40,32},{48,40},{56,48},{64,88... | collective-permute-start | bytes 1327112 | tf_op jit(solution)/shard_map/ppermute | solution.py:477
  102.8 3.2 %collective-permute-start.28 = (bf16[64,3328]{1,0:T(8,128)(2,1)S(1)}, bf16[64,3328]{1,0:T(8,128)(2,1)S(1)}, u32[]{:S(2)}, u32[]{:S(2)}) collective-permute-start(bf16[64,3328]{1,0:T(8,128)(2,1)S(1)} %get-tuple-element.83), channel_id=1, source_target_pairs={{0,96},{8,104},{16,112},{24,120},{32,0},{40,8},{48,16},{56,24},{64... | collective-permute-start | bytes 1277960 | tf_op jit(solution)/shard_map/ppermute | solution.py:483
  106.1 5.4 %shard_map.135 = (f32[64,3328]{1,0:T(8,128)S(1)}, f32[64,3328]{1,0:T(8,128)S(1)}, bf16[64,3328]{1,0:T(8,128)(2,1)S(1)}, bf16[64,3328]{1,0:T(8,128)(2,1)S(1)}, f3...) custom-call(bf16[4,4,32,1024]{3,2,1,0:T(8,128)(2,1)S(1)} %get-tuple-, ...), custom_call_target="tpu_custom_call" | custom-call | tf_op jit(solution)/shard_map/pallas_call | solution.py:418
  114.6 2.1 %collective-permute-start.23 = (bf16[128,3456]{1,0:T(8,128)(2,1)S(1)}, bf16[128,3456]{1,0:T(8,128)(2,1)S(1)}, u32[]{:S(2)}, u32[]{:S(2)}) collective-permute-start(bf16[128,3456]{1,0:T(8,128)(2,1)S(1)} %get-tuple-element.72), channel_id=1, source_target_pairs={{0,24},{8,0},{16,8},{24,16},{32,56},{40,32},{48,40},{56,48},{64,88... | collective-permute-start | bytes 2654216 | tf_op jit(solution)/shard_map/ppermute | solution.py:477
  117.0 3.2 %collective-permute-start.30 = (bf16[128,3328]{1,0:T(8,128)(2,1)S(1)}, bf16[128,3328]{1,0:T(8,128)(2,1)S(1)}, u32[]{:S(2)}, u32[]{:S(2)}) collective-permute-start(bf16[128,3328]{1,0:T(8,128)(2,1)S(1)} %get-tuple-element.85), channel_id=1, source_target_pairs={{0,96},{8,104},{16,112},{24,120},{32,0},{40,8},{48,16},{56,24},{64... | collective-permute-start | bytes 2555912 | tf_op jit(solution)/shard_map/ppermute | solution.py:483
  120.2 15.6 %collective-permute-done.22.before_ref = bf16[128,3456]{1,0:T(8,128)(2,1)S(1)} collective-permute-done((bf16[128,3456]{1,0:T(8,128)(2,1)S(1)}, bf16[128,3456]{1,0:T(8,128)(2,1)S(1)}, u32[]{:S(2)}, u32[]{:S(2)}) %collective-permute-start.22) | collective-permute-done | bytes 884768 | tf_op jit(solution)/shard_map/ppermute | solution.py:477
  136.9 2.9 %collective-permute-start.26 = (bf16[32,3456]{1,0:T(8,128)(2,1)S(1)}, bf16[32,3456]{1,0:T(8,128)(2,1)S(1)}, u32[]{:S(2)}, u32[]{:S(2)}) collective-permute-start(bf16[32,3456]{1,0:T(8,128)(2,1)S(1)} %get-tuple-element.76), channel_id=1, source_target_pairs={{0,96},{8,104},{16,112},{24,120},{32,0},{40,8},{48,16},{56,24},{64... | collective-permute-start | bytes 663560 | tf_op jit(solution)/shard_map/ppermute | solution.py:483
  139.8 3.4 %collective-permute-done.30.after_ref = bf16[128,3328]{1,0:T(8,128)(2,1)S(1)} collective-permute-done((bf16[128,3328]{1,0:T(8,128)(2,1)S(1)}, bf16[128,3328]{1,0:T(8,128)(2,1)S(1)}, u32[]{:S(2)}, u32[]{:S(2)}) %collective-permute-start.30) | collective-permute-done | bytes 852000 | tf_op jit(solution)/shard_map/ppermute | solution.py:483
  146.3 2.8 %collective-permute-start.33 = (bf16[32,3328]{1,0:T(8,128)(2,1)S(1)}, bf16[32,3328]{1,0:T(8,128)(2,1)S(1)}, u32[]{:S(2)}, u32[]{:S(2)}) collective-permute-start(bf16[32,3328]{1,0:T(8,128)(2,1)S(1)} %get-tuple-element.89), channel_id=1, source_target_pairs={{0,24},{8,0},{16,8},{24,16},{32,56},{40,32},{48,40},{56,48},{64,88... | collective-permute-start | bytes 638984 | tf_op jit(solution)/shard_map/ppermute | solution.py:477
  (98 shorter events, 50.6 us)
Async XLA Ops:
  2.4 16.7 %all-to-all-start = ((bf16[64,16,128]{2,1,0:T(8,128)(2,1)}), bf16[64,16,128]{2,1,0:T(8,128)(2,1)S(1)}, u32[]{:S(2)}, u32[]{:S(2)}) async-start(bf16[64,16,128]{2,1,0:T(8,128)(2,1)} %get-tuple-element.50), calls=%async_computation | async-start | bytes 524288 | tf_op jit(solution)/shard_map/all_to_all | solution.py:544
  41.6 7.9 %collective-permute-start.4 = (bf16[32,1024]{1,0:T(8,128)(2,1)S(1)}, bf16[32,1024]{1,0:T(8,128)(2,1)S(1)}, u32[]{:S(2)}, u32[]{:S(2)}) collective-permute-start(bf16[32,1024]{1,0:T(8,128)(2,1)S(1)} %get-tuple-element.54.refs_7_), channel_id=1, source_target_pairs={{0,64},{8,72},{16,80},{24,88},{32,96},{40,104},{48,112},{56,120},{... | collective-permute-start | bytes 196616 | tf_op jit(solution)/shard_map/ppermute | solution.py:483
  52.4 11.2 %collective-permute-start.8 = (bf16[4,32,1024]{2,1,0:T(8,128)(2,1)S(1)}, bf16[4,32,1024]{2,1,0:T(8,128)(2,1)S(1)}, u32[]{:S(2)}, u32[]{:S(2)}) collective-permute-start(bf16[4,32,1024]{2,1,0:T(8,128)(2,1)S(1)} %get-tuple-element.55.refs_3_), channel_id=1, source_target_pairs={{0,32},{8,40},{16,48},{24,56},{32,64},{40,72},{48,80},{56,88},{64,... | collective-permute-start | bytes 786440 | tf_op jit(solution)/shard_map/ppermute | solution.py:483
  53.1 12.9 %collective-permute-start.7 = (bf16[4,32,1024]{2,1,0:T(8,128)(2,1)S(1)}, bf16[4,32,1024]{2,1,0:T(8,128)(2,1)S(1)}, u32[]{:S(2)}, u32[]{:S(2)}) collective-permute-start(bf16[4,32,1024]{2,1,0:T(8,128)(2,1)S(1)} %get-tuple-element.55.refs_3_), channel_id=1, source_target_pairs={{0,64},{8,72},{16,80},{24,88},{32,96},{40,104},{48,112},{56,120},{... | collective-permute-start | bytes 786440 | tf_op jit(solution)/shard_map/ppermute | solution.py:483
  54.8 11.1 %collective-permute-start.6 = (bf16[4,32,1024]{2,1,0:T(8,128)(2,1)S(1)}, bf16[4,32,1024]{2,1,0:T(8,128)(2,1)S(1)}, u32[]{:S(2)}, u32[]{:S(2)}) collective-permute-start(bf16[4,32,1024]{2,1,0:T(8,128)(2,1)S(1)} %get-tuple-element.55.refs_3_), channel_id=1, source_target_pairs={{0,96},{8,104},{16,112},{24,120},{32,0},{40,8},{48,16},{56,24},{64... | collective-permute-start | bytes 786440 | tf_op jit(solution)/shard_map/ppermute | solution.py:483
  57.3 8.6 %collective-permute-start.11 = (bf16[4,32,1024]{2,1,0:T(8,128)(2,1)S(1)}, bf16[4,32,1024]{2,1,0:T(8,128)(2,1)S(1)}, u32[]{:S(2)}, u32[]{:S(2)}) collective-permute-start(bf16[4,32,1024]{2,1,0:T(8,128)(2,1)S(1)} %get-tuple-element.56.refs_7_), channel_id=1, source_target_pairs={{0,8},{8,16},{16,24},{24,0},{32,40},{40,48},{48,56},{56,32},{64,72... | collective-permute-start | bytes 786440 | tf_op jit(solution)/shard_map/ppermute | solution.py:477
  58.7 10.0 %collective-permute-start.10 = (bf16[4,32,1024]{2,1,0:T(8,128)(2,1)S(1)}, bf16[4,32,1024]{2,1,0:T(8,128)(2,1)S(1)}, u32[]{:S(2)}, u32[]{:S(2)}) collective-permute-start(bf16[4,32,1024]{2,1,0:T(8,128)(2,1)S(1)} %get-tuple-element.56.refs_7_), channel_id=1, source_target_pairs={{0,16},{8,24},{16,0},{24,8},{32,48},{40,56},{48,32},{56,40},{64,80... | collective-permute-start | bytes 786440 | tf_op jit(solution)/shard_map/ppermute | solution.py:477
  73.5 7.9 %collective-permute-start.13 = (bf16[64,1024]{1,0:T(8,128)(2,1)S(1)}, bf16[64,1024]{1,0:T(8,128)(2,1)S(1)}, u32[]{:S(2)}, u32[]{:S(2)}) collective-permute-start(bf16[64,1024]{1,0:T(8,128)(2,1)S(1)} %get-tuple-element.58), channel_id=1, source_target_pairs={{0,4},{1,5},{2,6},{3,7},{4,0},{5,1},{6,2},{7,3},{8,12},{9,13},{10,... | collective-permute-start | bytes 393224 | tf_op jit(solution)/shard_map/ppermute | solution.py:489
  76.6 7.1 %collective-permute-start.14 = (bf16[64,1024]{1,0:T(8,128)(2,1)S(1)}, bf16[64,1024]{1,0:T(8,128)(2,1)S(1)}, u32[]{:S(2)}, u32[]{:S(2)}) collective-permute-start(bf16[64,1024]{1,0:T(8,128)(2,1)S(1)} %get-tuple-element.59), channel_id=1, source_target_pairs={{0,2},{1,3},{2,4},{3,5},{4,6},{5,7},{6,0},{7,1},{8,10},{9,11},{10,... | collective-permute-start | bytes 393224 | tf_op jit(solution)/shard_map/ppermute | solution.py:489
  83.8 7.5 %collective-permute-start.18 = (bf16[64,1024]{1,0:T(8,128)(2,1)S(1)}, bf16[64,1024]{1,0:T(8,128)(2,1)S(1)}, u32[]{:S(2)}, u32[]{:S(2)}) collective-permute-start(bf16[64,1024]{1,0:T(8,128)(2,1)S(1)} %shard_map.132.own_ref), channel_id=1, source_target_pairs={{0,2},{1,3},{2,4},{3,5},{4,6},{5,7},{6,0},{7,1},{8,10},{9,11},{10,... | collective-permute-start | bytes 393224 | tf_op jit(solution)/shard_map/ppermute | solution.py:489
  85.2 8.3 %collective-permute-start.17 = (bf16[64,1024]{1,0:T(8,128)(2,1)S(1)}, bf16[64,1024]{1,0:T(8,128)(2,1)S(1)}, u32[]{:S(2)}, u32[]{:S(2)}) collective-permute-start(bf16[64,1024]{1,0:T(8,128)(2,1)S(1)} %shard_map.132.own_ref), channel_id=1, source_target_pairs={{0,4},{1,5},{2,6},{3,7},{4,0},{5,1},{6,2},{7,3},{8,12},{9,13},{10,... | collective-permute-start | bytes 393224 | tf_op jit(solution)/shard_map/ppermute | solution.py:489
  99.1 14.1 %collective-permute-start.20 = (bf16[64,3456]{1,0:T(8,128)(2,1)S(1)}, bf16[64,3456]{1,0:T(8,128)(2,1)S(1)}, u32[]{:S(2)}, u32[]{:S(2)}) collective-permute-start(bf16[64,3456]{1,0:T(8,128)(2,1)S(1)} %get-tuple-element.69), channel_id=1, source_target_pairs={{0,8},{8,16},{16,24},{24,0},{32,40},{40,48},{48,56},{56,32},{64,72... | collective-permute-start | bytes 1327112 | tf_op jit(solution)/shard_map/ppermute | solution.py:477
  100.2 13.0 %collective-permute-start.21 = (bf16[64,3456]{1,0:T(8,128)(2,1)S(1)}, bf16[64,3456]{1,0:T(8,128)(2,1)S(1)}, u32[]{:S(2)}, u32[]{:S(2)}) collective-permute-start(bf16[64,3456]{1,0:T(8,128)(2,1)S(1)} %get-tuple-element.70), channel_id=1, source_target_pairs={{0,24},{8,0},{16,8},{24,16},{32,56},{40,32},{48,40},{56,48},{64,88... | collective-permute-start | bytes 1327112 | tf_op jit(solution)/shard_map/ppermute | solution.py:477
  102.8 13.9 %collective-permute-start.27 = (bf16[64,3328]{1,0:T(8,128)(2,1)S(1)}, bf16[64,3328]{1,0:T(8,128)(2,1)S(1)}, u32[]{:S(2)}, u32[]{:S(2)}) collective-permute-start(bf16[64,3328]{1,0:T(8,128)(2,1)S(1)} %get-tuple-element.82), channel_id=1, source_target_pairs={{0,32},{8,40},{16,48},{24,56},{32,64},{40,72},{48,80},{56,88},{64,... | collective-permute-start | bytes 1277960 | tf_op jit(solution)/shard_map/ppermute | solution.py:483
  102.8 13.9 %collective-permute-start.28 = (bf16[64,3328]{1,0:T(8,128)(2,1)S(1)}, bf16[64,3328]{1,0:T(8,128)(2,1)S(1)}, u32[]{:S(2)}, u32[]{:S(2)}) collective-permute-start(bf16[64,3328]{1,0:T(8,128)(2,1)S(1)} %get-tuple-element.83), channel_id=1, source_target_pairs={{0,96},{8,104},{16,112},{24,120},{32,0},{40,8},{48,16},{56,24},{64... | collective-permute-start | bytes 1277960 | tf_op jit(solution)/shard_map/ppermute | solution.py:483
  113.4 22.5 %collective-permute-start.22 = (bf16[128,3456]{1,0:T(8,128)(2,1)S(1)}, bf16[128,3456]{1,0:T(8,128)(2,1)S(1)}, u32[]{:S(2)}, u32[]{:S(2)}) collective-permute-start(bf16[128,3456]{1,0:T(8,128)(2,1)S(1)} %get-tuple-element.71), channel_id=1, source_target_pairs={{0,8},{8,16},{16,24},{24,0},{32,40},{40,48},{48,56},{56,32},{64,72... | collective-permute-start | bytes 2654216 | tf_op jit(solution)/shard_map/ppermute | solution.py:477
  114.6 21.3 %collective-permute-start.23 = (bf16[128,3456]{1,0:T(8,128)(2,1)S(1)}, bf16[128,3456]{1,0:T(8,128)(2,1)S(1)}, u32[]{:S(2)}, u32[]{:S(2)}) collective-permute-start(bf16[128,3456]{1,0:T(8,128)(2,1)S(1)} %get-tuple-element.72), channel_id=1, source_target_pairs={{0,24},{8,0},{16,8},{24,16},{32,56},{40,32},{48,40},{56,48},{64,88... | collective-permute-start | bytes 2654216 | tf_op jit(solution)/shard_map/ppermute | solution.py:477
  116.9 22.9 %collective-permute-start.29 = (bf16[128,3328]{1,0:T(8,128)(2,1)S(1)}, bf16[128,3328]{1,0:T(8,128)(2,1)S(1)}, u32[]{:S(2)}, u32[]{:S(2)}) collective-permute-start(bf16[128,3328]{1,0:T(8,128)(2,1)S(1)} %get-tuple-element.84), channel_id=1, source_target_pairs={{0,32},{8,40},{16,48},{24,56},{32,64},{40,72},{48,80},{56,88},{64,... | collective-permute-start | bytes 2555912 | tf_op jit(solution)/shard_map/ppermute | solution.py:483
  117.0 26.2 %collective-permute-start.30 = (bf16[128,3328]{1,0:T(8,128)(2,1)S(1)}, bf16[128,3328]{1,0:T(8,128)(2,1)S(1)}, u32[]{:S(2)}, u32[]{:S(2)}) collective-permute-start(bf16[128,3328]{1,0:T(8,128)(2,1)S(1)} %get-tuple-element.85), channel_id=1, source_target_pairs={{0,96},{8,104},{16,112},{24,120},{32,0},{40,8},{48,16},{56,24},{64... | collective-permute-start | bytes 2555912 | tf_op jit(solution)/shard_map/ppermute | solution.py:483
  136.4 10.0 %collective-permute-start.24 = (bf16[32,3456]{1,0:T(8,128)(2,1)S(1)}, bf16[32,3456]{1,0:T(8,128)(2,1)S(1)}, u32[]{:S(2)}, u32[]{:S(2)}) collective-permute-start(bf16[32,3456]{1,0:T(8,128)(2,1)S(1)} %get-tuple-element.74), channel_id=1, source_target_pairs={{0,64},{8,72},{16,80},{24,88},{32,96},{40,104},{48,112},{56,120},{... | collective-permute-start | bytes 663560 | tf_op jit(solution)/shard_map/ppermute | solution.py:483
  136.5 12.6 %collective-permute-start.25 = (bf16[32,3456]{1,0:T(8,128)(2,1)S(1)}, bf16[32,3456]{1,0:T(8,128)(2,1)S(1)}, u32[]{:S(2)}, u32[]{:S(2)}) collective-permute-start(bf16[32,3456]{1,0:T(8,128)(2,1)S(1)} %get-tuple-element.75), channel_id=1, source_target_pairs={{0,32},{8,40},{16,48},{24,56},{32,64},{40,72},{48,80},{56,88},{64,... | collective-permute-start | bytes 663560 | tf_op jit(solution)/shard_map/ppermute | solution.py:483
  136.9 12.2 %collective-permute-start.26 = (bf16[32,3456]{1,0:T(8,128)(2,1)S(1)}, bf16[32,3456]{1,0:T(8,128)(2,1)S(1)}, u32[]{:S(2)}, u32[]{:S(2)}) collective-permute-start(bf16[32,3456]{1,0:T(8,128)(2,1)S(1)} %get-tuple-element.76), channel_id=1, source_target_pairs={{0,96},{8,104},{16,112},{24,120},{32,0},{40,8},{48,16},{56,24},{64... | collective-permute-start | bytes 663560 | tf_op jit(solution)/shard_map/ppermute | solution.py:483
  143.7 7.5 %collective-permute-start.31 = (bf16[32,3328]{1,0:T(8,128)(2,1)S(1)}, bf16[32,3328]{1,0:T(8,128)(2,1)S(1)}, u32[]{:S(2)}, u32[]{:S(2)}) collective-permute-start(bf16[32,3328]{1,0:T(8,128)(2,1)S(1)} %get-tuple-element.87), channel_id=1, source_target_pairs={{0,16},{8,24},{16,0},{24,8},{32,48},{40,56},{48,32},{56,40},{64,80... | collective-permute-start | bytes 638984 | tf_op jit(solution)/shard_map/ppermute | solution.py:477
  143.8 9.4 %collective-permute-start.32 = (bf16[32,3328]{1,0:T(8,128)(2,1)S(1)}, bf16[32,3328]{1,0:T(8,128)(2,1)S(1)}, u32[]{:S(2)}, u32[]{:S(2)}) collective-permute-start(bf16[32,3328]{1,0:T(8,128)(2,1)S(1)} %get-tuple-element.88), channel_id=1, source_target_pairs={{0,8},{8,16},{16,24},{24,0},{32,40},{40,48},{48,56},{56,32},{64,72... | collective-permute-start | bytes 638984 | tf_op jit(solution)/shard_map/ppermute | solution.py:477
  (24 other events, 287.6 us)

commit v5 on v4

--- a/solution.py
+++ b/solution.py
@@ -19,7 +19,7 @@
 SLOTS = N_ATTN * CAP
 SIDE = 4
 WIDTH = 1024
-GROUP = 4
+GROUP = 8
 LISTED = 128
 SHORT = MAXP // 2
 EPS = 1e-05
@@ -359,21 +359,22 @@
     )(*blocks)
 
 
+def scale(block, gain_ref):
+    widened = block.astype(jnp.float32)
+    totals = jnp.sum(widened * widened, axis=1, keepdims=True)
+    scaled = (widened * gain_ref[...].astype(jnp.float32)).astype(jnp.bfloat16)
+    return scaled, jnp.broadcast_to(totals, (block.shape[0], HD))
+
+
 def assemble_body(this_ref, other_ref, gain_ref, residual_ref, rows_ref, squares_ref):
     core = place()[3]
-    gain = gain_ref[...].astype(jnp.float32)
+    half = SIDE // 2
     for which, half_ref in ((core, this_ref), (1 - core, other_ref)):
         size = half_ref.shape[0]
         residual_ref[pl.ds(pl.multiple_of(which * size, size), size), :] = half_ref[...]
-        widened = half_ref[...].astype(jnp.float32)
-        totals = jnp.sum(widened * widened, axis=1, keepdims=True)
-        first = which * (SIDE // 2)
-        rows_ref[pl.ds(first, SIDE // 2)] = (
-            (widened * gain).astype(jnp.bfloat16).reshape(SIDE // 2, SIDE, ROWS, WIDTH)
-        )
-        squares_ref[pl.ds(first, SIDE // 2)] = jnp.broadcast_to(totals, (size, HD)).reshape(
-            SIDE // 2, SIDE, ROWS, HD
-        )
+        scaled, totals = scale(half_ref[...], gain_ref)
+        rows_ref[pl.ds(which * half, half)] = scaled.reshape(half, SIDE, ROWS, WIDTH)
+        squares_ref[pl.ds(which * half, half)] = totals.reshape(half, SIDE, ROWS, HD)
 
 
 def assemble(this_half, other_half, gain):
@@ -390,87 +391,104 @@
     )(this_half, other_half, gain)
 
 
-def project_body(outs, rows_ref, squares_ref, *refs):
-    size = 2 * ROWS
-    for line in (1, 0):
-        weight_ref = refs[line]
-        here = place()[line]
-        targets, at = [], []
-        for k, groups in enumerate(outs):
-            out = refs[2 + line * len(outs) + k]
-            for first, (step, half) in enumerate(groups):
-                targets.append((out, first * size))
-                there = (here + step) % SIDE
-                for other in (2 * half, 2 * half + 1):
-                    at.append((other, there) if line else (there, other))
-        lhs = jnp.concatenate([rows_ref[i, j] for i, j in at], axis=0)
-        columns = weight_ref.shape[1]
-        product = jnp.dot(lhs, weight_ref[...], preferred_element_type=jnp.float32)
-        for k, (out, first) in enumerate(targets):
-            out[first : first + size, :columns] = product[size * k : size * (k + 1)].astype(out.dtype)
-            if line:
-                piece = jnp.concatenate([squares_ref[i, j] for i, j in at[2 * k : 2 * k + 2]], axis=0)
-                out[first : first + size, columns:] = piece.astype(out.dtype)
-
-
-def project(outs, rows, squares, weights, dtypes):
-    columns = [weights[0].shape[1], weights[1].shape[1] + HD]
+CUTS = (0, 1664, 3328)
+
+
+def part_columns(line, part):
+    return CUTS[part + 1] - CUTS[part] + (HD if line and part else 0)
+
+
+def project_steps(steps, parts, block_of, up_ref, gate_ref, refs):
+    size = SIDE * ROWS
+    refs = iter(refs)
+    for line, weight_ref in ((1, gate_ref), (0, up_ref)):
+        here, core = place()[line], place()[3]
+        blocks = []
+        for step in steps:
+            there = (here + jnp.where(core == 0, SIDE - step, step)) % SIDE
+            for other in range(SIDE):
+                blocks.append(block_of(other, there) if line else block_of(there, other))
+        lhs = jnp.concatenate([rows for rows, _ in blocks], axis=0)
+        for part in parts:
+            width = CUTS[part + 1] - CUTS[part]
+            product = jnp.dot(
+                lhs, weight_ref[:, CUTS[part] : CUTS[part + 1]], preferred_element_type=jnp.float32
+            )
+            for k in range(len(steps)):
+                out = next(refs)
+                out[:, :width] = product[size * k : size * (k + 1)].astype(out.dtype)
+                if line and part:
+                    totals = [t for _, t in blocks[SIDE * k : SIDE * (k + 1)]]
+                    out[:, width:] = jnp.concatenate(totals, axis=0).astype(out.dtype)
+
+
+def first_body(steps, parts, this_ref, other_ref, gain_ref, up_ref, gate_ref, *refs):
+    core = place()[3]
+    this = this_ref.reshape(SIDE // 2, SIDE, ROWS, WIDTH)
+    other = other_ref.reshape(SIDE // 2, SIDE, ROWS, WIDTH)
+
+    def block_of(i, j):
+        block = jnp.where(i // 2 == core, this[i % 2, j], other[i % 2, j])
+        return scale(block, gain_ref)
+
+    project_steps(steps, parts, block_of, up_ref, gate_ref, refs)
+
+
+def rest_body(steps, parts, rows_ref, squares_ref, up_ref, gate_ref, *refs):
+    project_steps(steps, parts, lambda i, j: (rows_ref[i, j], squares_ref[i, j]), up_ref, gate_ref, refs)
+
+
+def project(body, steps, parts, dtype, weights, *arrays):
+    keys = [(line, part, step) for line in (1, 0) for part in parts for step in steps]
     results = pl.pallas_call(
-        functools.partial(project_body, outs),
+        functools.partial(body, steps, parts),
         out_shape=[
-            jax.ShapeDtypeStruct((2 * ROWS * len(groups), n), dtype)
-            for n in columns
-            for groups, dtype in zip(outs, dtypes)
+            jax.ShapeDtypeStruct((SIDE * ROWS, part_columns(line, part)), dtype) for line, part, _ in keys
         ],
-        in_specs=[VMEM] * 4,
-        out_specs=[VMEM] * (2 * len(outs)),
+        in_specs=[VMEM] * (len(arrays) + 2),
+        out_specs=[VMEM] * len(keys),
         compiler_params=params(24),
-    )(rows, squares, *weights)
-    return results[: len(outs)], results[len(outs) :]
-
-
-def relay_body(*refs):
-    size = 2 * ROWS
-    for k in range(2):
-        part_ref, near_ref, came_ref, out = refs[k], refs[2 + k], refs[4 + k], refs[6 + k]
-        out[:size] = (part_ref[...] + came_ref[...].astype(jnp.float32)).astype(out.dtype)
-        out[size:] = near_ref[...]
-
-
-def relay(parts, nears, came):
-    shape = (4 * ROWS, parts[0].shape[1])
+    )(*arrays, *weights)
+    return dict(zip(keys, results))
+
+
+def relay_body(own_ref, came_ref, out_ref):
+    out_ref[...] = (own_ref[...] + came_ref[...].astype(jnp.float32)).astype(jnp.bfloat16)
+
+
+def relay(own, came):
     return pl.pallas_call(
         relay_body,
-        out_shape=[jax.ShapeDtypeStruct(shape, jnp.bfloat16)] * 2,
-        in_specs=[VMEM] * 6,
-        out_specs=[VMEM] * 2,
-        compiler_params=params(),
-    )(*parts, *nears, *came)
-
-
-def merge_body(line, own_ref, before_ref, after_ref, *refs):
+        out_shape=jax.ShapeDtypeStruct(own.shape, jnp.bfloat16),
+        in_specs=[VMEM] * 2,
+        out_specs=VMEM,
+        compiler_params=params(),
+    )(own, came)
+
+
+def merge_body(line, first_ref, second_ref, first_came, second_came, *refs):
     outs, sums_ref = refs[:4], refs[4]
-    size = 2 * ROWS
-    for k in range(2):
-        total = own_ref[size * k : size * (k + 1)]
-        for ref, first in ((before_ref, size * k), (after_ref, size * (1 - k))):
-            total = total + ref[first : first + size].astype(jnp.float32)
-        sums_ref[2 * k : 2 * k + 2] = total.reshape(2, ROWS, sums_ref.shape[2])
+    start = 0
+    for own_ref, came_ref in ((first_ref, first_came), (second_ref, second_came)):
+        total = own_ref[...] + came_ref[...].astype(jnp.float32)
+        width = total.shape[1]
+        sums_ref[:, :, start : start + width] = total.reshape(SIDE, ROWS, width)
+        start += width
     for at, out in zip(relative(place()[1 - line]), outs):
         out[...] = sums_ref[at].astype(out.dtype)
 
 
-def merge(line, own, before, after):
-    columns = own.shape[1]
+def merge(line, own, came):
+    columns = sum(a.shape[1] for a in own)
     return pl.pallas_call(
         functools.partial(merge_body, line),
         out_shape=[jax.ShapeDtypeStruct((ROWS, columns), jnp.bfloat16)] * 3
         + [jax.ShapeDtypeStruct((ROWS, columns), jnp.float32)],
-        in_specs=[VMEM] * 3,
+        in_specs=[VMEM] * 4,
         out_specs=[VMEM] * 4,
         scratch_shapes=[pltpu.VMEM((SIDE, ROWS, columns), jnp.float32)],
         compiler_params=params(),
-    )(own, before, after)
+    )(*own, *came)
 
 
 def along_z(x, shift):
@@ -495,29 +513,42 @@
     return lax.ppermute(x, "ffn", [(f, f ^ 1) for f in range(8)])
 
 
-LINES = (along_y, along_z)
-
-
-def scatter(rows, squares, weights):
-    far = project((((2, 0),), ((2, 1),)), rows, squares, weights, [jnp.bfloat16] * 2)
-    came = {line: (LINES[line](far[line][0], 1), LINES[line](far[line][1], 3)) for line in (1, 0)}
-    outs = (((1, 0),), ((3, 1),), ((1, 1),), ((3, 0),), ((0, 0), (0, 1)))
-    dtypes = [jnp.float32] * 2 + [jnp.bfloat16] * 2 + [jnp.float32]
-    rest = project(outs, rows, squares, weights, dtypes)
-    parts = {}
-    for line in (1, 0):
-        up, down = relay(rest[line][:2], rest[line][2:4], came[line])
-        parts[line] = (rest[line][4], LINES[line](up, 1), LINES[line](down, 3))
+def along_ring(line, x):
+    pairs = []
+    for y in range(SIDE):
+        for z in range(SIDE):
+            for ffn in range(8):
+                way = 1 - 2 * (ffn % 2)
+                at = [y, z]
+                at[line] = (at[line] + way) % SIDE
+                pairs.append(((y * SIDE + z) * 8 + ffn, (at[0] * SIDE + at[1]) * 8 + ffn))
+    return lax.ppermute(x, ("attn", "ffn"), pairs)
+
+
+def scatter(halves, gain, weights):
+    came = {}
+    for part in range(2):
+        first = project(first_body, (1,), (part,), jnp.bfloat16, weights, *halves, gain)
+        for line in (1, 0):
+            came[line, part] = along_ring(line, first[line, part, 1])
+    residual, rows, squares = assemble(*halves, gain)
+    rest = project(rest_body, (2,), (0, 1), jnp.float32, weights, rows, squares)
+    rest |= project(rest_body, (3, 0), (0, 1), jnp.float32, weights, rows, squares)
+    for step in (2, 3):
+        for part in range(2):
+            for line in (1, 0):
+                came[line, part] = along_ring(line, relay(rest[line, part, step], came[line, part]))
     sums = []
-    for line in (1, 0):
-        cross = LINES[1 - line]
-        one, two, three, mine = merge(line, *parts[line])
+    for line, cross in ((1, along_y), (0, along_z)):
+        one, two, three, mine = merge(
+            line, [rest[line, part, 0] for part in range(2)], [came[line, part] for part in range(2)]
+        )
         sums.append((mine, cross(two, 2), cross(one, 1), cross(three, 3)))
-    return sums
+    return residual, sums
 
 
 def line_of(shift, x):
-    two, one, three = shift(x, 2), shift(x, 3), shift(x, 1)
+    one, three, two = shift(x, 3), shift(x, 1), shift(x, 2)
     return one, two, three, x
 
 
@@ -556,17 +587,16 @@
     one, two, three, own = pair(kept, came)
     pieces = (along_x(two, 2), along_x(one, 1), along_x(three, 3))
     mine_rows = settle(stream_rows, own, pieces)
-    others = (along_x(mine_rows, 3), along_x(mine_rows, 2), along_x(mine_rows, 1))
-    this_half = lay(others + (mine_rows,)).reshape(half, WIDTH)
+    first, third, second = along_x(mine_rows, 3), along_x(mine_rows, 1), along_x(mine_rows, 2)
+    this_half = lay((first, second, third, mine_rows)).reshape(half, WIDTH)
     other_half = to_sibling(this_half)
-    residual, rows, squares = assemble(this_half, other_half, norm_gain.reshape(1, WIDTH))
-
-    gate_parts, up_parts = scatter(rows, squares, (w_up, w_gate))
-    gate = sum(p.astype(f32) for p in gate_parts)
+
+    residual, sums = scatter((this_half, other_half), norm_gain.reshape(1, WIDTH), (w_up, w_gate))
+    gate, up = (sum(p.astype(f32) for p in parts) for parts in sums)
     columns = w_gate.shape[1]
     scaling = lax.rsqrt(gate[:, columns : columns + 1] / D + EPS)
     gate = gate[:, :columns] * scaling
-    up = sum(p.astype(f32) for p in up_parts) * scaling
+    up = up * scaling
     hidden = (jax.nn.silu(gate) * up).astype(jnp.bfloat16)
     return (residual, hidden)
 

time: 155 us -> 155 us (level)
  waiting for transfers between devices: 47.8 us -> 45.1 us
  blocking collectives: 15.8 us -> 17.8 us
    ppermute x0 -> x12, waiting for transfers between devices: none -> 20.3 us  [along_ring(): return lax.ppermute(x, ('attn', 'ffn'), pairs)]
    ppermute x13 -> x9, waiting for transfers between devices: 28.1 us -> 10.4 us  [along_z(): lax.ppermute(x, 'attn', [(y * SIDE + z, y * SIDE + (z + shift) % SIDE) fo...]
    ppermute x0 -> x12, starting transfers between devices: none -> 6.01 us  [along_ring(): return lax.ppermute(x, ('attn', 'ffn'), pairs)]
    ppermute x13 -> x9, waiting for transfers between devices: 7.42 us -> 2.1 us  [along_y(): lax.ppermute(x, 'attn', [(y * SIDE + z, (y + shift) % SIDE * SIDE + z) fo...]
    ppermute x13 -> x9, starting transfers between devices: 18.9 us -> 15 us  [along_y(): lax.ppermute(x, 'attn', [(y * SIDE + z, (y + shift) % SIDE * SIDE + z) fo...]
    all_to_all x1, blocking collectives: 15.8 us -> 17.8 us  [on_device(): lax.all_to_all(blended, 'attn', split_axis=0, concat_axis=0, tiled=True)]
    pallas_call x4 -> x12, Pallas kernels: 7.76 us -> 8.9 us  [the longest x4 8.29 us: project(): pl.pallas_call(functools.partial(body, steps, parts), out_shape=[jax.Shap...]
    ppermute x13 -> x9, starting transfers between devices: 21.3 us -> 20.2 us  [along_z(): lax.ppermute(x, 'attn', [(y * SIDE + z, y * SIDE + (z + shift) % SIDE) fo...]
  transfers between devices with their start and end apart: 35 -> 39, of which waited for: 20 -> 21; matrix products, arithmetic and copies ran while one was open for 0% -> 0% of each run, Pallas kernels for 7% -> 9%
where the time goes in v5:
time: 155 us
  starting transfers between devices  60.7 us (39%)
  waiting for transfers between devices  45.1 us (29%)
  Pallas kernels  24.4 us (16%)
  blocking collectives  17.8 us (11%)
  local copies, waits for them, and re-layouts  5.35 us (3%)
    ppermute x12, waiting for transfers between devices, along_ring(): return lax.ppermute(x, ('attn', 'ffn'), pairs)  20.3 us
    ppermute x9, starting transfers between devices, along_z(): lax.ppermute(x, 'attn', [(y * SIDE + z, y * SIDE + (z + shift) % SIDE) fo...  20.2 us
    all_to_all x1, blocking collectives, on_device(): lax.all_to_all(blended, 'attn', split_axis=0, concat_axis=0, tiled=True)  17.8 us
    ppermute x9, starting transfers between devices, along_y(): lax.ppermute(x, 'attn', [(y * SIDE + z, (y + shift) % SIDE * SIDE + z) fo...  15 us
    ppermute x6, starting transfers between devices, along_x(): lax.ppermute(x, 'ffn', [(chip * 2 + core, (chip + shift) % SIDE * 2 + cor...  11 us
    ppermute x9, waiting for transfers between devices, along_z(): lax.ppermute(x, 'attn', [(y * SIDE + z, y * SIDE + (z + shift) % SIDE) fo...  10.4 us
    ppermute x6, waiting for transfers between devices, along_x(): lax.ppermute(x, 'ffn', [(chip * 2 + core, (chip + shift) % SIDE * 2 + cor...  8.79 us
    pallas_call x4, Pallas kernels, project(): pl.pallas_call(functools.partial(body, steps, parts), out_shape=[jax.Shap...  8.29 us
  transfers between devices with their start and end apart: 39, of which 21 were waited for; matrix products, arithmetic and copies ran while one was open for 0% of the time, Pallas kernels for 9%

profile of v5, /device:TPU:0, one launch (start us, length us, event | category | flops | bytes accessed | tf_op | source)
XLA Modules:
  0.0 155.5 jit_solution(9281370923014872060)
XLA Ops:
  2.4 8.1 %all-to-all-start = ((bf16[64,16,128]{2,1,0:T(8,128)(2,1)}), bf16[64,16,128]{2,1,0:T(8,128)(2,1)S(1)}, u32[]{:S(2)}, u32[]{:S(2)}) async-start(bf16[64,16,128]{2,1,0:T(8,128)(2,1)} %get-tuple-element.48), calls=%async_computation | async-start | bytes 524288 | tf_op jit(solution)/shard_map/all_to_all | solution.py:575
  15.2 2.9 %shard_map.123 = (s32[2,128]{1,0:T(2,128)S(1)}, s32[1,512]{1,0:T(1,128)S(1)}, s32[32,512]{1,0:T(8,128)S(1)}, bf16[256,16,128]{2,1,0:T(8,128)(2,1)S(1)}, bf16[256,16,128]{2,1,0:T(8,128)(2,1)S(1)}) custom-call(s32[1,512]{1,0:T(1,128)S(1)} %bitcast.21, s32[1,512]{1,0:T(1,128)S(1)} %bitcast.22, s32[32,512]{1,0:T(8,128)S(1)} %bitcast.19, ...), custom_call_target="tpu_custom_call" | custom-call | tf_op jit(solution)/shard_map/pallas_call | solution.py:135
  19.1 5.2 %shard_map.124 = bf16[64,16,128]{2,1,0:T(8,128)(2,1)S(1)} custom-call(s32[1,512]{1,0:T(1,128)S(1)} %get-tuple-element.45.lengths_vmem, s32[32,512]{1,0:T(8,128)S(1)} %get-tuple-element.46.table_vmem, s32[2,128]{1,0:T(2,128)S(1)} %get-tuple-element.47.list_ref, bf16[64,16,128]{2,1,0:T(8,128)(2,1)S(1)} %all-to-all-done.queries_ref, ...), custom_call_target="tpu_custom_call" | custom-call | tf_op jit(solution)/shard_map/pallas_call | solution.py:204
  24.2 17.8 %all_to_all.10.slots_ref = bf16[64,16,128]{2,1,0:T(8,128)(2,1)S(1)} all-to-all(bf16[64,16,128]{2,1,0:T(8,128)(2,1)S(1)} %shard_map.124), channel_id=1, replica_groups=mesh['attn'=16,'ffn'=8] {'attn'}, dimensions={0} | all-to-all | bytes 524288 | tf_op jit(solution)/shard_map/all_to_all | solution.py:577
  43.7 2.3 %collective-permute-start.4 = (bf16[32,1024]{1,0:T(8,128)(2,1)S(1)}, bf16[32,1024]{1,0:T(8,128)(2,1)S(1)}, u32[]{:S(2)}, u32[]{:S(2)}) collective-permute-start(bf16[32,1024]{1,0:T(8,128)(2,1)S(1)} %get-tuple-element.52.refs_7_), channel_id=1, source_target_pairs={{0,64},{8,72},{16,80},{24,88},{32,96},{40,104},{48,112},{56,120},{... | collective-permute-start | bytes 196616 | tf_op jit(solution)/shard_map/ppermute | solution.py:501
  56.9 2.5 %collective-permute-start.6 = (bf16[4,32,1024]{2,1,0:T(8,128)(2,1)S(1)}, bf16[4,32,1024]{2,1,0:T(8,128)(2,1)S(1)}, u32[]{:S(2)}, u32[]{:S(2)}) collective-permute-start(bf16[4,32,1024]{2,1,0:T(8,128)(2,1)S(1)} %get-tuple-element.53.refs_3_), channel_id=1, source_target_pairs={{0,96},{8,104},{16,112},{24,120},{32,0},{40,8},{48,16},{56,24},{64... | collective-permute-start | bytes 786440 | tf_op jit(solution)/shard_map/ppermute | solution.py:501
  60.8 2.8 %collective-permute-start.10 = (bf16[4,32,1024]{2,1,0:T(8,128)(2,1)S(1)}, bf16[4,32,1024]{2,1,0:T(8,128)(2,1)S(1)}, u32[]{:S(2)}, u32[]{:S(2)}) collective-permute-start(bf16[4,32,1024]{2,1,0:T(8,128)(2,1)S(1)} %get-tuple-element.54.refs_7_), channel_id=1, source_target_pairs={{0,16},{8,24},{16,0},{24,8},{32,48},{40,56},{48,32},{56,40},{64,80... | collective-permute-start | bytes 786440 | tf_op jit(solution)/shard_map/ppermute | solution.py:495
  65.7 2.4 %collective-permute-start.9 = (bf16[4,32,1024]{2,1,0:T(8,128)(2,1)S(1)}, bf16[4,32,1024]{2,1,0:T(8,128)(2,1)S(1)}, u32[]{:S(2)}, u32[]{:S(2)}) collective-permute-start(bf16[4,32,1024]{2,1,0:T(8,128)(2,1)S(1)} %get-tuple-element.54.refs_7_), channel_id=1, source_target_pairs={{0,24},{8,0},{16,8},{24,16},{32,56},{40,32},{48,40},{56,48},{64,88... | collective-permute-start | bytes 786440 | tf_op jit(solution)/shard_map/ppermute | solution.py:495
  68.1 2.7 %collective-permute-done.10.refs_5_ = bf16[4,32,1024]{2,1,0:T(8,128)(2,1)S(1)} collective-permute-done((bf16[4,32,1024]{2,1,0:T(8,128)(2,1)S(1)}, bf16[4,32,1024]{2,1,0:T(8,128)(2,1)S(1)}, u32[]{:S(2)}, u32[]{:S(2)}) %collective-permute-start.10) | collective-permute-done | bytes 262176 | tf_op jit(solution)/shard_map/ppermute | solution.py:495
  75.7 3.1 %collective-permute-start.13 = (bf16[64,1024]{1,0:T(8,128)(2,1)S(1)}, bf16[64,1024]{1,0:T(8,128)(2,1)S(1)}, u32[]{:S(2)}, u32[]{:S(2)}) collective-permute-start(bf16[64,1024]{1,0:T(8,128)(2,1)S(1)} %get-tuple-element.56), channel_id=1, source_target_pairs={{0,4},{1,5},{2,6},{3,7},{4,0},{5,1},{6,2},{7,3},{8,12},{9,13},{10,... | collective-permute-start | bytes 393224 | tf_op jit(solution)/shard_map/ppermute | solution.py:507
  79.4 2.6 %collective-permute-start.15 = (bf16[64,1024]{1,0:T(8,128)(2,1)S(1)}, bf16[64,1024]{1,0:T(8,128)(2,1)S(1)}, u32[]{:S(2)}, u32[]{:S(2)}) collective-permute-start(bf16[64,1024]{1,0:T(8,128)(2,1)S(1)} %get-tuple-element.58), channel_id=1, source_target_pairs={{0,6},{1,7},{2,0},{3,1},{4,2},{5,3},{6,4},{7,5},{8,14},{9,15},{10,... | collective-permute-start | bytes 393224 | tf_op jit(solution)/shard_map/ppermute | solution.py:507
  87.3 3.0 %collective-permute-start.17 = (bf16[64,1024]{1,0:T(8,128)(2,1)S(1)}, bf16[64,1024]{1,0:T(8,128)(2,1)S(1)}, u32[]{:S(2)}, u32[]{:S(2)}) collective-permute-start(bf16[64,1024]{1,0:T(8,128)(2,1)S(1)} %shard_map.132.own_ref), channel_id=1, source_target_pairs={{0,4},{1,5},{2,6},{3,7},{4,0},{5,1},{6,2},{7,3},{8,12},{9,13},{10,... | collective-permute-start | bytes 393224 | tf_op jit(solution)/shard_map/ppermute | solution.py:507
  90.5 2.8 %collective-permute-done.18.three_ref = bf16[64,1024]{1,0:T(8,128)(2,1)S(1)} collective-permute-done((bf16[64,1024]{1,0:T(8,128)(2,1)S(1)}, bf16[64,1024]{1,0:T(8,128)(2,1)S(1)}, u32[]{:S(2)}, u32[]{:S(2)}) %collective-permute-start.18) | collective-permute-done | bytes 131104 | tf_op jit(solution)/shard_map/ppermute | solution.py:507
  93.4 2.2 %collective-permute-done.17.two_ref = bf16[64,1024]{1,0:T(8,128)(2,1)S(1)} collective-permute-done((bf16[64,1024]{1,0:T(8,128)(2,1)S(1)}, bf16[64,1024]{1,0:T(8,128)(2,1)S(1)}, u32[]{:S(2)}, u32[]{:S(2)}) %collective-permute-start.17) | collective-permute-done | bytes 131104 | tf_op jit(solution)/shard_map/ppermute | solution.py:507
  105.6 3.6 %collective-permute-done.23.came_ref = bf16[128,1792]{1,0:T(8,128)(2,1)S(1)} collective-permute-done((bf16[128,1792]{1,0:T(8,128)(2,1)S(1)}, bf16[128,1792]{1,0:T(8,128)(2,1)S(1)}, u32[]{:S(2)}, u32[]{:S(2)}) %collective-permute-start.23) | collective-permute-done | bytes 458784 | tf_op jit(solution)/shard_map/ppermute | solution.py:525
  109.4 4.4 %collective-permute-done.20.came_ref = bf16[128,1664]{1,0:T(8,128)(2,1)S(1)} collective-permute-done((bf16[128,1664]{1,0:T(8,128)(2,1)S(1)}, bf16[128,1664]{1,0:T(8,128)(2,1)S(1)}, u32[]{:S(2)}, u32[]{:S(2)}) %collective-permute-start.20) | collective-permute-done | bytes 426016 | tf_op jit(solution)/shard_map/ppermute | solution.py:525
  116.2 4.0 %shard_map.135 = (f32[128,1664]{1,0:T(8,128)S(1)}, f32[128,1664]{1,0:T(8,128)S(1)}, f32[128,1792]{1,0:T(8,128)S(1)}, f32[128,1792]{1,0:T(8,128)S(1)}, f32[128,16...) custom-call(bf16[4,4,32,1024]{3,2,1,0:T(8,128)(2,1)S(1)} %get-tuple-element.60.rows_, ...), custom_call_target="tpu_custom_call" | custom-call | tf_op jit(solution)/shard_map/pallas_call | solution.py:443
  120.3 3.3 %collective-permute-start.25 = (bf16[128,1792]{1,0:T(8,128)(2,1)S(1)}, bf16[128,1792]{1,0:T(8,128)(2,1)S(1)}, u32[]{:S(2)}, u32[]{:S(2)}) collective-permute-start(bf16[128,1792]{1,0:T(8,128)(2,1)S(1)} %shard_map.142), channel_id=1, source_target_pairs={{0,8},{1,25},{2,10},{3,27},{4,12},{5,29},{6,14},{7,31},{8,16},{9,1... | collective-permute-start | bytes 1376264 | tf_op jit(solution)/shard_map/ppermute | solution.py:525
  124.2 3.8 %collective-permute-done.33.came_ref = bf16[128,1664]{1,0:T(8,128)(2,1)S(1)} collective-permute-done((bf16[128,1664]{1,0:T(8,128)(2,1)S(1)}, bf16[128,1664]{1,0:T(8,128)(2,1)S(1)}, u32[]{:S(2)}, u32[]{:S(2)}) %collective-permute-start.33) | collective-permute-done | bytes 426016 | tf_op jit(solution)/shard_map/ppermute | solution.py:525
  128.1 6.4 %collective-permute-done.22.first_came = bf16[128,1664]{1,0:T(8,128)(2,1)S(1)} collective-permute-done((bf16[128,1664]{1,0:T(8,128)(2,1)S(1)}, bf16[128,1664]{1,0:T(8,128)(2,1)S(1)}, u32[]{:S(2)}, u32[]{:S(2)}) %collective-permute-start.22) | collective-permute-done | bytes 426016 | tf_op jit(solution)/shard_map/ppermute | solution.py:525
  134.9 2.8 %collective-permute-start.26 = (bf16[32,3456]{1,0:T(8,128)(2,1)S(1)}, bf16[32,3456]{1,0:T(8,128)(2,1)S(1)}, u32[]{:S(2)}, u32[]{:S(2)}) collective-permute-start(bf16[32,3456]{1,0:T(8,128)(2,1)S(1)} %get-tuple-element.71), channel_id=1, source_target_pairs={{0,64},{8,72},{16,80},{24,88},{32,96},{40,104},{48,112},{56,120},{... | collective-permute-start | bytes 663560 | tf_op jit(solution)/shard_map/ppermute | solution.py:501
  141.2 6.3 %collective-permute-start.35 = (bf16[32,3328]{1,0:T(8,128)(2,1)S(1)}, bf16[32,3328]{1,0:T(8,128)(2,1)S(1)}, u32[]{:S(2)}, u32[]{:S(2)}) collective-permute-start(bf16[32,3328]{1,0:T(8,128)(2,1)S(1)} %get-tuple-element.83), channel_id=1, source_target_pairs={{0,16},{8,24},{16,0},{24,8},{32,48},{40,56},{48,32},{56,40},{64,80... | collective-permute-start | bytes 638984 | tf_op jit(solution)/shard_map/ppermute | solution.py:495
  147.5 3.2 %collective-permute-start.37 = (bf16[32,3328]{1,0:T(8,128)(2,1)S(1)}, bf16[32,3328]{1,0:T(8,128)(2,1)S(1)}, u32[]{:S(2)}, u32[]{:S(2)}) collective-permute-start(bf16[32,3328]{1,0:T(8,128)(2,1)S(1)} %get-tuple-element.85), channel_id=1, source_target_pairs={{0,24},{8,0},{16,8},{24,16},{32,56},{40,32},{48,40},{56,48},{64,88... | collective-permute-start | bytes 638984 | tf_op jit(solution)/shard_map/ppermute | solution.py:495
  151.3 3.2 %collective-permute-done.36 = bf16[32,3328]{1,0:T(8,128)(2,1)S(1)} collective-permute-done((bf16[32,3328]{1,0:T(8,128)(2,1)S(1)}, bf16[32,3328]{1,0:T(8,128)(2,1)S(1)}, u32[]{:S(2)}, u32[]{:S(2)}) %collective-permute-start.36) | collective-permute-done | bytes 213024 | tf_op jit(solution)/shard_map/ppermute | solution.py:495
  (114 shorter events, 52.8 us)
Async XLA Ops:
  2.4 16.7 %all-to-all-start = ((bf16[64,16,128]{2,1,0:T(8,128)(2,1)}), bf16[64,16,128]{2,1,0:T(8,128)(2,1)S(1)}, u32[]{:S(2)}, u32[]{:S(2)}) async-start(bf16[64,16,128]{2,1,0:T(8,128)(2,1)} %get-tuple-element.48), calls=%async_computation | async-start | bytes 524288 | tf_op jit(solution)/shard_map/all_to_all | solution.py:575
  54.5 11.2 %collective-permute-start.8 = (bf16[4,32,1024]{2,1,0:T(8,128)(2,1)S(1)}, bf16[4,32,1024]{2,1,0:T(8,128)(2,1)S(1)}, u32[]{:S(2)}, u32[]{:S(2)}) collective-permute-start(bf16[4,32,1024]{2,1,0:T(8,128)(2,1)S(1)} %get-tuple-element.53.refs_3_), channel_id=1, source_target_pairs={{0,32},{8,40},{16,48},{24,56},{32,64},{40,72},{48,80},{56,88},{64,... | collective-permute-start | bytes 786440 | tf_op jit(solution)/shard_map/ppermute | solution.py:501
  55.2 12.9 %collective-permute-start.7 = (bf16[4,32,1024]{2,1,0:T(8,128)(2,1)S(1)}, bf16[4,32,1024]{2,1,0:T(8,128)(2,1)S(1)}, u32[]{:S(2)}, u32[]{:S(2)}) collective-permute-start(bf16[4,32,1024]{2,1,0:T(8,128)(2,1)S(1)} %get-tuple-element.53.refs_3_), channel_id=1, source_target_pairs={{0,64},{8,72},{16,80},{24,88},{32,96},{40,104},{48,112},{56,120},{... | collective-permute-start | bytes 786440 | tf_op jit(solution)/shard_map/ppermute | solution.py:501
  56.9 11.1 %collective-permute-start.6 = (bf16[4,32,1024]{2,1,0:T(8,128)(2,1)S(1)}, bf16[4,32,1024]{2,1,0:T(8,128)(2,1)S(1)}, u32[]{:S(2)}, u32[]{:S(2)}) collective-permute-start(bf16[4,32,1024]{2,1,0:T(8,128)(2,1)S(1)} %get-tuple-element.53.refs_3_), channel_id=1, source_target_pairs={{0,96},{8,104},{16,112},{24,120},{32,0},{40,8},{48,16},{56,24},{64... | collective-permute-start | bytes 786440 | tf_op jit(solution)/shard_map/ppermute | solution.py:501
  59.5 8.6 %collective-permute-start.11 = (bf16[4,32,1024]{2,1,0:T(8,128)(2,1)S(1)}, bf16[4,32,1024]{2,1,0:T(8,128)(2,1)S(1)}, u32[]{:S(2)}, u32[]{:S(2)}) collective-permute-start(bf16[4,32,1024]{2,1,0:T(8,128)(2,1)S(1)} %get-tuple-element.54.refs_7_), channel_id=1, source_target_pairs={{0,8},{8,16},{16,24},{24,0},{32,40},{40,48},{48,56},{56,32},{64,72... | collective-permute-start | bytes 786440 | tf_op jit(solution)/shard_map/ppermute | solution.py:495
  60.8 10.0 %collective-permute-start.10 = (bf16[4,32,1024]{2,1,0:T(8,128)(2,1)S(1)}, bf16[4,32,1024]{2,1,0:T(8,128)(2,1)S(1)}, u32[]{:S(2)}, u32[]{:S(2)}) collective-permute-start(bf16[4,32,1024]{2,1,0:T(8,128)(2,1)S(1)} %get-tuple-element.54.refs_7_), channel_id=1, source_target_pairs={{0,16},{8,24},{16,0},{24,8},{32,48},{40,56},{48,32},{56,40},{64,80... | collective-permute-start | bytes 786440 | tf_op jit(solution)/shard_map/ppermute | solution.py:495
  75.7 7.9 %collective-permute-start.13 = (bf16[64,1024]{1,0:T(8,128)(2,1)S(1)}, bf16[64,1024]{1,0:T(8,128)(2,1)S(1)}, u32[]{:S(2)}, u32[]{:S(2)}) collective-permute-start(bf16[64,1024]{1,0:T(8,128)(2,1)S(1)} %get-tuple-element.56), channel_id=1, source_target_pairs={{0,4},{1,5},{2,6},{3,7},{4,0},{5,1},{6,2},{7,3},{8,12},{9,13},{10,... | collective-permute-start | bytes 393224 | tf_op jit(solution)/shard_map/ppermute | solution.py:507
  87.3 8.3 %collective-permute-start.17 = (bf16[64,1024]{1,0:T(8,128)(2,1)S(1)}, bf16[64,1024]{1,0:T(8,128)(2,1)S(1)}, u32[]{:S(2)}, u32[]{:S(2)}) collective-permute-start(bf16[64,1024]{1,0:T(8,128)(2,1)S(1)} %shard_map.132.own_ref), channel_id=1, source_target_pairs={{0,4},{1,5},{2,6},{3,7},{4,0},{5,1},{6,2},{7,3},{8,12},{9,13},{10,... | collective-permute-start | bytes 393224 | tf_op jit(solution)/shard_map/ppermute | solution.py:507
  99.1 10.1 %collective-permute-start.23 = (bf16[128,1792]{1,0:T(8,128)(2,1)S(1)}, bf16[128,1792]{1,0:T(8,128)(2,1)S(1)}, u32[]{:S(2)}, u32[]{:S(2)}) collective-permute-start(bf16[128,1792]{1,0:T(8,128)(2,1)S(1)} %get-tuple-element.69), channel_id=1, source_target_pairs={{0,8},{1,25},{2,10},{3,27},{4,12},{5,29},{6,14},{7,31},{8,16},{9,1... | collective-permute-start | bytes 1376264 | tf_op jit(solution)/shard_map/ppermute | solution.py:525
  101.3 12.4 %collective-permute-start.20 = (bf16[128,1664]{1,0:T(8,128)(2,1)S(1)}, bf16[128,1664]{1,0:T(8,128)(2,1)S(1)}, u32[]{:S(2)}, u32[]{:S(2)}) collective-permute-start(bf16[128,1664]{1,0:T(8,128)(2,1)S(1)} %get-tuple-element.66), channel_id=1, source_target_pairs={{0,8},{1,25},{2,10},{3,27},{4,12},{5,29},{6,14},{7,31},{8,16},{9,1... | collective-permute-start | bytes 1277960 | tf_op jit(solution)/shard_map/ppermute | solution.py:525
  102.1 11.8 %collective-permute-start.29 = (bf16[128,1664]{1,0:T(8,128)(2,1)S(1)}, bf16[128,1664]{1,0:T(8,128)(2,1)S(1)}, u32[]{:S(2)}, u32[]{:S(2)}) collective-permute-start(bf16[128,1664]{1,0:T(8,128)(2,1)S(1)} %get-tuple-element.78), channel_id=1, source_target_pairs={{0,32},{1,97},{2,34},{3,99},{4,36},{5,101},{6,38},{7,103},{8,40},{... | collective-permute-start | bytes 1277960 | tf_op jit(solution)/shard_map/ppermute | solution.py:525
  102.1 13.9 %collective-permute-start.32 = (bf16[128,1664]{1,0:T(8,128)(2,1)S(1)}, bf16[128,1664]{1,0:T(8,128)(2,1)S(1)}, u32[]{:S(2)}, u32[]{:S(2)}) collective-permute-start(bf16[128,1664]{1,0:T(8,128)(2,1)S(1)} %get-tuple-element.81), channel_id=1, source_target_pairs={{0,32},{1,97},{2,34},{3,99},{4,36},{5,101},{6,38},{7,103},{8,40},{... | collective-permute-start | bytes 1277960 | tf_op jit(solution)/shard_map/ppermute | solution.py:525
  109.3 10.9 %collective-permute-start.24 = (bf16[128,1792]{1,0:T(8,128)(2,1)S(1)}, bf16[128,1792]{1,0:T(8,128)(2,1)S(1)}, u32[]{:S(2)}, u32[]{:S(2)}) collective-permute-start(bf16[128,1792]{1,0:T(8,128)(2,1)S(1)} %shard_map.141), channel_id=1, source_target_pairs={{0,8},{1,25},{2,10},{3,27},{4,12},{5,29},{6,14},{7,31},{8,16},{9,1... | collective-permute-start | bytes 1376264 | tf_op jit(solution)/shard_map/ppermute | solution.py:525
  113.8 9.8 %collective-permute-start.21 = (bf16[128,1664]{1,0:T(8,128)(2,1)S(1)}, bf16[128,1664]{1,0:T(8,128)(2,1)S(1)}, u32[]{:S(2)}, u32[]{:S(2)}) collective-permute-start(bf16[128,1664]{1,0:T(8,128)(2,1)S(1)} %shard_map.138), channel_id=1, source_target_pairs={{0,8},{1,25},{2,10},{3,27},{4,12},{5,29},{6,14},{7,31},{8,16},{9,1... | collective-permute-start | bytes 1277960 | tf_op jit(solution)/shard_map/ppermute | solution.py:525
  114.0 9.8 %collective-permute-start.30 = (bf16[128,1664]{1,0:T(8,128)(2,1)S(1)}, bf16[128,1664]{1,0:T(8,128)(2,1)S(1)}, u32[]{:S(2)}, u32[]{:S(2)}) collective-permute-start(bf16[128,1664]{1,0:T(8,128)(2,1)S(1)} %shard_map.144), channel_id=1, source_target_pairs={{0,32},{1,97},{2,34},{3,99},{4,36},{5,101},{6,38},{7,103},{8,40},{... | collective-permute-start | bytes 1277960 | tf_op jit(solution)/shard_map/ppermute | solution.py:525
  116.1 11.9 %collective-permute-start.33 = (bf16[128,1664]{1,0:T(8,128)(2,1)S(1)}, bf16[128,1664]{1,0:T(8,128)(2,1)S(1)}, u32[]{:S(2)}, u32[]{:S(2)}) collective-permute-start(bf16[128,1664]{1,0:T(8,128)(2,1)S(1)} %shard_map.146), channel_id=1, source_target_pairs={{0,32},{1,97},{2,34},{3,99},{4,36},{5,101},{6,38},{7,103},{8,40},{... | collective-permute-start | bytes 1277960 | tf_op jit(solution)/shard_map/ppermute | solution.py:525
  120.3 14.3 %collective-permute-start.25 = (bf16[128,1792]{1,0:T(8,128)(2,1)S(1)}, bf16[128,1792]{1,0:T(8,128)(2,1)S(1)}, u32[]{:S(2)}, u32[]{:S(2)}) collective-permute-start(bf16[128,1792]{1,0:T(8,128)(2,1)S(1)} %shard_map.142), channel_id=1, source_target_pairs={{0,8},{1,25},{2,10},{3,27},{4,12},{5,29},{6,14},{7,31},{8,16},{9,1... | collective-permute-start | bytes 1376264 | tf_op jit(solution)/shard_map/ppermute | solution.py:525
  123.7 10.9 %collective-permute-start.22 = (bf16[128,1664]{1,0:T(8,128)(2,1)S(1)}, bf16[128,1664]{1,0:T(8,128)(2,1)S(1)}, u32[]{:S(2)}, u32[]{:S(2)}) collective-permute-start(bf16[128,1664]{1,0:T(8,128)(2,1)S(1)} %shard_map.139), channel_id=1, source_target_pairs={{0,8},{1,25},{2,10},{3,27},{4,12},{5,29},{6,14},{7,31},{8,16},{9,1... | collective-permute-start | bytes 1277960 | tf_op jit(solution)/shard_map/ppermute | solution.py:525
  123.9 17.1 %collective-permute-start.31 = (bf16[128,1664]{1,0:T(8,128)(2,1)S(1)}, bf16[128,1664]{1,0:T(8,128)(2,1)S(1)}, u32[]{:S(2)}, u32[]{:S(2)}) collective-permute-start(bf16[128,1664]{1,0:T(8,128)(2,1)S(1)} %shard_map.145), channel_id=1, source_target_pairs={{0,32},{1,97},{2,34},{3,99},{4,36},{5,101},{6,38},{7,103},{8,40},{... | collective-permute-start | bytes 1277960 | tf_op jit(solution)/shard_map/ppermute | solution.py:525
  128.1 12.9 %collective-permute-start.34 = (bf16[128,1664]{1,0:T(8,128)(2,1)S(1)}, bf16[128,1664]{1,0:T(8,128)(2,1)S(1)}, u32[]{:S(2)}, u32[]{:S(2)}) collective-permute-start(bf16[128,1664]{1,0:T(8,128)(2,1)S(1)} %shard_map.147), channel_id=1, source_target_pairs={{0,32},{1,97},{2,34},{3,99},{4,36},{5,101},{6,38},{7,103},{8,40},{... | collective-permute-start | bytes 1277960 | tf_op jit(solution)/shard_map/ppermute | solution.py:525
  134.9 12.6 %collective-permute-start.26 = (bf16[32,3456]{1,0:T(8,128)(2,1)S(1)}, bf16[32,3456]{1,0:T(8,128)(2,1)S(1)}, u32[]{:S(2)}, u32[]{:S(2)}) collective-permute-start(bf16[32,3456]{1,0:T(8,128)(2,1)S(1)} %get-tuple-element.71), channel_id=1, source_target_pairs={{0,64},{8,72},{16,80},{24,88},{32,96},{40,104},{48,112},{56,120},{... | collective-permute-start | bytes 663560 | tf_op jit(solution)/shard_map/ppermute | solution.py:501
  137.7 13.1 %collective-permute-start.27 = (bf16[32,3456]{1,0:T(8,128)(2,1)S(1)}, bf16[32,3456]{1,0:T(8,128)(2,1)S(1)}, u32[]{:S(2)}, u32[]{:S(2)}) collective-permute-start(bf16[32,3456]{1,0:T(8,128)(2,1)S(1)} %get-tuple-element.72), channel_id=1, source_target_pairs={{0,32},{8,40},{16,48},{24,56},{32,64},{40,72},{48,80},{56,88},{64,... | collective-permute-start | bytes 663560 | tf_op jit(solution)/shard_map/ppermute | solution.py:501
  139.0 11.7 %collective-permute-start.28 = (bf16[32,3456]{1,0:T(8,128)(2,1)S(1)}, bf16[32,3456]{1,0:T(8,128)(2,1)S(1)}, u32[]{:S(2)}, u32[]{:S(2)}) collective-permute-start(bf16[32,3456]{1,0:T(8,128)(2,1)S(1)} %get-tuple-element.73), channel_id=1, source_target_pairs={{0,96},{8,104},{16,112},{24,120},{32,0},{40,8},{48,16},{56,24},{64... | collective-permute-start | bytes 663560 | tf_op jit(solution)/shard_map/ppermute | solution.py:501
  141.2 10.1 %collective-permute-start.35 = (bf16[32,3328]{1,0:T(8,128)(2,1)S(1)}, bf16[32,3328]{1,0:T(8,128)(2,1)S(1)}, u32[]{:S(2)}, u32[]{:S(2)}) collective-permute-start(bf16[32,3328]{1,0:T(8,128)(2,1)S(1)} %get-tuple-element.83), channel_id=1, source_target_pairs={{0,16},{8,24},{16,0},{24,8},{32,48},{40,56},{48,32},{56,40},{64,80... | collective-permute-start | bytes 638984 | tf_op jit(solution)/shard_map/ppermute | solution.py:495
  (28 other events, 277.8 us)

commit v6 on v5

--- a/solution.py
+++ b/solution.py
@@ -39,6 +39,16 @@
 def place():
     attn, ffn = lax.axis_index("attn"), lax.axis_index("ffn")
     return attn // SIDE, attn % SIDE, ffn // 2, ffn % 2
+
+
+def stand():
+    y, z, _, core = place()
+    return jnp.where(core == 0, z, y), jnp.where(core == 0, y, z)
+
+
+def spot(first, second):
+    core = place()[3]
+    return jnp.where(core == 0, second, first), jnp.where(core == 0, first, second)
 
 
 def start_all(copies):
@@ -91,10 +101,8 @@
     )(home, queries)
 
 
-def prepare_body(home_hbm, *refs):
-    sources, list_ref, targets = refs[:4], refs[4], refs[5:9]
-    home_ref, lengths_ref, found_ref, sems = refs[9:]
-    pairs = [(home_hbm, home_ref), (sources[0], lengths_ref)] + list(zip(sources, targets))
+def prepare_body(home_hbm, lengths_hbm, list_ref, home_ref, lengths_ref, found_ref, sems):
+    pairs = ((home_hbm, home_ref), (lengths_hbm, lengths_ref))
     copies = start_all([pltpu.make_async_copy(a, b, sems.at[k]) for k, (a, b) in enumerate(pairs)])
     mine = lax.axis_index("attn")
     copies[0].wait()
@@ -127,38 +135,39 @@
         for extra in range(GROUP):
             list_ref[kind, counts[kind] + extra] = last
         list_ref[kind, LISTED - 1] = counts[kind]
-    for copy in copies[2:]:
-        copy.wait()
-
-
-def prepare(home, *arrays):
+
+
+def prepare(home, lengths):
     return pl.pallas_call(
         prepare_body,
-        out_shape=[jax.ShapeDtypeStruct((2, LISTED), jnp.int32)]
-        + [jax.ShapeDtypeStruct(a.shape, a.dtype) for a in arrays],
-        in_specs=[HBM] * 5,
-        out_specs=[SMEM] + [VMEM] * 4,
+        out_shape=jax.ShapeDtypeStruct((2, LISTED), jnp.int32),
+        in_specs=[HBM] * 2,
+        out_specs=SMEM,
         scratch_shapes=[
             pltpu.SMEM(home.shape, jnp.int32),
-            pltpu.SMEM(arrays[0].shape, jnp.int32),
+            pltpu.SMEM(lengths.shape, jnp.int32),
             pltpu.SMEM((LISTED,), jnp.int32),
-            pltpu.SemaphoreType.DMA((6,)),
+            pltpu.SemaphoreType.DMA((2,)),
         ],
-        compiler_params=params(),
-    )(home, *arrays)
-
-
-def attend_body(lengths_vmem, table_vmem, list_ref, queries_ref, k_ref, v_ref, out_ref, lengths_ref, table_ref, sems):
+        compiler_params=params(WIDE),
+    )(home, lengths)
+
+
+def attend_body(list_ref, queries_hbm, lengths_hbm, table_hbm, k_hbm, v_hbm, out_ref, *refs):
+    queries_ref, lengths_ref, table_ref, k_ref, v_ref, sems = refs
     first, rest = pl.ds(0, SHORT), pl.ds(SHORT, MAXP - SHORT)
     pairs = (
-        (lengths_vmem, lengths_ref),
-        (table_vmem.at[first], table_ref.at[first]),
-        (table_vmem.at[rest], table_ref.at[rest]),
+        (lengths_hbm, lengths_ref),
+        (table_hbm.at[first], table_ref.at[first]),
+        (k_hbm, k_ref),
+        (queries_hbm, queries_ref),
+        (v_hbm, v_ref),
+        (table_hbm.at[rest], table_ref.at[rest]),
     )
     copies = start_all([pltpu.make_async_copy(a, b, sems.at[k]) for k, (a, b) in enumerate(pairs)])
     out_ref[...] = jnp.zeros_like(out_ref)
-    copies[0].wait()
-    copies[1].wait()
+    for copy in copies[:-1]:
+        copy.wait()
 
     def step(kind, count, index, carry):
         positions = lax.broadcasted_iota(jnp.int32, (HEADS, count * PAGE), 1)
@@ -195,79 +204,79 @@
 
     for kind, count in ((0, SHORT), (1, MAXP)):
         if kind:
-            copies[2].wait()
+            copies[-1].wait()
         groups = (list_ref[kind, LISTED - 1] + GROUP - 1) // GROUP
         lax.fori_loop(0, groups, functools.partial(step, kind, count), 0)
 
 
 def attend(listed, queries, lengths, table, k_pool, v_pool):
+    arrays = (queries, lengths, table, k_pool, v_pool)
+    spaces = (pltpu.VMEM, pltpu.SMEM, pltpu.SMEM, pltpu.VMEM, pltpu.VMEM)
     return pl.pallas_call(
         attend_body,
         out_shape=jax.ShapeDtypeStruct((SLOTS, HEADS, HD), jnp.bfloat16),
-        in_specs=[VMEM, VMEM, SMEM] + [VMEM] * 3,
-        out_specs=VMEM,
-        scratch_shapes=[
-            pltpu.SMEM(lengths.shape, jnp.int32),
-            pltpu.SMEM(table.shape, jnp.int32),
-            pltpu.SemaphoreType.DMA((3,)),
-        ],
-        compiler_params=params(),
-    )(lengths, table, listed, queries, k_pool, v_pool)
-
-
-def collect_body(dest_ref, slots_ref, left_ref, right_ref, wide_ref):
+        in_specs=[SMEM, pl.BlockSpec(memory_space=pl.ANY)] + [HBM] * 4,
+        out_specs=VMEM,
+        scratch_shapes=[space(a.shape, a.dtype) for space, a in zip(spaces, arrays)]
+        + [pltpu.SemaphoreType.DMA((6,))],
+        compiler_params=params(WIDE),
+    )(listed, *arrays)
+
+
+def collect_body(dest_hbm, slots_ref, out_ref, wide_ref, dest_ref, sem):
+    pltpu.async_copy(dest_hbm, dest_ref, sem).wait()
     for row in range(ROWS):
         heads = slots_ref[dest_ref[row]].astype(jnp.float32)
         for head in range(HEADS):
             wide_ref[row : row + 1, head * HD : (head + 1) * HD] = heads[head : head + 1]
-    left_ref[...] = wide_ref[:, :WIDTH].astype(jnp.bfloat16)
-    right_ref[...] = wide_ref[:, WIDTH:].astype(jnp.bfloat16)
+    out_ref[...] = wide_ref[...].astype(jnp.bfloat16)
 
 
 def collect(dest, slots):
     return pl.pallas_call(
         collect_body,
-        out_shape=[jax.ShapeDtypeStruct((ROWS, WIDTH), jnp.bfloat16)] * 2,
-        in_specs=[SMEM, VMEM],
-        out_specs=[VMEM] * 2,
-        scratch_shapes=[pltpu.VMEM((ROWS, HEADS * HD), jnp.float32)],
+        out_shape=jax.ShapeDtypeStruct((ROWS, HEADS * HD), jnp.bfloat16),
+        in_specs=[pl.BlockSpec(memory_space=pl.ANY), VMEM],
+        out_specs=VMEM,
+        scratch_shapes=[
+            pltpu.VMEM((ROWS, HEADS * HD), jnp.float32),
+            pltpu.SMEM((ROWS,), jnp.int32),
+            pltpu.SemaphoreType.DMA,
+        ],
         compiler_params=params(),
     )(dest, slots)
 
 
 def gather_line_body(*refs):
-    for line, ins, out in ((1, refs[:4], refs[8]), (0, refs[4:8], refs[9])):
-        for at, block in zip(relative(place()[line]), ins):
-            out[at] = block[...]
-
-
-def gather_line(left, right):
+    for at, block in zip(relative(stand()[0]), refs[:4]):
+        refs[4][at] = block[...]
+
+
+def gather_line(blocks):
     return pl.pallas_call(
         gather_line_body,
-        out_shape=[jax.ShapeDtypeStruct((SIDE, ROWS, WIDTH), jnp.bfloat16)] * 2,
-        in_specs=[VMEM] * 8,
-        out_specs=[VMEM] * 2,
-        compiler_params=params(),
-    )(*left, *right)
+        out_shape=jax.ShapeDtypeStruct((SIDE,) + blocks[0].shape, jnp.bfloat16),
+        in_specs=[VMEM] * 4,
+        out_specs=VMEM,
+        compiler_params=params(),
+    )(*blocks)
 
 
 def gather_all_body(*refs):
-    out = refs[8]
-    for at, block in zip(relative(place()[0]), refs[:4]):
-        out[pl.ds(at * SIDE, SIDE), :, :WIDTH] = block[...]
-    for at, block in zip(relative(place()[1]), refs[4:8]):
-        for y in range(SIDE):
-            out[y * SIDE + at, :, WIDTH:] = block[y]
-
-
-def gather_all(left, right):
+    for at, block in zip(relative(stand()[1]), refs[:4]):
+        for k in range(SIDE):
+            y, z = spot(k, at)
+            refs[4][y * SIDE + z] = block[k]
+
+
+def gather_all(blocks):
     return pl.pallas_call(
         gather_all_body,
-        out_shape=jax.ShapeDtypeStruct((N_ATTN, ROWS, HEADS * HD), jnp.bfloat16),
-        in_specs=[VMEM] * 8,
-        out_specs=VMEM,
-        compiler_params=params(),
-    )(*left, *right)
+        out_shape=jax.ShapeDtypeStruct((N_ATTN,) + blocks[0].shape[1:], jnp.bfloat16),
+        in_specs=[VMEM] * 4,
+        out_specs=VMEM,
+        compiler_params=params(),
+    )(*blocks)
 
 
 def own_stream_body(stream_hbm, after_hbm, out_ref, sem):
@@ -394,20 +403,20 @@
 CUTS = (0, 1664, 3328)
 
 
-def part_columns(line, part):
-    return CUTS[part + 1] - CUTS[part] + (HD if line and part else 0)
+def part_columns(kind, part):
+    return CUTS[part + 1] - CUTS[part] + (HD if kind and part else 0)
 
 
 def project_steps(steps, parts, block_of, up_ref, gate_ref, refs):
     size = SIDE * ROWS
     refs = iter(refs)
-    for line, weight_ref in ((1, gate_ref), (0, up_ref)):
-        here, core = place()[line], place()[3]
+    here = stand()[0]
+    for kind, weight_ref in ((1, gate_ref), (0, up_ref)):
         blocks = []
         for step in steps:
-            there = (here + jnp.where(core == 0, SIDE - step, step)) % SIDE
+            there = (here + (SIDE - step if kind else step)) % SIDE
             for other in range(SIDE):
-                blocks.append(block_of(other, there) if line else block_of(there, other))
+                blocks.append(block_of(*spot(there, other)))
         lhs = jnp.concatenate([rows for rows, _ in blocks], axis=0)
         for part in parts:
             width = CUTS[part + 1] - CUTS[part]
@@ -417,7 +426,7 @@
             for k in range(len(steps)):
                 out = next(refs)
                 out[:, :width] = product[size * k : size * (k + 1)].astype(out.dtype)
-                if line and part:
+                if kind and part:
                     totals = [t for _, t in blocks[SIDE * k : SIDE * (k + 1)]]
                     out[:, width:] = jnp.concatenate(totals, axis=0).astype(out.dtype)
 
@@ -439,11 +448,11 @@
 
 
 def project(body, steps, parts, dtype, weights, *arrays):
-    keys = [(line, part, step) for line in (1, 0) for part in parts for step in steps]
+    keys = [(kind, part, step) for kind in (1, 0) for part in parts for step in steps]
     results = pl.pallas_call(
         functools.partial(body, steps, parts),
         out_shape=[
-            jax.ShapeDtypeStruct((SIDE * ROWS, part_columns(line, part)), dtype) for line, part, _ in keys
+            jax.ShapeDtypeStruct((SIDE * ROWS, part_columns(kind, part)), dtype) for kind, part, _ in keys
         ],
         in_specs=[VMEM] * (len(arrays) + 2),
         out_specs=[VMEM] * len(keys),
@@ -466,41 +475,41 @@
     )(own, came)
 
 
-def merge_body(line, first_ref, second_ref, first_came, second_came, *refs):
-    outs, sums_ref = refs[:4], refs[4]
+def merge_body(*refs):
+    outs, sums_ref = refs[8:12], refs[12]
     start = 0
-    for own_ref, came_ref in ((first_ref, first_came), (second_ref, second_came)):
+    for own_ref, came_ref in zip(refs[:4], refs[4:8]):
         total = own_ref[...] + came_ref[...].astype(jnp.float32)
         width = total.shape[1]
         sums_ref[:, :, start : start + width] = total.reshape(SIDE, ROWS, width)
         start += width
-    for at, out in zip(relative(place()[1 - line]), outs):
+    for at, out in zip(relative(stand()[1]), outs):
         out[...] = sums_ref[at].astype(out.dtype)
 
 
-def merge(line, own, came):
+def merge(own, came):
     columns = sum(a.shape[1] for a in own)
     return pl.pallas_call(
-        functools.partial(merge_body, line),
+        merge_body,
         out_shape=[jax.ShapeDtypeStruct((ROWS, columns), jnp.bfloat16)] * 3
         + [jax.ShapeDtypeStruct((ROWS, columns), jnp.float32)],
-        in_specs=[VMEM] * 4,
+        in_specs=[VMEM] * 8,
         out_specs=[VMEM] * 4,
         scratch_shapes=[pltpu.VMEM((SIDE, ROWS, columns), jnp.float32)],
-        compiler_params=params(),
+        compiler_params=params(24),
     )(*own, *came)
 
 
-def along_z(x, shift):
-    return lax.ppermute(
-        x, "attn", [(y * SIDE + z, y * SIDE + (z + shift) % SIDE) for y in range(SIDE) for z in range(SIDE)]
-    )
-
-
-def along_y(x, shift):
-    return lax.ppermute(
-        x, "attn", [(y * SIDE + z, (y + shift) % SIDE * SIDE + z) for y in range(SIDE) for z in range(SIDE)]
-    )
+def along(second, x, shift):
+    pairs = []
+    for y in range(SIDE):
+        for z in range(SIDE):
+            for ffn in range(8):
+                at = [y, z]
+                line = (1 - ffn % 2) ^ second
+                at[line] = (at[line] + shift) % SIDE
+                pairs.append(((y * SIDE + z) * 8 + ffn, (at[0] * SIDE + at[1]) * 8 + ffn))
+    return lax.ppermute(x, ("attn", "ffn"), pairs)
 
 
 def along_x(x, shift):
@@ -513,42 +522,30 @@
     return lax.ppermute(x, "ffn", [(f, f ^ 1) for f in range(8)])
 
 
-def along_ring(line, x):
-    pairs = []
-    for y in range(SIDE):
-        for z in range(SIDE):
-            for ffn in range(8):
-                way = 1 - 2 * (ffn % 2)
-                at = [y, z]
-                at[line] = (at[line] + way) % SIDE
-                pairs.append(((y * SIDE + z) * 8 + ffn, (at[0] * SIDE + at[1]) * 8 + ffn))
-    return lax.ppermute(x, ("attn", "ffn"), pairs)
-
-
 def scatter(halves, gain, weights):
     came = {}
+    keys = [(kind, part) for part in range(2) for kind in (1, 0)]
+
+    def send(kind, x):
+        return along(0, x, 1 if kind else 3)
+
     for part in range(2):
         first = project(first_body, (1,), (part,), jnp.bfloat16, weights, *halves, gain)
-        for line in (1, 0):
-            came[line, part] = along_ring(line, first[line, part, 1])
+        for kind in (1, 0):
+            came[kind, part] = send(kind, first[kind, part, 1])
     residual, rows, squares = assemble(*halves, gain)
     rest = project(rest_body, (2,), (0, 1), jnp.float32, weights, rows, squares)
     rest |= project(rest_body, (3, 0), (0, 1), jnp.float32, weights, rows, squares)
     for step in (2, 3):
-        for part in range(2):
-            for line in (1, 0):
-                came[line, part] = along_ring(line, relay(rest[line, part, step], came[line, part]))
-    sums = []
-    for line, cross in ((1, along_y), (0, along_z)):
-        one, two, three, mine = merge(
-            line, [rest[line, part, 0] for part in range(2)], [came[line, part] for part in range(2)]
-        )
-        sums.append((mine, cross(two, 2), cross(one, 1), cross(three, 3)))
-    return residual, sums
-
-
-def line_of(shift, x):
-    one, three, two = shift(x, 3), shift(x, 1), shift(x, 2)
+        for kind, part in keys:
+            came[kind, part] = send(kind, relay(rest[kind, part, step], came[kind, part]))
+    order = ((1, 0), (1, 1), (0, 0), (0, 1))
+    one, two, three, mine = merge([rest[key + (0,)] for key in order], [came[key] for key in order])
+    return residual, (mine, along(1, two, 2), along(1, one, 1), along(1, three, 3))
+
+
+def line_of(second, x):
+    one, three, two = along(second, x, 3), along(second, x, 1), along(second, x, 2)
     return one, two, three, x
 
 
@@ -571,14 +568,13 @@
 
     table = page_table.T
     outgoing, dest = dispatch(home, queries)
-    listed, *here = prepare(home, lengths, table, k_pool, v_pool)
+    listed = prepare(home, lengths)
     arrived = lax.all_to_all(outgoing, "attn", split_axis=0, concat_axis=0, tiled=True)
-    blended = attend(listed, arrived, *here)
+    blended = attend(listed, arrived, lengths, table, k_pool, v_pool)
     returned = lax.all_to_all(blended, "attn", split_axis=0, concat_axis=0, tiled=True)
-    left, right = collect(dest, returned)
-    stream_rows = own_stream(stream, left)
-    left, right = gather_line(line_of(along_z, left), line_of(along_y, right))
-    gathered = gather_all(line_of(along_y, left), line_of(along_z, right))
+    attention = collect(dest, returned)
+    stream_rows = own_stream(stream, attention)
+    gathered = gather_all(line_of(1, gather_line(line_of(0, attention))))
     half = REQS // 2
     gathered = gathered.reshape(2, half, HEADS * HD)
 
@@ -592,11 +588,11 @@
     other_half = to_sibling(this_half)
 
     residual, sums = scatter((this_half, other_half), norm_gain.reshape(1, WIDTH), (w_up, w_gate))
-    gate, up = (sum(p.astype(f32) for p in parts) for parts in sums)
+    total = sum(part.astype(f32) for part in sums)
     columns = w_gate.shape[1]
-    scaling = lax.rsqrt(gate[:, columns : columns + 1] / D + EPS)
-    gate = gate[:, :columns] * scaling
-    up = up * scaling
+    scaling = lax.rsqrt(total[:, columns : columns + 1] / D + EPS)
+    gate = total[:, :columns] * scaling
+    up = total[:, columns + HD :] * scaling
     hidden = (jax.nn.silu(gate) * up).astype(jnp.bfloat16)
     return (residual, hidden)
 

time: 155 us -> 149 us (0.961)
  starting transfers between devices: 60.7 us -> 51.3 us
  waiting for transfers between devices: 45.1 us -> 53.5 us
  blocking collectives: 17.8 us -> 12 us
  Pallas kernels: 24.4 us -> 29.3 us
  local copies, waits for them, and re-layouts: 5.35 us -> 1.37 us
    ppermute x30 -> x21, starting transfers between devices: 41.2 us -> 32 us  [along(): return lax.ppermute(x, ('attn', 'ffn'), pairs)]
    all_to_all x1, blocking collectives: 17.8 us -> 12 us  [on_device(): lax.all_to_all(blended, 'attn', split_axis=0, concat_axis=0, tiled=True)]
    pallas_call x1, Pallas kernels: 5.15 us -> 9.47 us  [attend(): pl.pallas_call(attend_body, out_shape=jax.ShapeDtypeStruct((SLOTS, HEADS,...]
    ppermute x30 -> x21, waiting for transfers between devices: 32.8 us -> 37 us  [along(): return lax.ppermute(x, ('attn', 'ffn'), pairs)]
    all_to_all x1, waiting for transfers between devices: 0.99 us -> 5.15 us  [on_device(): lax.all_to_all(outgoing, 'attn', split_axis=0, concat_axis=0, tiled=True)]
    unnamed x26 -> x18, local copies, waits for them, and re-layouts: 5.34 us -> 1.37 us
    pallas_call x6 -> x5, Pallas kernels: 4.32 us -> 4.89 us  [the longest x1 3.35 us: prepare(): pl.pallas_call(prepare_body, out_shape=jax.ShapeDtypeStruct((2, LISTED),...]
  transfers between devices with their start and end apart: 39 -> 30, of which waited for: 21 -> 18; matrix products, arithmetic and copies ran while one was open for 0% -> 0% of each run, Pallas kernels for 9% -> 9%
where the time goes in v6:
time: 149 us; the launch traced here: 150 us
  waiting for transfers between devices  53.5 us (36%)
  starting transfers between devices  51.3 us (34%)
  Pallas kernels  29.3 us (20%)
  blocking collectives  12 us (8%)
    ppermute x21, waiting for transfers between devices, along(): return lax.ppermute(x, ('attn', 'ffn'), pairs)  37 us
    ppermute x21, starting transfers between devices, along(): return lax.ppermute(x, ('attn', 'ffn'), pairs)  32 us
    all_to_all x1, blocking collectives, on_device(): lax.all_to_all(blended, 'attn', split_axis=0, concat_axis=0, tiled=True)  12 us
    ppermute x6, starting transfers between devices, along_x(): lax.ppermute(x, 'ffn', [(chip * 2 + core, (chip + shift) % SIDE * 2 + cor...  11 us
    pallas_call x1, Pallas kernels, attend(): pl.pallas_call(attend_body, out_shape=jax.ShapeDtypeStruct((SLOTS, HEADS,...  9.47 us
    ppermute x6, waiting for transfers between devices, along_x(): lax.ppermute(x, 'ffn', [(chip * 2 + core, (chip + shift) % SIDE * 2 + cor...  8.79 us
    pallas_call x4, Pallas kernels, project(): pl.pallas_call(functools.partial(body, steps, parts), out_shape=[jax.Shap...  8.34 us
    all_to_all x1, starting transfers between devices, on_device(): lax.all_to_all(outgoing, 'attn', split_axis=0, concat_axis=0, tiled=True)  8.14 us
  transfers between devices with their start and end apart: 30, of which 18 were waited for; matrix products, arithmetic and copies ran while one was open for 0% of the time, Pallas kernels for 9%

profile of v6, /device:TPU:0, one launch (start us, length us, event | category | flops | bytes accessed | tf_op | source)
XLA Modules:
  0.0 149.6 jit_solution(6905871903366687496)
XLA Ops:
  2.4 8.1 %all-to-all-start = ((bf16[64,16,128]{2,1,0:T(8,128)(2,1)}), bf16[64,16,128]{2,1,0:T(8,128)(2,1)S(1)}, u32[]{:S(2)}, u32[]{:S(2)}) async-start(bf16[64,16,128]{2,1,0:T(8,128)(2,1)} %get-tuple-element.32), calls=%async_computation | async-start | bytes 524288 | tf_op jit(solution)/shard_map/all_to_all | solution.py:572
  10.6 3.4 %shard_map.123.list_ref = s32[2,128]{1,0:T(2,128)} custom-call(s32[1,512]{1,0:T(1,128)} %bitcast.21, s32[1,512]{1,0:T(1,128)} %bitcast.22), custom_call_target="tpu_custom_call" | custom-call | tf_op jit(solution)/shard_map/pallas_call | solution.py:141
  13.9 5.2 %all-to-all-done.queries_hbm = bf16[64,16,128]{2,1,0:T(8,128)(2,1)S(1)} async-done(((bf16[64,16,128]{2,1,0:T(8,128)(2,1)}), bf16[64,16,128]{2,1,0:T(8,128)(2,1)S(1)}, u32[]{:S(2)}, u32[]{:S(2)}) %all-to-all-start) | async-done | bytes 262176 | tf_op jit(solution)/shard_map/all_to_all | solution.py:572
  19.8 9.5 %shard_map.124 = bf16[64,16,128]{2,1,0:T(8,128)(2,1)} custom-call(s32[2,128]{1,0:T(2,128)} %shard_map.123.list_ref, bf16[64,16,128]{2,1,0:T(8,128)(2,1)} %copy-done.3, s32[1,512]{1,0:T(1,128)} %bitcast.23, s32[32,512]{1,0:T(8,128)} %bitcast.19, bf16[256,16,128]{2,1,0:T(8,128)(2,1)} %k_hbm.1, bf16[256,16,128]{2,1,0:T(8,128)(2,1)} %v_hbm.1), custom_call_target="tpu_custom_call" | custom-call | tf_op jit(solution)/shard_map/pallas_call | solution.py:215
  29.2 12.0 %all_to_all.10.slots_ref = bf16[64,16,128]{2,1,0:T(8,128)(2,1)S(1)} all-to-all(bf16[64,16,128]{2,1,0:T(8,128)(2,1)} %shard_map.124), channel_id=1, replica_groups=mesh['attn'=16,'ffn'=8] {'attn'}, dimensions={0} | all-to-all | bytes 524288 | tf_op jit(solution)/shard_map/all_to_all | solution.py:574
  46.7 3.5 %collective-permute-done.2.refs_2_ = bf16[32,2048]{1,0:T(8,128)(2,1)S(1)} collective-permute-done((bf16[32,2048]{1,0:T(8,128)(2,1)S(1)}, bf16[32,2048]{1,0:T(8,128)(2,1)S(1)}, u32[]{:S(2)}, u32[]{:S(2)}) %collective-permute-start.2) | collective-permute-done | bytes 131104 | tf_op jit(solution)/shard_map/ppermute | solution.py:512
  51.5 2.2 %collective-permute-start.4 = (bf16[4,32,2048]{2,1,0:T(8,128)(2,1)S(1)}, bf16[4,32,2048]{2,1,0:T(8,128)(2,1)S(1)}, u32[]{:S(2)}, u32[]{:S(2)}) collective-permute-start(bf16[4,32,2048]{2,1,0:T(8,128)(2,1)S(1)} %shard_map.127.refs_3_), channel_id=1, source_target_pairs={{0,64},{1,17},{2,66},{3,19},{4,68},{5,21},{6,70},{7,23},{8,72},{9,... | collective-permute-start | bytes 1572872 | tf_op jit(solution)/shard_map/ppermute | solution.py:512
  55.2 12.0 %collective-permute-done.5.refs_2_ = bf16[4,32,2048]{2,1,0:T(8,128)(2,1)S(1)} collective-permute-done((bf16[4,32,2048]{2,1,0:T(8,128)(2,1)S(1)}, bf16[4,32,2048]{2,1,0:T(8,128)(2,1)S(1)}, u32[]{:S(2)}, u32[]{:S(2)}) %collective-permute-start.5) | collective-permute-done | bytes 524320 | tf_op jit(solution)/shard_map/ppermute | solution.py:512
  71.8 3.1 %collective-permute-start.7 = (bf16[64,1024]{1,0:T(8,128)(2,1)S(1)}, bf16[64,1024]{1,0:T(8,128)(2,1)S(1)}, u32[]{:S(2)}, u32[]{:S(2)}) collective-permute-start(bf16[64,1024]{1,0:T(8,128)(2,1)S(1)} %get-tuple-element.34), channel_id=1, source_target_pairs={{0,4},{1,5},{2,6},{3,7},{4,0},{5,1},{6,2},{7,3},{8,12},{9,13},{10,... | collective-permute-start | bytes 393224 | tf_op jit(solution)/shard_map/ppermute | solution.py:516
  75.5 2.6 %collective-permute-start.9 = (bf16[64,1024]{1,0:T(8,128)(2,1)S(1)}, bf16[64,1024]{1,0:T(8,128)(2,1)S(1)}, u32[]{:S(2)}, u32[]{:S(2)}) collective-permute-start(bf16[64,1024]{1,0:T(8,128)(2,1)S(1)} %get-tuple-element.36), channel_id=1, source_target_pairs={{0,6},{1,7},{2,0},{3,1},{4,2},{5,3},{6,4},{7,5},{8,14},{9,15},{10,... | collective-permute-start | bytes 393224 | tf_op jit(solution)/shard_map/ppermute | solution.py:516
  79.7 2.2 %collective-permute-done.8.b_ref = bf16[64,1024]{1,0:T(8,128)(2,1)S(1)} collective-permute-done((bf16[64,1024]{1,0:T(8,128)(2,1)S(1)}, bf16[64,1024]{1,0:T(8,128)(2,1)S(1)}, u32[]{:S(2)}, u32[]{:S(2)}) %collective-permute-start.8) | collective-permute-done | bytes 131104 | tf_op jit(solution)/shard_map/ppermute | solution.py:516
  83.4 3.0 %collective-permute-start.11 = (bf16[64,1024]{1,0:T(8,128)(2,1)S(1)}, bf16[64,1024]{1,0:T(8,128)(2,1)S(1)}, u32[]{:S(2)}, u32[]{:S(2)}) collective-permute-start(bf16[64,1024]{1,0:T(8,128)(2,1)S(1)} %shard_map.132.own_ref), channel_id=1, source_target_pairs={{0,4},{1,5},{2,6},{3,7},{4,0},{5,1},{6,2},{7,3},{8,12},{9,13},{10,... | collective-permute-start | bytes 393224 | tf_op jit(solution)/shard_map/ppermute | solution.py:516
  86.7 2.8 %collective-permute-done.12.three_ref = bf16[64,1024]{1,0:T(8,128)(2,1)S(1)} collective-permute-done((bf16[64,1024]{1,0:T(8,128)(2,1)S(1)}, bf16[64,1024]{1,0:T(8,128)(2,1)S(1)}, u32[]{:S(2)}, u32[]{:S(2)}) %collective-permute-start.12) | collective-permute-done | bytes 131104 | tf_op jit(solution)/shard_map/ppermute | solution.py:516
  89.5 2.2 %collective-permute-done.11.two_ref = bf16[64,1024]{1,0:T(8,128)(2,1)S(1)} collective-permute-done((bf16[64,1024]{1,0:T(8,128)(2,1)S(1)}, bf16[64,1024]{1,0:T(8,128)(2,1)S(1)}, u32[]{:S(2)}, u32[]{:S(2)}) %collective-permute-start.11) | collective-permute-done | bytes 131104 | tf_op jit(solution)/shard_map/ppermute | solution.py:516
  98.0 2.7 %collective-permute-start.20 = (bf16[128,1664]{1,0:T(8,128)(2,1)S(1)}, bf16[128,1664]{1,0:T(8,128)(2,1)S(1)}, u32[]{:S(2)}, u32[]{:S(2)}) collective-permute-start(bf16[128,1664]{1,0:T(8,128)(2,1)S(1)} %get-tuple-element.52), channel_id=1, source_target_pairs={{0,24},{1,97},{2,26},{3,99},{4,28},{5,101},{6,30},{7,103},{8,0},{9... | collective-permute-start | bytes 1277960 | tf_op jit(solution)/shard_map/ppermute | solution.py:512
  106.2 3.1 %collective-permute-done.14.came_ref = bf16[128,1664]{1,0:T(8,128)(2,1)S(1)} collective-permute-done((bf16[128,1664]{1,0:T(8,128)(2,1)S(1)}, bf16[128,1664]{1,0:T(8,128)(2,1)S(1)}, u32[]{:S(2)}, u32[]{:S(2)}) %collective-permute-start.14) | collective-permute-done | bytes 426016 | tf_op jit(solution)/shard_map/ppermute | solution.py:512
  109.6 3.3 %collective-permute-start.21 = (bf16[128,1664]{1,0:T(8,128)(2,1)S(1)}, bf16[128,1664]{1,0:T(8,128)(2,1)S(1)}, u32[]{:S(2)}, u32[]{:S(2)}) collective-permute-start(bf16[128,1664]{1,0:T(8,128)(2,1)S(1)} %shard_map.143), channel_id=1, source_target_pairs={{0,24},{1,97},{2,26},{3,99},{4,28},{5,101},{6,30},{7,103},{8,0},{9... | collective-permute-start | bytes 1277960 | tf_op jit(solution)/shard_map/ppermute | solution.py:512
  114.7 4.0 %shard_map.135 = (f32[128,1664]{1,0:T(8,128)S(1)}, f32[128,1664]{1,0:T(8,128)S(1)}, f32[128,1792]{1,0:T(8,128)S(1)}, f32[128,1792]{1,0:T(8,128)S(1)}, f32[128,16...) custom-call(bf16[4,4,32,1024]{3,2,1,0:T(8,128)(2,1)S(1)} %get-tuple-element.38.rows_, ...), custom_call_target="tpu_custom_call" | custom-call | tf_op jit(solution)/shard_map/pallas_call | solution.py:452
  119.9 3.3 %collective-permute-start.22 = (bf16[128,1664]{1,0:T(8,128)(2,1)S(1)}, bf16[128,1664]{1,0:T(8,128)(2,1)S(1)}, u32[]{:S(2)}, u32[]{:S(2)}) collective-permute-start(bf16[128,1664]{1,0:T(8,128)(2,1)S(1)} %shard_map.144), channel_id=1, source_target_pairs={{0,24},{1,97},{2,26},{3,99},{4,28},{5,101},{6,30},{7,103},{8,0},{9... | collective-permute-start | bytes 1277960 | tf_op jit(solution)/shard_map/ppermute | solution.py:512
  123.2 3.7 %collective-permute-start.25 = (bf16[128,1664]{1,0:T(8,128)(2,1)S(1)}, bf16[128,1664]{1,0:T(8,128)(2,1)S(1)}, u32[]{:S(2)}, u32[]{:S(2)}) collective-permute-start(bf16[128,1664]{1,0:T(8,128)(2,1)S(1)} %shard_map.146), channel_id=1, source_target_pairs={{0,24},{1,97},{2,26},{3,99},{4,28},{5,101},{6,30},{7,103},{8,0},{9... | collective-permute-start | bytes 1277960 | tf_op jit(solution)/shard_map/ppermute | solution.py:512
  127.0 6.1 %collective-permute-done.16.refs_4_ = bf16[128,1664]{1,0:T(8,128)(2,1)S(1)} collective-permute-done((bf16[128,1664]{1,0:T(8,128)(2,1)S(1)}, bf16[128,1664]{1,0:T(8,128)(2,1)S(1)}, u32[]{:S(2)}, u32[]{:S(2)}) %collective-permute-start.16) | collective-permute-done | bytes 426016 | tf_op jit(solution)/shard_map/ppermute | solution.py:512
  135.3 2.1 %collective-permute-start.27 = (bf16[32,6784]{1,0:T(8,128)(2,1)S(1)}, bf16[32,6784]{1,0:T(8,128)(2,1)S(1)}, u32[]{:S(2)}, u32[]{:S(2)}) collective-permute-start(bf16[32,6784]{1,0:T(8,128)(2,1)S(1)} %get-tuple-element.58), channel_id=1, source_target_pairs={{0,32},{1,9},{2,34},{3,11},{4,36},{5,13},{6,38},{7,15},{8,40},{9,1... | collective-permute-start | bytes 1302536 | tf_op jit(solution)/shard_map/ppermute | solution.py:512
  138.6 5.2 %collective-permute-done.26 = bf16[32,6784]{1,0:T(8,128)(2,1)S(1)} collective-permute-done((bf16[32,6784]{1,0:T(8,128)(2,1)S(1)}, bf16[32,6784]{1,0:T(8,128)(2,1)S(1)}, u32[]{:S(2)}, u32[]{:S(2)}) %collective-permute-start.26) | collective-permute-done | bytes 434208 | tf_op jit(solution)/shard_map/ppermute | solution.py:512
  143.8 4.5 %collective-permute-done.27 = bf16[32,6784]{1,0:T(8,128)(2,1)S(1)} collective-permute-done((bf16[32,6784]{1,0:T(8,128)(2,1)S(1)}, bf16[32,6784]{1,0:T(8,128)(2,1)S(1)}, u32[]{:S(2)}, u32[]{:S(2)}) %collective-permute-start.27) | collective-permute-done | bytes 434208 | tf_op jit(solution)/shard_map/ppermute | solution.py:512
  (87 shorter events, 38.7 us)
Async XLA Ops:
  2.4 16.7 %all-to-all-start = ((bf16[64,16,128]{2,1,0:T(8,128)(2,1)}), bf16[64,16,128]{2,1,0:T(8,128)(2,1)S(1)}, u32[]{:S(2)}, u32[]{:S(2)}) async-start(bf16[64,16,128]{2,1,0:T(8,128)(2,1)} %get-tuple-element.32), calls=%async_computation | async-start | bytes 524288 | tf_op jit(solution)/shard_map/all_to_all | solution.py:572
  42.6 7.7 %collective-permute-start.2 = (bf16[32,2048]{1,0:T(8,128)(2,1)S(1)}, bf16[32,2048]{1,0:T(8,128)(2,1)S(1)}, u32[]{:S(2)}, u32[]{:S(2)}) collective-permute-start(bf16[32,2048]{1,0:T(8,128)(2,1)S(1)} %shard_map.125.after_hbm.refs_3_), channel_id=1, source_target_pairs={{0,8},{1,33},{2,10},{3,35},{4,12},{5,37},{6,14},{7,39},{8,16},{9,4... | collective-permute-start | bytes 393224 | tf_op jit(solution)/shard_map/ppermute | solution.py:512
  43.1 7.2 %collective-permute-start.1 = (bf16[32,2048]{1,0:T(8,128)(2,1)S(1)}, bf16[32,2048]{1,0:T(8,128)(2,1)S(1)}, u32[]{:S(2)}, u32[]{:S(2)}) collective-permute-start(bf16[32,2048]{1,0:T(8,128)(2,1)S(1)} %shard_map.125.after_hbm.refs_3_), channel_id=1, source_target_pairs={{0,16},{1,65},{2,18},{3,67},{4,20},{5,69},{6,22},{7,71},{8,24},{9,... | collective-permute-start | bytes 393224 | tf_op jit(solution)/shard_map/ppermute | solution.py:512
  51.1 16.1 %collective-permute-start.5 = (bf16[4,32,2048]{2,1,0:T(8,128)(2,1)S(1)}, bf16[4,32,2048]{2,1,0:T(8,128)(2,1)S(1)}, u32[]{:S(2)}, u32[]{:S(2)}) collective-permute-start(bf16[4,32,2048]{2,1,0:T(8,128)(2,1)S(1)} %shard_map.127.refs_3_), channel_id=1, source_target_pairs={{0,32},{1,9},{2,34},{3,11},{4,36},{5,13},{6,38},{7,15},{8,40},{9,1... | collective-permute-start | bytes 1572872 | tf_op jit(solution)/shard_map/ppermute | solution.py:512
  51.5 15.8 %collective-permute-start.4 = (bf16[4,32,2048]{2,1,0:T(8,128)(2,1)S(1)}, bf16[4,32,2048]{2,1,0:T(8,128)(2,1)S(1)}, u32[]{:S(2)}, u32[]{:S(2)}) collective-permute-start(bf16[4,32,2048]{2,1,0:T(8,128)(2,1)S(1)} %shard_map.127.refs_3_), channel_id=1, source_target_pairs={{0,64},{1,17},{2,66},{3,19},{4,68},{5,21},{6,70},{7,23},{8,72},{9,... | collective-permute-start | bytes 1572872 | tf_op jit(solution)/shard_map/ppermute | solution.py:512
  53.7 14.4 %collective-permute-start.3 = (bf16[4,32,2048]{2,1,0:T(8,128)(2,1)S(1)}, bf16[4,32,2048]{2,1,0:T(8,128)(2,1)S(1)}, u32[]{:S(2)}, u32[]{:S(2)}) collective-permute-start(bf16[4,32,2048]{2,1,0:T(8,128)(2,1)S(1)} %shard_map.127.refs_3_), channel_id=1, source_target_pairs={{0,96},{1,25},{2,98},{3,27},{4,100},{5,29},{6,102},{7,31},{8,104},... | collective-permute-start | bytes 1572872 | tf_op jit(solution)/shard_map/ppermute | solution.py:512
  71.8 7.9 %collective-permute-start.7 = (bf16[64,1024]{1,0:T(8,128)(2,1)S(1)}, bf16[64,1024]{1,0:T(8,128)(2,1)S(1)}, u32[]{:S(2)}, u32[]{:S(2)}) collective-permute-start(bf16[64,1024]{1,0:T(8,128)(2,1)S(1)} %get-tuple-element.34), channel_id=1, source_target_pairs={{0,4},{1,5},{2,6},{3,7},{4,0},{5,1},{6,2},{7,3},{8,12},{9,13},{10,... | collective-permute-start | bytes 393224 | tf_op jit(solution)/shard_map/ppermute | solution.py:516
  82.0 7.5 %collective-permute-start.12 = (bf16[64,1024]{1,0:T(8,128)(2,1)S(1)}, bf16[64,1024]{1,0:T(8,128)(2,1)S(1)}, u32[]{:S(2)}, u32[]{:S(2)}) collective-permute-start(bf16[64,1024]{1,0:T(8,128)(2,1)S(1)} %shard_map.132.own_ref), channel_id=1, source_target_pairs={{0,2},{1,3},{2,4},{3,5},{4,6},{5,7},{6,0},{7,1},{8,10},{9,11},{10,... | collective-permute-start | bytes 393224 | tf_op jit(solution)/shard_map/ppermute | solution.py:516
  83.4 8.3 %collective-permute-start.11 = (bf16[64,1024]{1,0:T(8,128)(2,1)S(1)}, bf16[64,1024]{1,0:T(8,128)(2,1)S(1)}, u32[]{:S(2)}, u32[]{:S(2)}) collective-permute-start(bf16[64,1024]{1,0:T(8,128)(2,1)S(1)} %shard_map.132.own_ref), channel_id=1, source_target_pairs={{0,4},{1,5},{2,6},{3,7},{4,0},{5,1},{6,2},{7,3},{8,12},{9,13},{10,... | collective-permute-start | bytes 393224 | tf_op jit(solution)/shard_map/ppermute | solution.py:516
  95.0 10.2 %collective-permute-start.17 = (bf16[128,1792]{1,0:T(8,128)(2,1)S(1)}, bf16[128,1792]{1,0:T(8,128)(2,1)S(1)}, u32[]{:S(2)}, u32[]{:S(2)}) collective-permute-start(bf16[128,1792]{1,0:T(8,128)(2,1)S(1)} %get-tuple-element.49), channel_id=1, source_target_pairs={{0,8},{1,33},{2,10},{3,35},{4,12},{5,37},{6,14},{7,39},{8,16},{9,4... | collective-permute-start | bytes 1376264 | tf_op jit(solution)/shard_map/ppermute | solution.py:512
  97.1 12.2 %collective-permute-start.14 = (bf16[128,1664]{1,0:T(8,128)(2,1)S(1)}, bf16[128,1664]{1,0:T(8,128)(2,1)S(1)}, u32[]{:S(2)}, u32[]{:S(2)}) collective-permute-start(bf16[128,1664]{1,0:T(8,128)(2,1)S(1)} %get-tuple-element.46), channel_id=1, source_target_pairs={{0,8},{1,33},{2,10},{3,35},{4,12},{5,37},{6,14},{7,39},{8,16},{9,4... | collective-permute-start | bytes 1277960 | tf_op jit(solution)/shard_map/ppermute | solution.py:512
  98.0 11.6 %collective-permute-start.20 = (bf16[128,1664]{1,0:T(8,128)(2,1)S(1)}, bf16[128,1664]{1,0:T(8,128)(2,1)S(1)}, u32[]{:S(2)}, u32[]{:S(2)}) collective-permute-start(bf16[128,1664]{1,0:T(8,128)(2,1)S(1)} %get-tuple-element.52), channel_id=1, source_target_pairs={{0,24},{1,97},{2,26},{3,99},{4,28},{5,101},{6,30},{7,103},{8,0},{9... | collective-permute-start | bytes 1277960 | tf_op jit(solution)/shard_map/ppermute | solution.py:512
  100.6 12.3 %collective-permute-start.23 = (bf16[128,1664]{1,0:T(8,128)(2,1)S(1)}, bf16[128,1664]{1,0:T(8,128)(2,1)S(1)}, u32[]{:S(2)}, u32[]{:S(2)}) collective-permute-start(bf16[128,1664]{1,0:T(8,128)(2,1)S(1)} %get-tuple-element.55), channel_id=1, source_target_pairs={{0,24},{1,97},{2,26},{3,99},{4,28},{5,101},{6,30},{7,103},{8,0},{9... | collective-permute-start | bytes 1277960 | tf_op jit(solution)/shard_map/ppermute | solution.py:512
  105.3 13.3 %collective-permute-start.18 = (bf16[128,1792]{1,0:T(8,128)(2,1)S(1)}, bf16[128,1792]{1,0:T(8,128)(2,1)S(1)}, u32[]{:S(2)}, u32[]{:S(2)}) collective-permute-start(bf16[128,1792]{1,0:T(8,128)(2,1)S(1)} %shard_map.141), channel_id=1, source_target_pairs={{0,8},{1,33},{2,10},{3,35},{4,12},{5,37},{6,14},{7,39},{8,16},{9,4... | collective-permute-start | bytes 1376264 | tf_op jit(solution)/shard_map/ppermute | solution.py:512
  109.4 10.2 %collective-permute-start.15 = (bf16[128,1664]{1,0:T(8,128)(2,1)S(1)}, bf16[128,1664]{1,0:T(8,128)(2,1)S(1)}, u32[]{:S(2)}, u32[]{:S(2)}) collective-permute-start(bf16[128,1664]{1,0:T(8,128)(2,1)S(1)} %shard_map.138), channel_id=1, source_target_pairs={{0,8},{1,33},{2,10},{3,35},{4,12},{5,37},{6,14},{7,39},{8,16},{9,4... | collective-permute-start | bytes 1277960 | tf_op jit(solution)/shard_map/ppermute | solution.py:512
  109.6 10.2 %collective-permute-start.21 = (bf16[128,1664]{1,0:T(8,128)(2,1)S(1)}, bf16[128,1664]{1,0:T(8,128)(2,1)S(1)}, u32[]{:S(2)}, u32[]{:S(2)}) collective-permute-start(bf16[128,1664]{1,0:T(8,128)(2,1)S(1)} %shard_map.143), channel_id=1, source_target_pairs={{0,24},{1,97},{2,26},{3,99},{4,28},{5,101},{6,30},{7,103},{8,0},{9... | collective-permute-start | bytes 1277960 | tf_op jit(solution)/shard_map/ppermute | solution.py:512
  113.0 10.2 %collective-permute-start.24 = (bf16[128,1664]{1,0:T(8,128)(2,1)S(1)}, bf16[128,1664]{1,0:T(8,128)(2,1)S(1)}, u32[]{:S(2)}, u32[]{:S(2)}) collective-permute-start(bf16[128,1664]{1,0:T(8,128)(2,1)S(1)} %shard_map.145), channel_id=1, source_target_pairs={{0,24},{1,97},{2,26},{3,99},{4,28},{5,101},{6,30},{7,103},{8,0},{9... | collective-permute-start | bytes 1277960 | tf_op jit(solution)/shard_map/ppermute | solution.py:512
  118.7 14.6 %collective-permute-start.19 = (bf16[128,1792]{1,0:T(8,128)(2,1)S(1)}, bf16[128,1792]{1,0:T(8,128)(2,1)S(1)}, u32[]{:S(2)}, u32[]{:S(2)}) collective-permute-start(bf16[128,1792]{1,0:T(8,128)(2,1)S(1)} %shard_map.142), channel_id=1, source_target_pairs={{0,8},{1,33},{2,10},{3,35},{4,12},{5,37},{6,14},{7,39},{8,16},{9,4... | collective-permute-start | bytes 1376264 | tf_op jit(solution)/shard_map/ppermute | solution.py:512
  119.7 13.4 %collective-permute-start.16 = (bf16[128,1664]{1,0:T(8,128)(2,1)S(1)}, bf16[128,1664]{1,0:T(8,128)(2,1)S(1)}, u32[]{:S(2)}, u32[]{:S(2)}) collective-permute-start(bf16[128,1664]{1,0:T(8,128)(2,1)S(1)} %shard_map.139), channel_id=1, source_target_pairs={{0,8},{1,33},{2,10},{3,35},{4,12},{5,37},{6,14},{7,39},{8,16},{9,4... | collective-permute-start | bytes 1277960 | tf_op jit(solution)/shard_map/ppermute | solution.py:512
  119.9 13.2 %collective-permute-start.22 = (bf16[128,1664]{1,0:T(8,128)(2,1)S(1)}, bf16[128,1664]{1,0:T(8,128)(2,1)S(1)}, u32[]{:S(2)}, u32[]{:S(2)}) collective-permute-start(bf16[128,1664]{1,0:T(8,128)(2,1)S(1)} %shard_map.144), channel_id=1, source_target_pairs={{0,24},{1,97},{2,26},{3,99},{4,28},{5,101},{6,30},{7,103},{8,0},{9... | collective-permute-start | bytes 1277960 | tf_op jit(solution)/shard_map/ppermute | solution.py:512
  123.2 10.1 %collective-permute-start.25 = (bf16[128,1664]{1,0:T(8,128)(2,1)S(1)}, bf16[128,1664]{1,0:T(8,128)(2,1)S(1)}, u32[]{:S(2)}, u32[]{:S(2)}) collective-permute-start(bf16[128,1664]{1,0:T(8,128)(2,1)S(1)} %shard_map.146), channel_id=1, source_target_pairs={{0,24},{1,97},{2,26},{3,99},{4,28},{5,101},{6,30},{7,103},{8,0},{9... | collective-permute-start | bytes 1277960 | tf_op jit(solution)/shard_map/ppermute | solution.py:512
  133.9 9.9 %collective-permute-start.26 = (bf16[32,6784]{1,0:T(8,128)(2,1)S(1)}, bf16[32,6784]{1,0:T(8,128)(2,1)S(1)}, u32[]{:S(2)}, u32[]{:S(2)}) collective-permute-start(bf16[32,6784]{1,0:T(8,128)(2,1)S(1)} %get-tuple-element.57), channel_id=1, source_target_pairs={{0,64},{1,17},{2,66},{3,19},{4,68},{5,21},{6,70},{7,23},{8,72},{9,... | collective-permute-start | bytes 1302536 | tf_op jit(solution)/shard_map/ppermute | solution.py:512
  135.3 13.0 %collective-permute-start.27 = (bf16[32,6784]{1,0:T(8,128)(2,1)S(1)}, bf16[32,6784]{1,0:T(8,128)(2,1)S(1)}, u32[]{:S(2)}, u32[]{:S(2)}) collective-permute-start(bf16[32,6784]{1,0:T(8,128)(2,1)S(1)} %get-tuple-element.58), channel_id=1, source_target_pairs={{0,32},{1,9},{2,34},{3,11},{4,36},{5,13},{6,38},{7,15},{8,40},{9,1... | collective-permute-start | bytes 1302536 | tf_op jit(solution)/shard_map/ppermute | solution.py:512
  137.5 10.9 %collective-permute-start.28 = (bf16[32,6784]{1,0:T(8,128)(2,1)S(1)}, bf16[32,6784]{1,0:T(8,128)(2,1)S(1)}, u32[]{:S(2)}, u32[]{:S(2)}) collective-permute-start(bf16[32,6784]{1,0:T(8,128)(2,1)S(1)} %get-tuple-element.59), channel_id=1, source_target_pairs={{0,96},{1,25},{2,98},{3,27},{4,100},{5,29},{6,102},{7,31},{8,104},... | collective-permute-start | bytes 1302536 | tf_op jit(solution)/shard_map/ppermute | solution.py:512
  (15 other events, 211.2 us)

commit v7 on v6

--- a/solution.py
+++ b/solution.py
@@ -407,11 +407,11 @@
     return CUTS[part + 1] - CUTS[part] + (HD if kind and part else 0)
 
 
-def project_steps(steps, parts, block_of, up_ref, gate_ref, refs):
+def project_steps(kinds, steps, parts, block_of, weights, refs):
     size = SIDE * ROWS
     refs = iter(refs)
     here = stand()[0]
-    for kind, weight_ref in ((1, gate_ref), (0, up_ref)):
+    for kind, weight_ref in zip(kinds, weights):
         blocks = []
         for step in steps:
             there = (here + (SIDE - step if kind else step)) % SIDE
@@ -431,7 +431,7 @@
                     out[:, width:] = jnp.concatenate(totals, axis=0).astype(out.dtype)
 
 
-def first_body(steps, parts, this_ref, other_ref, gain_ref, up_ref, gate_ref, *refs):
+def first_body(kinds, steps, parts, this_ref, other_ref, gain_ref, *refs):
     core = place()[3]
     this = this_ref.reshape(SIDE // 2, SIDE, ROWS, WIDTH)
     other = other_ref.reshape(SIDE // 2, SIDE, ROWS, WIDTH)
@@ -440,21 +440,29 @@
         block = jnp.where(i // 2 == core, this[i % 2, j], other[i % 2, j])
         return scale(block, gain_ref)
 
-    project_steps(steps, parts, block_of, up_ref, gate_ref, refs)
-
-
-def rest_body(steps, parts, rows_ref, squares_ref, up_ref, gate_ref, *refs):
-    project_steps(steps, parts, lambda i, j: (rows_ref[i, j], squares_ref[i, j]), up_ref, gate_ref, refs)
-
-
-def project(body, steps, parts, dtype, weights, *arrays):
-    keys = [(kind, part, step) for kind in (1, 0) for part in parts for step in steps]
+    project_steps(kinds, steps, parts, block_of, refs[: len(kinds)], refs[len(kinds) :])
+
+
+def rest_body(kinds, steps, parts, rows_ref, squares_ref, *refs):
+    project_steps(
+        kinds,
+        steps,
+        parts,
+        lambda i, j: (rows_ref[i, j], squares_ref[i, j]),
+        refs[: len(kinds)],
+        refs[len(kinds) :],
+    )
+
+
+def project(body, kinds, steps, parts, dtype, weights, *arrays):
+    weights = [weights[kind] for kind in kinds]
+    keys = [(kind, part, step) for kind in kinds for part in parts for step in steps]
     results = pl.pallas_call(
-        functools.partial(body, steps, parts),
+        functools.partial(body, kinds, steps, parts),
         out_shape=[
             jax.ShapeDtypeStruct((SIDE * ROWS, part_columns(kind, part)), dtype) for kind, part, _ in keys
         ],
-        in_specs=[VMEM] * (len(arrays) + 2),
+        in_specs=[VMEM] * (len(arrays) + len(kinds)),
         out_specs=[VMEM] * len(keys),
         compiler_params=params(24),
     )(*arrays, *weights)
@@ -529,13 +537,13 @@
     def send(kind, x):
         return along(0, x, 1 if kind else 3)
 
-    for part in range(2):
-        first = project(first_body, (1,), (part,), jnp.bfloat16, weights, *halves, gain)
-        for kind in (1, 0):
+    for kind in (1, 0):
+        first = project(first_body, (kind,), (1,), (0, 1), jnp.bfloat16, weights, *halves, gain)
+        for part in range(2):
             came[kind, part] = send(kind, first[kind, part, 1])
     residual, rows, squares = assemble(*halves, gain)
-    rest = project(rest_body, (2,), (0, 1), jnp.float32, weights, rows, squares)
-    rest |= project(rest_body, (3, 0), (0, 1), jnp.float32, weights, rows, squares)
+    rest = project(rest_body, (1, 0), (2,), (0, 1), jnp.float32, weights, rows, squares)
+    rest |= project(rest_body, (1, 0), (3, 0), (0, 1), jnp.float32, weights, rows, squares)
     for step in (2, 3):
         for kind, part in keys:
             came[kind, part] = send(kind, relay(rest[kind, part, step], came[kind, part]))

time: 149 us -> 149 us (level)
  transfers between devices with their start and end apart: 30 -> 30, of which waited for: 18 -> 19; matrix products, arithmetic and copies ran while one was open for 0% -> 0% of each run, Pallas kernels for 9% -> 9%
where the time goes in v7:
time: 149 us
  waiting for transfers between devices  53.4 us (36%)
  starting transfers between devices  51.2 us (34%)
  Pallas kernels  29.3 us (20%)
  blocking collectives  12 us (8%)
    ppermute x21, waiting for transfers between devices, along(): return lax.ppermute(x, ('attn', 'ffn'), pairs)  37 us
    ppermute x21, starting transfers between devices, along(): return lax.ppermute(x, ('attn', 'ffn'), pairs)  31.9 us
    all_to_all x1, blocking collectives, on_device(): lax.all_to_all(blended, 'attn', split_axis=0, concat_axis=0, tiled=True)  12 us
    ppermute x6, starting transfers between devices, along_x(): lax.ppermute(x, 'ffn', [(chip * 2 + core, (chip + shift) % SIDE * 2 + cor...  11 us
    pallas_call x1, Pallas kernels, attend(): pl.pallas_call(attend_body, out_shape=jax.ShapeDtypeStruct((SLOTS, HEADS,...  9.47 us
    ppermute x6, waiting for transfers between devices, along_x(): lax.ppermute(x, 'ffn', [(chip * 2 + core, (chip + shift) % SIDE * 2 + cor...  8.79 us
    pallas_call x4, Pallas kernels, project(): pl.pallas_call(functools.partial(body, kinds, steps, parts), out_shape=[j...  8.33 us
    all_to_all x1, starting transfers between devices, on_device(): lax.all_to_all(outgoing, 'attn', split_axis=0, concat_axis=0, tiled=True)  8.14 us
  transfers between devices with their start and end apart: 30, of which 19 were waited for; matrix products, arithmetic and copies ran while one was open for 0% of the time, Pallas kernels for 9%

profile of v7, /device:TPU:0, one launch (start us, length us, event | category | flops | bytes accessed | tf_op | source)
XLA Modules:
  0.0 149.4 jit_solution(9834547050608432024)
XLA Ops:
  2.4 8.1 %all-to-all-start = ((bf16[64,16,128]{2,1,0:T(8,128)(2,1)}), bf16[64,16,128]{2,1,0:T(8,128)(2,1)S(1)}, u32[]{:S(2)}, u32[]{:S(2)}) async-start(bf16[64,16,128]{2,1,0:T(8,128)(2,1)} %get-tuple-element.32), calls=%async_computation | async-start | bytes 524288 | tf_op jit(solution)/shard_map/all_to_all | solution.py:580
  10.6 3.4 %shard_map.123.list_ref = s32[2,128]{1,0:T(2,128)} custom-call(s32[1,512]{1,0:T(1,128)} %bitcast.21, s32[1,512]{1,0:T(1,128)} %bitcast.22), custom_call_target="tpu_custom_call" | custom-call | tf_op jit(solution)/shard_map/pallas_call | solution.py:141
  13.9 5.2 %all-to-all-done.queries_hbm = bf16[64,16,128]{2,1,0:T(8,128)(2,1)S(1)} async-done(((bf16[64,16,128]{2,1,0:T(8,128)(2,1)}), bf16[64,16,128]{2,1,0:T(8,128)(2,1)S(1)}, u32[]{:S(2)}, u32[]{:S(2)}) %all-to-all-start) | async-done | bytes 262176 | tf_op jit(solution)/shard_map/all_to_all | solution.py:580
  19.8 9.5 %shard_map.124 = bf16[64,16,128]{2,1,0:T(8,128)(2,1)} custom-call(s32[2,128]{1,0:T(2,128)} %shard_map.123.list_ref, bf16[64,16,128]{2,1,0:T(8,128)(2,1)} %copy-done.3, s32[1,512]{1,0:T(1,128)} %bitcast.23, s32[32,512]{1,0:T(8,128)} %bitcast.19, bf16[256,16,128]{2,1,0:T(8,128)(2,1)} %k_hbm.1, bf16[256,16,128]{2,1,0:T(8,128)(2,1)} %v_hbm.1), custom_call_target="tpu_custom_call" | custom-call | tf_op jit(solution)/shard_map/pallas_call | solution.py:215
  29.2 12.0 %all_to_all.10.slots_ref = bf16[64,16,128]{2,1,0:T(8,128)(2,1)S(1)} all-to-all(bf16[64,16,128]{2,1,0:T(8,128)(2,1)} %shard_map.124), channel_id=1, replica_groups=mesh['attn'=16,'ffn'=8] {'attn'}, dimensions={0} | all-to-all | bytes 524288 | tf_op jit(solution)/shard_map/all_to_all | solution.py:582
  46.7 3.5 %collective-permute-done.2.refs_2_ = bf16[32,2048]{1,0:T(8,128)(2,1)S(1)} collective-permute-done((bf16[32,2048]{1,0:T(8,128)(2,1)S(1)}, bf16[32,2048]{1,0:T(8,128)(2,1)S(1)}, u32[]{:S(2)}, u32[]{:S(2)}) %collective-permute-start.2) | collective-permute-done | bytes 131104 | tf_op jit(solution)/shard_map/ppermute | solution.py:520
  51.5 2.2 %collective-permute-start.4 = (bf16[4,32,2048]{2,1,0:T(8,128)(2,1)S(1)}, bf16[4,32,2048]{2,1,0:T(8,128)(2,1)S(1)}, u32[]{:S(2)}, u32[]{:S(2)}) collective-permute-start(bf16[4,32,2048]{2,1,0:T(8,128)(2,1)S(1)} %shard_map.127.refs_3_), channel_id=1, source_target_pairs={{0,64},{1,17},{2,66},{3,19},{4,68},{5,21},{6,70},{7,23},{8,72},{9,... | collective-permute-start | bytes 1572872 | tf_op jit(solution)/shard_map/ppermute | solution.py:520
  55.2 12.0 %collective-permute-done.5.refs_2_ = bf16[4,32,2048]{2,1,0:T(8,128)(2,1)S(1)} collective-permute-done((bf16[4,32,2048]{2,1,0:T(8,128)(2,1)S(1)}, bf16[4,32,2048]{2,1,0:T(8,128)(2,1)S(1)}, u32[]{:S(2)}, u32[]{:S(2)}) %collective-permute-start.5) | collective-permute-done | bytes 524320 | tf_op jit(solution)/shard_map/ppermute | solution.py:520
  71.8 3.1 %collective-permute-start.7 = (bf16[64,1024]{1,0:T(8,128)(2,1)S(1)}, bf16[64,1024]{1,0:T(8,128)(2,1)S(1)}, u32[]{:S(2)}, u32[]{:S(2)}) collective-permute-start(bf16[64,1024]{1,0:T(8,128)(2,1)S(1)} %get-tuple-element.34), channel_id=1, source_target_pairs={{0,4},{1,5},{2,6},{3,7},{4,0},{5,1},{6,2},{7,3},{8,12},{9,13},{10,... | collective-permute-start | bytes 393224 | tf_op jit(solution)/shard_map/ppermute | solution.py:524
  75.5 2.6 %collective-permute-start.9 = (bf16[64,1024]{1,0:T(8,128)(2,1)S(1)}, bf16[64,1024]{1,0:T(8,128)(2,1)S(1)}, u32[]{:S(2)}, u32[]{:S(2)}) collective-permute-start(bf16[64,1024]{1,0:T(8,128)(2,1)S(1)} %get-tuple-element.36), channel_id=1, source_target_pairs={{0,6},{1,7},{2,0},{3,1},{4,2},{5,3},{6,4},{7,5},{8,14},{9,15},{10,... | collective-permute-start | bytes 393224 | tf_op jit(solution)/shard_map/ppermute | solution.py:524
  79.7 2.2 %collective-permute-done.8.b_ref = bf16[64,1024]{1,0:T(8,128)(2,1)S(1)} collective-permute-done((bf16[64,1024]{1,0:T(8,128)(2,1)S(1)}, bf16[64,1024]{1,0:T(8,128)(2,1)S(1)}, u32[]{:S(2)}, u32[]{:S(2)}) %collective-permute-start.8) | collective-permute-done | bytes 131104 | tf_op jit(solution)/shard_map/ppermute | solution.py:524
  83.4 3.0 %collective-permute-start.11 = (bf16[64,1024]{1,0:T(8,128)(2,1)S(1)}, bf16[64,1024]{1,0:T(8,128)(2,1)S(1)}, u32[]{:S(2)}, u32[]{:S(2)}) collective-permute-start(bf16[64,1024]{1,0:T(8,128)(2,1)S(1)} %shard_map.132.own_ref), channel_id=1, source_target_pairs={{0,4},{1,5},{2,6},{3,7},{4,0},{5,1},{6,2},{7,3},{8,12},{9,13},{10,... | collective-permute-start | bytes 393224 | tf_op jit(solution)/shard_map/ppermute | solution.py:524
  86.6 2.8 %collective-permute-done.12.three_ref = bf16[64,1024]{1,0:T(8,128)(2,1)S(1)} collective-permute-done((bf16[64,1024]{1,0:T(8,128)(2,1)S(1)}, bf16[64,1024]{1,0:T(8,128)(2,1)S(1)}, u32[]{:S(2)}, u32[]{:S(2)}) %collective-permute-start.12) | collective-permute-done | bytes 131104 | tf_op jit(solution)/shard_map/ppermute | solution.py:524
  89.5 2.2 %collective-permute-done.11.two_ref = bf16[64,1024]{1,0:T(8,128)(2,1)S(1)} collective-permute-done((bf16[64,1024]{1,0:T(8,128)(2,1)S(1)}, bf16[64,1024]{1,0:T(8,128)(2,1)S(1)}, u32[]{:S(2)}, u32[]{:S(2)}) %collective-permute-start.11) | collective-permute-done | bytes 131104 | tf_op jit(solution)/shard_map/ppermute | solution.py:524
  97.7 2.7 %collective-permute-start.20 = (bf16[128,1664]{1,0:T(8,128)(2,1)S(1)}, bf16[128,1664]{1,0:T(8,128)(2,1)S(1)}, u32[]{:S(2)}, u32[]{:S(2)}) collective-permute-start(bf16[128,1664]{1,0:T(8,128)(2,1)S(1)} %get-tuple-element.52), channel_id=1, source_target_pairs={{0,24},{1,97},{2,26},{3,99},{4,28},{5,101},{6,30},{7,103},{8,0},{9... | collective-permute-start | bytes 1277960 | tf_op jit(solution)/shard_map/ppermute | solution.py:520
  106.0 3.3 %collective-permute-done.14.came_ref = bf16[128,1664]{1,0:T(8,128)(2,1)S(1)} collective-permute-done((bf16[128,1664]{1,0:T(8,128)(2,1)S(1)}, bf16[128,1664]{1,0:T(8,128)(2,1)S(1)}, u32[]{:S(2)}, u32[]{:S(2)}) %collective-permute-start.14) | collective-permute-done | bytes 426016 | tf_op jit(solution)/shard_map/ppermute | solution.py:520
  109.6 3.3 %collective-permute-start.21 = (bf16[128,1664]{1,0:T(8,128)(2,1)S(1)}, bf16[128,1664]{1,0:T(8,128)(2,1)S(1)}, u32[]{:S(2)}, u32[]{:S(2)}) collective-permute-start(bf16[128,1664]{1,0:T(8,128)(2,1)S(1)} %shard_map.143), channel_id=1, source_target_pairs={{0,24},{1,97},{2,26},{3,99},{4,28},{5,101},{6,30},{7,103},{8,0},{9... | collective-permute-start | bytes 1277960 | tf_op jit(solution)/shard_map/ppermute | solution.py:520
  114.5 4.0 %shard_map.135 = (f32[128,1664]{1,0:T(8,128)S(1)}, f32[128,1664]{1,0:T(8,128)S(1)}, f32[128,1792]{1,0:T(8,128)S(1)}, f32[128,1792]{1,0:T(8,128)S(1)}, f32[128,16...) custom-call(bf16[4,4,32,1024]{3,2,1,0:T(8,128)(2,1)S(1)} %get-tuple-element.38.rows_, ...), custom_call_target="tpu_custom_call" | custom-call | tf_op jit(solution)/shard_map/pallas_call | solution.py:460
  119.7 3.3 %collective-permute-start.22 = (bf16[128,1664]{1,0:T(8,128)(2,1)S(1)}, bf16[128,1664]{1,0:T(8,128)(2,1)S(1)}, u32[]{:S(2)}, u32[]{:S(2)}) collective-permute-start(bf16[128,1664]{1,0:T(8,128)(2,1)S(1)} %shard_map.144), channel_id=1, source_target_pairs={{0,24},{1,97},{2,26},{3,99},{4,28},{5,101},{6,30},{7,103},{8,0},{9... | collective-permute-start | bytes 1277960 | tf_op jit(solution)/shard_map/ppermute | solution.py:520
  123.1 3.8 %collective-permute-start.25 = (bf16[128,1664]{1,0:T(8,128)(2,1)S(1)}, bf16[128,1664]{1,0:T(8,128)(2,1)S(1)}, u32[]{:S(2)}, u32[]{:S(2)}) collective-permute-start(bf16[128,1664]{1,0:T(8,128)(2,1)S(1)} %shard_map.146), channel_id=1, source_target_pairs={{0,24},{1,97},{2,26},{3,99},{4,28},{5,101},{6,30},{7,103},{8,0},{9... | collective-permute-start | bytes 1277960 | tf_op jit(solution)/shard_map/ppermute | solution.py:520
  126.9 5.9 %collective-permute-done.16.refs_4_ = bf16[128,1664]{1,0:T(8,128)(2,1)S(1)} collective-permute-done((bf16[128,1664]{1,0:T(8,128)(2,1)S(1)}, bf16[128,1664]{1,0:T(8,128)(2,1)S(1)}, u32[]{:S(2)}, u32[]{:S(2)}) %collective-permute-start.16) | collective-permute-done | bytes 426016 | tf_op jit(solution)/shard_map/ppermute | solution.py:520
  135.1 2.1 %collective-permute-start.27 = (bf16[32,6784]{1,0:T(8,128)(2,1)S(1)}, bf16[32,6784]{1,0:T(8,128)(2,1)S(1)}, u32[]{:S(2)}, u32[]{:S(2)}) collective-permute-start(bf16[32,6784]{1,0:T(8,128)(2,1)S(1)} %get-tuple-element.58), channel_id=1, source_target_pairs={{0,32},{1,9},{2,34},{3,11},{4,36},{5,13},{6,38},{7,15},{8,40},{9,1... | collective-permute-start | bytes 1302536 | tf_op jit(solution)/shard_map/ppermute | solution.py:520
  138.4 5.2 %collective-permute-done.26 = bf16[32,6784]{1,0:T(8,128)(2,1)S(1)} collective-permute-done((bf16[32,6784]{1,0:T(8,128)(2,1)S(1)}, bf16[32,6784]{1,0:T(8,128)(2,1)S(1)}, u32[]{:S(2)}, u32[]{:S(2)}) %collective-permute-start.26) | collective-permute-done | bytes 434208 | tf_op jit(solution)/shard_map/ppermute | solution.py:520
  143.6 4.5 %collective-permute-done.27 = bf16[32,6784]{1,0:T(8,128)(2,1)S(1)} collective-permute-done((bf16[32,6784]{1,0:T(8,128)(2,1)S(1)}, bf16[32,6784]{1,0:T(8,128)(2,1)S(1)}, u32[]{:S(2)}, u32[]{:S(2)}) %collective-permute-start.27) | collective-permute-done | bytes 434208 | tf_op jit(solution)/shard_map/ppermute | solution.py:520
  (87 shorter events, 38.4 us)
Async XLA Ops:
  2.4 16.7 %all-to-all-start = ((bf16[64,16,128]{2,1,0:T(8,128)(2,1)}), bf16[64,16,128]{2,1,0:T(8,128)(2,1)S(1)}, u32[]{:S(2)}, u32[]{:S(2)}) async-start(bf16[64,16,128]{2,1,0:T(8,128)(2,1)} %get-tuple-element.32), calls=%async_computation | async-start | bytes 524288 | tf_op jit(solution)/shard_map/all_to_all | solution.py:580
  42.6 7.7 %collective-permute-start.2 = (bf16[32,2048]{1,0:T(8,128)(2,1)S(1)}, bf16[32,2048]{1,0:T(8,128)(2,1)S(1)}, u32[]{:S(2)}, u32[]{:S(2)}) collective-permute-start(bf16[32,2048]{1,0:T(8,128)(2,1)S(1)} %shard_map.125.after_hbm.refs_3_), channel_id=1, source_target_pairs={{0,8},{1,33},{2,10},{3,35},{4,12},{5,37},{6,14},{7,39},{8,16},{9,4... | collective-permute-start | bytes 393224 | tf_op jit(solution)/shard_map/ppermute | solution.py:520
  43.1 7.2 %collective-permute-start.1 = (bf16[32,2048]{1,0:T(8,128)(2,1)S(1)}, bf16[32,2048]{1,0:T(8,128)(2,1)S(1)}, u32[]{:S(2)}, u32[]{:S(2)}) collective-permute-start(bf16[32,2048]{1,0:T(8,128)(2,1)S(1)} %shard_map.125.after_hbm.refs_3_), channel_id=1, source_target_pairs={{0,16},{1,65},{2,18},{3,67},{4,20},{5,69},{6,22},{7,71},{8,24},{9,... | collective-permute-start | bytes 393224 | tf_op jit(solution)/shard_map/ppermute | solution.py:520
  51.1 16.1 %collective-permute-start.5 = (bf16[4,32,2048]{2,1,0:T(8,128)(2,1)S(1)}, bf16[4,32,2048]{2,1,0:T(8,128)(2,1)S(1)}, u32[]{:S(2)}, u32[]{:S(2)}) collective-permute-start(bf16[4,32,2048]{2,1,0:T(8,128)(2,1)S(1)} %shard_map.127.refs_3_), channel_id=1, source_target_pairs={{0,32},{1,9},{2,34},{3,11},{4,36},{5,13},{6,38},{7,15},{8,40},{9,1... | collective-permute-start | bytes 1572872 | tf_op jit(solution)/shard_map/ppermute | solution.py:520
  51.5 15.8 %collective-permute-start.4 = (bf16[4,32,2048]{2,1,0:T(8,128)(2,1)S(1)}, bf16[4,32,2048]{2,1,0:T(8,128)(2,1)S(1)}, u32[]{:S(2)}, u32[]{:S(2)}) collective-permute-start(bf16[4,32,2048]{2,1,0:T(8,128)(2,1)S(1)} %shard_map.127.refs_3_), channel_id=1, source_target_pairs={{0,64},{1,17},{2,66},{3,19},{4,68},{5,21},{6,70},{7,23},{8,72},{9,... | collective-permute-start | bytes 1572872 | tf_op jit(solution)/shard_map/ppermute | solution.py:520
  53.7 14.4 %collective-permute-start.3 = (bf16[4,32,2048]{2,1,0:T(8,128)(2,1)S(1)}, bf16[4,32,2048]{2,1,0:T(8,128)(2,1)S(1)}, u32[]{:S(2)}, u32[]{:S(2)}) collective-permute-start(bf16[4,32,2048]{2,1,0:T(8,128)(2,1)S(1)} %shard_map.127.refs_3_), channel_id=1, source_target_pairs={{0,96},{1,25},{2,98},{3,27},{4,100},{5,29},{6,102},{7,31},{8,104},... | collective-permute-start | bytes 1572872 | tf_op jit(solution)/shard_map/ppermute | solution.py:520
  71.8 7.9 %collective-permute-start.7 = (bf16[64,1024]{1,0:T(8,128)(2,1)S(1)}, bf16[64,1024]{1,0:T(8,128)(2,1)S(1)}, u32[]{:S(2)}, u32[]{:S(2)}) collective-permute-start(bf16[64,1024]{1,0:T(8,128)(2,1)S(1)} %get-tuple-element.34), channel_id=1, source_target_pairs={{0,4},{1,5},{2,6},{3,7},{4,0},{5,1},{6,2},{7,3},{8,12},{9,13},{10,... | collective-permute-start | bytes 393224 | tf_op jit(solution)/shard_map/ppermute | solution.py:524
  82.0 7.5 %collective-permute-start.12 = (bf16[64,1024]{1,0:T(8,128)(2,1)S(1)}, bf16[64,1024]{1,0:T(8,128)(2,1)S(1)}, u32[]{:S(2)}, u32[]{:S(2)}) collective-permute-start(bf16[64,1024]{1,0:T(8,128)(2,1)S(1)} %shard_map.132.own_ref), channel_id=1, source_target_pairs={{0,2},{1,3},{2,4},{3,5},{4,6},{5,7},{6,0},{7,1},{8,10},{9,11},{10,... | collective-permute-start | bytes 393224 | tf_op jit(solution)/shard_map/ppermute | solution.py:524
  83.4 8.3 %collective-permute-start.11 = (bf16[64,1024]{1,0:T(8,128)(2,1)S(1)}, bf16[64,1024]{1,0:T(8,128)(2,1)S(1)}, u32[]{:S(2)}, u32[]{:S(2)}) collective-permute-start(bf16[64,1024]{1,0:T(8,128)(2,1)S(1)} %shard_map.132.own_ref), channel_id=1, source_target_pairs={{0,4},{1,5},{2,6},{3,7},{4,0},{5,1},{6,2},{7,3},{8,12},{9,13},{10,... | collective-permute-start | bytes 393224 | tf_op jit(solution)/shard_map/ppermute | solution.py:524
  95.0 10.0 %collective-permute-start.17 = (bf16[128,1792]{1,0:T(8,128)(2,1)S(1)}, bf16[128,1792]{1,0:T(8,128)(2,1)S(1)}, u32[]{:S(2)}, u32[]{:S(2)}) collective-permute-start(bf16[128,1792]{1,0:T(8,128)(2,1)S(1)} %get-tuple-element.49), channel_id=1, source_target_pairs={{0,8},{1,33},{2,10},{3,35},{4,12},{5,37},{6,14},{7,39},{8,16},{9,4... | collective-permute-start | bytes 1376264 | tf_op jit(solution)/shard_map/ppermute | solution.py:520
  95.9 13.4 %collective-permute-start.14 = (bf16[128,1664]{1,0:T(8,128)(2,1)S(1)}, bf16[128,1664]{1,0:T(8,128)(2,1)S(1)}, u32[]{:S(2)}, u32[]{:S(2)}) collective-permute-start(bf16[128,1664]{1,0:T(8,128)(2,1)S(1)} %get-tuple-element.46), channel_id=1, source_target_pairs={{0,8},{1,33},{2,10},{3,35},{4,12},{5,37},{6,14},{7,39},{8,16},{9,4... | collective-permute-start | bytes 1277960 | tf_op jit(solution)/shard_map/ppermute | solution.py:520
  97.7 11.8 %collective-permute-start.20 = (bf16[128,1664]{1,0:T(8,128)(2,1)S(1)}, bf16[128,1664]{1,0:T(8,128)(2,1)S(1)}, u32[]{:S(2)}, u32[]{:S(2)}) collective-permute-start(bf16[128,1664]{1,0:T(8,128)(2,1)S(1)} %get-tuple-element.52), channel_id=1, source_target_pairs={{0,24},{1,97},{2,26},{3,99},{4,28},{5,101},{6,30},{7,103},{8,0},{9... | collective-permute-start | bytes 1277960 | tf_op jit(solution)/shard_map/ppermute | solution.py:520
  100.4 12.4 %collective-permute-start.23 = (bf16[128,1664]{1,0:T(8,128)(2,1)S(1)}, bf16[128,1664]{1,0:T(8,128)(2,1)S(1)}, u32[]{:S(2)}, u32[]{:S(2)}) collective-permute-start(bf16[128,1664]{1,0:T(8,128)(2,1)S(1)} %get-tuple-element.55), channel_id=1, source_target_pairs={{0,24},{1,97},{2,26},{3,99},{4,28},{5,101},{6,30},{7,103},{8,0},{9... | collective-permute-start | bytes 1277960 | tf_op jit(solution)/shard_map/ppermute | solution.py:520
  105.1 13.4 %collective-permute-start.18 = (bf16[128,1792]{1,0:T(8,128)(2,1)S(1)}, bf16[128,1792]{1,0:T(8,128)(2,1)S(1)}, u32[]{:S(2)}, u32[]{:S(2)}) collective-permute-start(bf16[128,1792]{1,0:T(8,128)(2,1)S(1)} %shard_map.140), channel_id=1, source_target_pairs={{0,8},{1,33},{2,10},{3,35},{4,12},{5,37},{6,14},{7,39},{8,16},{9,4... | collective-permute-start | bytes 1376264 | tf_op jit(solution)/shard_map/ppermute | solution.py:520
  109.4 10.0 %collective-permute-start.15 = (bf16[128,1664]{1,0:T(8,128)(2,1)S(1)}, bf16[128,1664]{1,0:T(8,128)(2,1)S(1)}, u32[]{:S(2)}, u32[]{:S(2)}) collective-permute-start(bf16[128,1664]{1,0:T(8,128)(2,1)S(1)} %shard_map.138), channel_id=1, source_target_pairs={{0,8},{1,33},{2,10},{3,35},{4,12},{5,37},{6,14},{7,39},{8,16},{9,4... | collective-permute-start | bytes 1277960 | tf_op jit(solution)/shard_map/ppermute | solution.py:520
  109.6 10.0 %collective-permute-start.21 = (bf16[128,1664]{1,0:T(8,128)(2,1)S(1)}, bf16[128,1664]{1,0:T(8,128)(2,1)S(1)}, u32[]{:S(2)}, u32[]{:S(2)}) collective-permute-start(bf16[128,1664]{1,0:T(8,128)(2,1)S(1)} %shard_map.143), channel_id=1, source_target_pairs={{0,24},{1,97},{2,26},{3,99},{4,28},{5,101},{6,30},{7,103},{8,0},{9... | collective-permute-start | bytes 1277960 | tf_op jit(solution)/shard_map/ppermute | solution.py:520
  112.9 10.1 %collective-permute-start.24 = (bf16[128,1664]{1,0:T(8,128)(2,1)S(1)}, bf16[128,1664]{1,0:T(8,128)(2,1)S(1)}, u32[]{:S(2)}, u32[]{:S(2)}) collective-permute-start(bf16[128,1664]{1,0:T(8,128)(2,1)S(1)} %shard_map.145), channel_id=1, source_target_pairs={{0,24},{1,97},{2,26},{3,99},{4,28},{5,101},{6,30},{7,103},{8,0},{9... | collective-permute-start | bytes 1277960 | tf_op jit(solution)/shard_map/ppermute | solution.py:520
  118.5 14.6 %collective-permute-start.19 = (bf16[128,1792]{1,0:T(8,128)(2,1)S(1)}, bf16[128,1792]{1,0:T(8,128)(2,1)S(1)}, u32[]{:S(2)}, u32[]{:S(2)}) collective-permute-start(bf16[128,1792]{1,0:T(8,128)(2,1)S(1)} %shard_map.141), channel_id=1, source_target_pairs={{0,8},{1,33},{2,10},{3,35},{4,12},{5,37},{6,14},{7,39},{8,16},{9,4... | collective-permute-start | bytes 1376264 | tf_op jit(solution)/shard_map/ppermute | solution.py:520
  119.5 13.4 %collective-permute-start.16 = (bf16[128,1664]{1,0:T(8,128)(2,1)S(1)}, bf16[128,1664]{1,0:T(8,128)(2,1)S(1)}, u32[]{:S(2)}, u32[]{:S(2)}) collective-permute-start(bf16[128,1664]{1,0:T(8,128)(2,1)S(1)} %shard_map.139), channel_id=1, source_target_pairs={{0,8},{1,33},{2,10},{3,35},{4,12},{5,37},{6,14},{7,39},{8,16},{9,4... | collective-permute-start | bytes 1277960 | tf_op jit(solution)/shard_map/ppermute | solution.py:520
  119.7 13.2 %collective-permute-start.22 = (bf16[128,1664]{1,0:T(8,128)(2,1)S(1)}, bf16[128,1664]{1,0:T(8,128)(2,1)S(1)}, u32[]{:S(2)}, u32[]{:S(2)}) collective-permute-start(bf16[128,1664]{1,0:T(8,128)(2,1)S(1)} %shard_map.144), channel_id=1, source_target_pairs={{0,24},{1,97},{2,26},{3,99},{4,28},{5,101},{6,30},{7,103},{8,0},{9... | collective-permute-start | bytes 1277960 | tf_op jit(solution)/shard_map/ppermute | solution.py:520
  123.1 10.0 %collective-permute-start.25 = (bf16[128,1664]{1,0:T(8,128)(2,1)S(1)}, bf16[128,1664]{1,0:T(8,128)(2,1)S(1)}, u32[]{:S(2)}, u32[]{:S(2)}) collective-permute-start(bf16[128,1664]{1,0:T(8,128)(2,1)S(1)} %shard_map.146), channel_id=1, source_target_pairs={{0,24},{1,97},{2,26},{3,99},{4,28},{5,101},{6,30},{7,103},{8,0},{9... | collective-permute-start | bytes 1277960 | tf_op jit(solution)/shard_map/ppermute | solution.py:520
  133.7 9.9 %collective-permute-start.26 = (bf16[32,6784]{1,0:T(8,128)(2,1)S(1)}, bf16[32,6784]{1,0:T(8,128)(2,1)S(1)}, u32[]{:S(2)}, u32[]{:S(2)}) collective-permute-start(bf16[32,6784]{1,0:T(8,128)(2,1)S(1)} %get-tuple-element.57), channel_id=1, source_target_pairs={{0,64},{1,17},{2,66},{3,19},{4,68},{5,21},{6,70},{7,23},{8,72},{9,... | collective-permute-start | bytes 1302536 | tf_op jit(solution)/shard_map/ppermute | solution.py:520
  135.1 13.0 %collective-permute-start.27 = (bf16[32,6784]{1,0:T(8,128)(2,1)S(1)}, bf16[32,6784]{1,0:T(8,128)(2,1)S(1)}, u32[]{:S(2)}, u32[]{:S(2)}) collective-permute-start(bf16[32,6784]{1,0:T(8,128)(2,1)S(1)} %get-tuple-element.58), channel_id=1, source_target_pairs={{0,32},{1,9},{2,34},{3,11},{4,36},{5,13},{6,38},{7,15},{8,40},{9,1... | collective-permute-start | bytes 1302536 | tf_op jit(solution)/shard_map/ppermute | solution.py:520
  137.3 10.9 %collective-permute-start.28 = (bf16[32,6784]{1,0:T(8,128)(2,1)S(1)}, bf16[32,6784]{1,0:T(8,128)(2,1)S(1)}, u32[]{:S(2)}, u32[]{:S(2)}) collective-permute-start(bf16[32,6784]{1,0:T(8,128)(2,1)S(1)} %get-tuple-element.59), channel_id=1, source_target_pairs={{0,96},{1,25},{2,98},{3,27},{4,100},{5,29},{6,102},{7,31},{8,104},... | collective-permute-start | bytes 1302536 | tf_op jit(solution)/shard_map/ppermute | solution.py:520
  (15 other events, 202.5 us)
